TPU v7x, 512 devices: a whole 4x4x16 slice. The times are simulated.
512 devices in a mesh: gx: 4 (over z_hi, core), gy: 4 (over x), gz: 32 (over y, z_lo).
Axes of the slice: x: 4, y: 4, z: 16 (z_hi: 2, z_lo: 8; z = z_hi * 8 + z_lo), core: 2. Of those that a mesh axis runs over, the one named last changes fastest.
Arguments:
- positions: float32 [3, 4, 4, 32, 8192], P(None, 'gx', 'gy', 'gz'), may hold values from 0 to 8
- charges: float32 [4, 4, 32, 8192], P('gx', 'gy', 'gz'), may hold values from -4 to 4
- cluster_tile: int32 [4, 4, 32, 128], P('gx', 'gy', 'gz'), may hold values from 0 to 215
- live_clusters: int32 [4, 4, 32], P('gx', 'gy', 'gz'), may hold values from 42 to 128, as said below
- kernel_blocks: bfloat16 [4, 512, 512], replicated, may hold values from -0.09375 to 0.09375
- restrict_weights: float32 [512], replicated, may hold values from -4 to 4
- top_kernel: float32 [4096, 4096], P('gz', ('gx', 'gy')), may hold values from -0.09375 to 0.09375
Outputs:
- forces: float32 [3, 4, 4, 32, 8192], P(None, 'gx', 'gy', 'gz')
- virial: float32 [6, 4, 4, 32, 8192], P(None, 'gx', 'gy', 'gz')
Inputs may be any that keep to these rules, and one draw needn't show every extreme that they name: `cluster_tile`: tiles are numbered (tx 6 + ty) * 6 + tz within a brick. `live_clusters`: some brick has all 128 slots live.
All inputs are finite; a program needn't handle non-finite values.
Results may differ from a plain program's by a relative error of at most 0.0023.
Values may be sent and summed in bfloat16 or wider, within the bound.
No kernel may reach another device: no remote copies, remote signals or barrier semaphores. Data moves between devices by JAX's collectives and lax.ppermute only.
A program may use at most 64 MiB of HBM per device.

v0:
```python
import math

import jax
import jax.numpy as jnp
from jax import lax
from jax.sharding import PartitionSpec as P

TL = 8
CS = 64
TD = 6
CL_DEV = 128


HIGHEST_PRECISION = lax.Precision.HIGHEST


def shifted(value, axis, steps):
    count = lax.axis_size(axis)
    pairs = [(source, (source + steps) % count) for source in range(count)]
    return lax.ppermute(value, axis, pairs)


def bump_weights(coord, tile_edge):
    grid_nodes = jnp.arange(tile_edge, dtype=jnp.float32).reshape((tile_edge,) + (1,) * coord.ndim)
    offset = coord[None] - grid_nodes
    weight = jnp.exp(-0.5 * offset * offset)
    return (weight, -offset * weight)


def spread(coords, charge_live, onehot, tile_edge):
    weight_x = bump_weights(coords[0], tile_edge)[0]
    weight_y = bump_weights(coords[1], tile_edge)[0]
    weight_z = bump_weights(coords[2], tile_edge)[0]
    plane_weights = (charge_live[None] * weight_x)[:, None] * weight_y[None]
    cluster_cells = jnp.einsum(
        "ijcn,kcn->cijk", plane_weights, weight_z, precision=HIGHEST_PRECISION
    )
    cluster_cells = cluster_cells.reshape(cluster_cells.shape[0], -1)
    return jnp.einsum("ct,cp->tp", onehot, cluster_cells, precision=HIGHEST_PRECISION)


def prolong(potential, coarse_pot, restrict_weights, tile_count):
    half_tiles = tile_count // 2
    spread_pot = jnp.broadcast_to(
        coarse_pot.reshape(2, 1, 2, 1, 2, 1, 1), (2, half_tiles, 2, half_tiles, 2, half_tiles, 1)
    )
    return potential + spread_pot.reshape(-1, 1) * restrict_weights[None]


def forces_virial(full_field, tile_ids, coords, charge_live, tile_edge, tile_count):
    weight_x, slope_x = bump_weights(coords[0], tile_edge)
    weight_y, slope_y = bump_weights(coords[1], tile_edge)
    weight_z, slope_z = bump_weights(coords[2], tile_edge)
    cluster_field = jnp.take(full_field, tile_ids, axis=0).reshape(
        -1, tile_edge, tile_edge, tile_edge
    )
    field_z = jnp.einsum("cijk,kcn->ijcn", cluster_field, weight_z, precision=HIGHEST_PRECISION)
    field_dz = jnp.einsum("cijk,kcn->ijcn", cluster_field, slope_z, precision=HIGHEST_PRECISION)
    grad_x = jnp.sum(slope_x[:, None] * weight_y[None] * field_z, axis=(0, 1))
    grad_y = jnp.sum(weight_x[:, None] * slope_y[None] * field_z, axis=(0, 1))
    grad_z = jnp.sum(weight_x[:, None] * weight_y[None] * field_dz, axis=(0, 1))
    forces = -charge_live[None] * jnp.stack([grad_x, grad_y, grad_z])
    tile_x = tile_ids // (tile_count * tile_count)
    tile_y = tile_ids // tile_count % tile_count
    tile_z = tile_ids % tile_count
    anchor = jnp.stack([tile_x, tile_y, tile_z]).astype(coords.dtype)[:, :, None] * tile_edge
    brick_frac = (anchor + coords) / (tile_edge * tile_count)
    virial = jnp.stack(
        [
            brick_frac[0] * forces[0],
            brick_frac[1] * forces[1],
            brick_frac[2] * forces[2],
            brick_frac[0] * forces[1],
            brick_frac[0] * forces[2],
            brick_frac[1] * forces[2],
        ]
    )
    return (forces, virial)


def apply_block(rows, block, flipped):
    contract_dims = ((1,), (0,)) if flipped else ((1,), (1,))
    return lax.dot_general(
        rows, block, (contract_dims, ((), ())), preferred_element_type=jnp.float32
    )


def as_rows(view):
    return view.reshape(-1, view.shape[-1])


def face_field(grid_bf, kernel_blocks):
    upper_x = shifted(grid_bf[0], "gx", -1)
    lower_x = shifted(grid_bf[-1], "gx", 1)
    upper_y = shifted(grid_bf[:, 0], "gy", -1)
    lower_y = shifted(grid_bf[:, -1], "gy", 1)
    upper_z = shifted(grid_bf[:, :, 0], "gz", -1)
    lower_z = shifted(grid_bf[:, :, -1], "gz", 1)
    next_x = jnp.concatenate([grid_bf[1:], upper_x[None]], axis=0)
    prev_x = jnp.concatenate([lower_x[None], grid_bf[:-1]], axis=0)
    next_y = jnp.concatenate([grid_bf[:, 1:], upper_y[:, None]], axis=1)
    prev_y = jnp.concatenate([lower_y[:, None], grid_bf[:, :-1]], axis=1)
    next_z = jnp.concatenate([grid_bf[:, :, 1:], upper_z[:, :, None]], axis=2)
    prev_z = jnp.concatenate([lower_z[:, :, None], grid_bf[:, :, :-1]], axis=2)
    potential = apply_block(as_rows(grid_bf), kernel_blocks[0], False)
    potential = potential + apply_block(as_rows(next_x), kernel_blocks[1], False)
    potential = potential + apply_block(as_rows(prev_x), kernel_blocks[1], True)
    potential = potential + apply_block(as_rows(next_y), kernel_blocks[2], False)
    potential = potential + apply_block(as_rows(prev_y), kernel_blocks[2], True)
    potential = potential + apply_block(as_rows(next_z), kernel_blocks[3], False)
    potential = potential + apply_block(as_rows(prev_z), kernel_blocks[3], True)
    return potential


def level_one(grid_bf, kernel_blocks):
    return face_field(grid_bf, kernel_blocks)


def coarse_field(fine_charge, restrict_weights, top_kernel):
    half_tiles = TD // 2
    tile_points = restrict_weights.shape[0]
    moments = jnp.dot(fine_charge, restrict_weights, precision=HIGHEST_PRECISION)
    coarse = (
        moments.reshape(2, half_tiles, 2, half_tiles, 2, half_tiles).sum(axis=(1, 3, 5)).reshape(8)
    )
    coarse = coarse / math.sqrt(tile_points * half_tiles**3)
    column = lax.all_gather(coarse, "gz", axis=0, tiled=True)
    partial_value = jnp.dot(top_kernel, column, precision=HIGHEST_PRECISION)
    return lax.psum_scatter(partial_value, ("gx", "gy"), scatter_dimension=0, tiled=True)


def shards(
    positions, charges, cluster_tile, live_clusters, kernel_blocks, restrict_weights, top_kernel
):
    tile_points = TL**3
    cubes = TD**3
    coords = positions.reshape(3, CL_DEV, CS)
    charge_rows = charges.reshape(CL_DEV, CS)
    tile_ids = cluster_tile.reshape(CL_DEV)
    alive_mask = jnp.arange(CL_DEV, dtype=jnp.int32) < live_clusters.reshape(())
    onehot = (
        (tile_ids[:, None] == jnp.arange(cubes, dtype=jnp.int32)[None]) & alive_mask[:, None]
    ).astype(jnp.float32)
    charge_live = charge_rows * alive_mask[:, None].astype(jnp.float32)
    fine_charge = spread(coords, charge_live, onehot, TL)
    grid_bf = fine_charge.astype(jnp.bfloat16).reshape(TD, TD, TD, tile_points)
    near_pot = level_one(grid_bf, kernel_blocks)
    coarse_pot = coarse_field(fine_charge, restrict_weights, top_kernel)
    full_field = prolong(near_pot, coarse_pot, restrict_weights, TD)
    forces, virial = forces_virial(full_field, tile_ids, coords, charge_live, TL, TD)
    return (forces.reshape(3, 1, 1, 1, -1), virial.reshape(6, 1, 1, 1, -1))


def solution(mesh):
    placed = (
        P(None, "gx", "gy", "gz", None),
        P("gx", "gy", "gz", None),
        P("gx", "gy", "gz", None),
        P("gx", "gy", "gz"),
        P(),
        P(),
        P("gz", ("gx", "gy")),
    )
    return jax.shard_map(
        shards,
        mesh=mesh,
        in_specs=placed,
        out_specs=(P(None, "gx", "gy", "gz", None), P(None, "gx", "gy", "gz", None)),
        check_vma=False,
    )
```

profile of v0, /device:TPU:2, one launch (start us, length us, event | category | flops | bytes accessed | tf_op | source)
XLA Modules:
  0.0 299.4 jit_solution(14537285414077311263)
XLA Ops:
  1.3 0.5 broadcast.335
  1.9 1.5 reduce.16
  3.4 1.0 slice_reduce_fusion
  4.6 0.9 negate_multiply_fusion
  5.6 0.7 fusion.56
  6.3 1.2 negate_multiply_fusion.1
  7.5 5.4 %fusion.3 = f32[128,8,8,8]{3,2,1,0:T(8,128)} fusion(f32[8,128,64]{2,0,1:T(8,128)S(1)} %get-tuple-element.31, f32[8,128,64]{2,0,1:T(8,128)S(1)} %get-tuple-element.28, f32[128,64]{1,0:T(8,128)S(1)} %sub.101), kind=kOutput, calls=%fused_computation.7 | convolution fusion | flops 51052544 | bytes 819200 | tf_op jit(solution)/shard_map/ijcn,kcn->cijk/dot_general | solution.py:35
  12.9 3.9 %copy.33 = f32[128,8,8,8]{0,3,2,1:T(8,128)S(1)} copy(f32[128,8,8,8]{3,2,1,0:T(8,128)} %fusion.3) | data formatting | bytes 524288 | tf_op jit(solution)/shard_map/ijcn,kcn->cijk/dot_general | solution.py:35
  16.8 1.2 fusion.62
  18.0 0.6 squeeze.21
  18.7 15.2 %collective-permute-start = (bf16[6,6,512]{2,1,0:T(8,128)(2,1)}, bf16[6,6,512]{2,1,0:T(8,128)(2,1)}, u32[]{:S(2)}, u32[]{:S(2)}) collective-permute-start(bf16[6,6,512]{2,1,0:T(8,128)(2,1)} %squeeze.21), channel_id=1, source_target_pairs={{0,384},{128,0},{256,128},{384,256},{1,385},{129,1},{257,129},{385... | collective-permute-start | bytes 110600 | tf_op jit(solution)/shard_map/ppermute | solution.py:20
  33.8 0.6 squeeze.23
  34.5 1.9 collective-permute-start.1
  36.5 0.6 slice_bitcast_fusion
  37.1 2.4 collective-permute-start.2
  39.5 3.4 %collective-permute-start.3 = (bf16[6,6,512]{2,1,0:T(8,128)(2,1)}, bf16[6,6,512]{2,1,0:T(8,128)(2,1)}, u32[]{:S(2)}, u32[]{:S(2)}) collective-permute-start(bf16[6,6,512]{2,1,0:T(8,128)(2,1)} %get-tuple-element.19), channel_id=1, source_target_pairs={{0,32},{32,64},{64,96},{96,0},{1,33},{33,65},{65,97},{97,1},{2,34}... | collective-permute-start | bytes 110600 | tf_op jit(solution)/shard_map/ppermute | solution.py:20
  43.1 0.6 copy.51
  43.7 8.1 %collective-permute-start.4 = (bf16[6,6,512]{2,1,0:T(8,128)(2,1)}, bf16[6,6,512]{2,1,0:T(8,128)(2,1)}, u32[]{:S(2)}, u32[]{:S(2)}) collective-permute-start(bf16[6,6,512]{2,1,0:T(8,128)(2,1)} %bitcast.120), channel_id=1, source_target_pairs={{0,31},{1,0},{2,1},{3,2},{4,3},{5,4},{6,5},{7,6},{8,7},{9,8},{10,9... | collective-permute-start | bytes 110600 | tf_op jit(solution)/shard_map/ppermute | solution.py:20
  51.8 0.8 fusion.61
  52.6 0.8 fusion.59
  53.4 0.9 fusion.58
  54.3 0.5 fusion.51
  54.8 0.5 compare_and_fusion
  55.3 0.6 fusion.49
  55.9 0.9 reduce.4
  57.2 1.5 fusion.63
  59.0 1.3 dynamic-slice
  61.1 114.1 %all-reduce = f32[256]{0:T(256)S(1)} all-reduce(f32[256]{0:T(256)S(1)} %dynamic-update-slice), channel_id=1, replica_groups=mesh['gx'=4,'gy'=4,'gz'=32] {'gz'}, use_global_device_ids=true, to_apply=%add | all-reduce | flops 256 | bytes 2048
  175.2 1.1 reshape.420
  176.3 1.4 mul.231
  177.7 1.5 mul.232
  179.4 0.7 fusion.48
  180.1 0.8 add_multiply_fusion
  180.9 1.4 multiply_negate_fusion
  182.3 1.2 pad_clamp_fusion
  183.5 1.7 slice.103
  185.2 1.7 slice.108
  186.8 0.6 copy.50
  187.5 1.3 dynamic-slice.1
  189.3 63.8 %all-reduce.1 = f32[128]{0:T(128)S(1)} all-reduce(f32[128]{0:T(128)S(1)} %convolution_bitcast_fusion), channel_id=2, replica_groups=mesh['gx'=4,'gy'=4,'gz'=32] {'gx','gy'}, use_global_device_ids=true, to_apply=%region_1.0.clone | all-reduce | flops 128 | bytes 1024
  253.3 0.7 broadcast_in_dim.61
  254.0 2.8 collective-permute-start.5
  256.9 1.0 pad_maximum_fusion
  257.9 1.7 pad_maximum_fusion.1
  259.6 1.8 pad_maximum_fusion.2
  261.4 0.9 copy.37
  262.3 1.7 pad_maximum_fusion.3
  264.0 1.8 pad_maximum_fusion.4
  265.8 0.8 reshape.411
  266.6 1.7 reshape.412
  268.3 1.7 reshape.414
  270.0 1.7 reshape.415
  271.8 1.7 reshape.416
  273.5 0.9 copy.39
  274.4 1.1 pad_maximum_fusion.5
  275.5 0.8 reshape.417
  276.3 1.3 convolution_add_fusion.5
  277.6 1.2 convolution_add_fusion.4
  278.8 1.3 convolution_add_fusion.3
  281.1 1.0 gather_fusion
  282.3 4.4 %copy.41 = f32[128,8,8,8]{3,2,1,0:T(8,128)} copy(f32[128,8,8,8]{0,3,2,1:T(8,128)S(1)} %broadcast_select_fusion) | data formatting | bytes 524288 | tf_op jit(solution)/shard_map/jit(_take)/select_n | solution.py:54
  286.7 5.9 %fusion = f32[128,64]{1,0:T(8,128)S(1)} fusion(f32[128,8,8,8]{3,2,1,0:T(8,128)} %copy.41, f32[8,128,64]{2,0,1:T(8,128)S(1)} %copy-done.3, f32[8,128,64]{2,0,1:T(8,128)S(1)} %get-tuple-element.28, f32[128,64]{1,0:T(8,128)S(1)} %sub.101), kind=kOutput, calls=%fused_computation.2 | convolution fusion | flops 52224000 | bytes 851968 | tf_op jit(solution)/shard_map/cijk,kcn->ijcn/dot_general | solution.py:58
  292.7 4.8 %fusion.1 = (f32[128,64]{1,0:T(8,128)S(1)}, f32[128,64]{1,0:T(8,128)S(1)}) fusion(f32[8,128,64]{2,0,1:T(8,128)S(1)} %get-tuple-element.28, f32[8,128,64]{2,0,1:T(8,128)S(1)} %copy-done.9, f32[8,128,64]{2,0,1:T(8,128)S(1)} %copy-done.8, f32[8,128,64]{2,0,1:T(8,128)S(1)} %copy-done.3, f32[128,8,8,8]{3,2,1,0:T(8,128)S(1)} %copy-done.1, f32[128,64]{1,0:T(8,128)S(1)} %sub.101), kind=kOutput, calls=%fused_computation.5 | convolution fusion | flops 53657600 | bytes 1409024 | tf_op jit(solution)/shard_map/cijk,kcn->ijcn/dot_general | solution.py:57
  298.6 0.8 maximum_multiply_fusion.1
  (85 shorter events, 4.0 us)
Async XLA Ops:
  0.6 178.6 %copy-start = (f32[128,256]{1,0:T(8,128)S(1)}, f32[128,256]{1,0:T(8,128)}, u32[]{:S(2)}) copy-start(f32[128,256]{1,0:T(8,128)} %param.13) | copy-start | bytes 393220
  1.3 6.2 %copy-start.16 = (f32[128]{0:T(128)}, f32[128]{0:T(128)S(1)}, u32[]{:S(2)}) copy-start(f32[128]{0:T(128)S(1)} %get-tuple-element.38) | copy-start | bytes 1540
  7.5 9.3 %copy-start.17 = (s32[1,1,1,128]{3,2,1,0:T(1,128)S(1)}, s32[1,1,1,128]{3,2,1,0:T(1,128)}, u32[]{:S(2)}) copy-start(s32[1,1,1,128]{3,2,1,0:T(1,128)} %param.9) | copy-start | bytes 1540
  12.9 43.0 %copy-start.10 = (f32[3,1,1,1,8192]{4,3,2,1,0:T(1,128)S(1)}, f32[3,1,1,1,8192]{4,3,2,1,0:T(1,128)}, u32[]{:S(2)}) copy-start(f32[3,1,1,1,8192]{4,3,2,1,0:T(1,128)} %param.7) | copy-start | bytes 294916
  12.9 44.0 %copy-start.2 = (bf16[4,512,512]{2,1,0:T(8,128)(2,1)S(1)}, bf16[4,512,512]{2,1,0:T(8,128)(2,1)}, u32[]{:S(2)}) copy-start(bf16[4,512,512]{2,1,0:T(8,128)(2,1)} %param.11) | copy-start | bytes 6291460
  18.7 235.3 %collective-permute-start = (bf16[6,6,512]{2,1,0:T(8,128)(2,1)}, bf16[6,6,512]{2,1,0:T(8,128)(2,1)}, u32[]{:S(2)}, u32[]{:S(2)}) collective-permute-start(bf16[6,6,512]{2,1,0:T(8,128)(2,1)} %squeeze.21), channel_id=1, source_target_pairs={{0,384},{128,0},{256,128},{384,256},{1,385},{129,1},{257,129},{385... | collective-permute-start | bytes 110600 | tf_op jit(solution)/shard_map/ppermute | solution.py:20
  34.5 223.5 %collective-permute-start.1 = (bf16[6,6,512]{2,1,0:T(8,128)(2,1)}, bf16[6,6,512]{2,1,0:T(8,128)(2,1)}, u32[]{:S(2)}, u32[]{:S(2)}) collective-permute-start(bf16[6,6,512]{2,1,0:T(8,128)(2,1)} %squeeze.23), channel_id=1, source_target_pairs={{0,128},{128,256},{256,384},{384,0},{1,129},{129,257},{257,385},{3... | collective-permute-start | bytes 110600 | tf_op jit(solution)/shard_map/ppermute | solution.py:20
  37.1 222.5 %collective-permute-start.2 = (bf16[6,6,512]{2,1,0:T(8,128)(2,1)}, bf16[6,6,512]{2,1,0:T(8,128)(2,1)}, u32[]{:S(2)}, u32[]{:S(2)}) collective-permute-start(bf16[6,6,512]{2,1,0:T(8,128)(2,1)} %get-tuple-element.20), channel_id=1, source_target_pairs={{0,96},{32,0},{64,32},{96,64},{1,97},{33,1},{65,33},{97,65},{2,98}... | collective-permute-start | bytes 110600 | tf_op jit(solution)/shard_map/ppermute | solution.py:20
  39.5 222.7 %collective-permute-start.3 = (bf16[6,6,512]{2,1,0:T(8,128)(2,1)}, bf16[6,6,512]{2,1,0:T(8,128)(2,1)}, u32[]{:S(2)}, u32[]{:S(2)}) collective-permute-start(bf16[6,6,512]{2,1,0:T(8,128)(2,1)} %get-tuple-element.19), channel_id=1, source_target_pairs={{0,32},{32,64},{64,96},{96,0},{1,33},{33,65},{65,97},{97,1},{2,34}... | collective-permute-start | bytes 110600 | tf_op jit(solution)/shard_map/ppermute | solution.py:20
  43.7 217.7 %collective-permute-start.4 = (bf16[6,6,512]{2,1,0:T(8,128)(2,1)}, bf16[6,6,512]{2,1,0:T(8,128)(2,1)}, u32[]{:S(2)}, u32[]{:S(2)}) collective-permute-start(bf16[6,6,512]{2,1,0:T(8,128)(2,1)} %bitcast.120), channel_id=1, source_target_pairs={{0,31},{1,0},{2,1},{3,2},{4,3},{5,4},{6,5},{7,6},{8,7},{9,8},{10,9... | collective-permute-start | bytes 110600 | tf_op jit(solution)/shard_map/ppermute | solution.py:20
  254.0 19.5 %collective-permute-start.5 = (bf16[6,6,512]{2,1,0:T(8,128)(2,1)}, bf16[6,6,512]{2,1,0:T(8,128)(2,1)}, u32[]{:S(2)}, u32[]{:S(2)}) collective-permute-start(bf16[6,6,512]{2,1,0:T(8,128)(2,1)} %bitcast.119), channel_id=1, source_target_pairs={{0,1},{1,2},{2,3},{3,4},{4,5},{5,6},{6,7},{7,8},{8,9},{9,10},{10,1... | collective-permute-start | bytes 110600 | tf_op jit(solution)/shard_map/ppermute | solution.py:20
  276.3 3.8 %copy-start.5 = (bf16[216,512]{1,0:T(8,128)(2,1)S(1)}, bf16[216,512]{1,0:T(8,128)(2,1)}, u32[]{:S(2)}) copy-start(bf16[216,512]{1,0:T(8,128)(2,1)} %reshape.415) | copy-start | bytes 663556
  276.3 4.1 %copy-start.4 = (bf16[216,512]{1,0:T(8,128)(2,1)S(1)}, bf16[216,512]{1,0:T(8,128)(2,1)}, u32[]{:S(2)}) copy-start(bf16[216,512]{1,0:T(8,128)(2,1)} %reshape.416) | copy-start | bytes 663556
  276.3 4.5 %copy-start.6 = (bf16[216,512]{1,0:T(8,128)(2,1)S(1)}, bf16[216,512]{1,0:T(8,128)(2,1)}, u32[]{:S(2)}) copy-start(bf16[216,512]{1,0:T(8,128)(2,1)} %reshape.417) | copy-start | bytes 663556
  276.3 4.5 %copy-start.13 = (f32[512]{0:T(512)S(1)}, f32[512]{0:T(512)}, u32[]{:S(2)}) copy-start(f32[512]{0:T(512)} %param.12) | copy-start | bytes 6148
  276.3 4.5 %copy-start.15 = (f32[216]{0:T(256)S(1)}, f32[216]{0:T(256)}, u32[]{:S(2)}) copy-start(f32[216]{0:T(256)} %broadcast_in_dim.61) | copy-start | bytes 2596
  280.1 2.1 copy-start.18
  281.1 5.6 %copy-start.3 = (f32[8,128,64]{2,0,1:T(8,128)S(1)}, f32[8,128,64]{2,0,1:T(8,128)}, u32[]{:S(2)}) copy-start(f32[8,128,64]{2,0,1:T(8,128)} %get-tuple-element.30) | copy-start | bytes 786436
  282.3 10.3 %copy-start.8 = (f32[8,128,64]{2,0,1:T(8,128)S(1)}, f32[8,128,64]{2,0,1:T(8,128)}, u32[]{:S(2)}) copy-start(f32[8,128,64]{2,0,1:T(8,128)} %get-tuple-element.27) | copy-start | bytes 786436
  282.3 10.3 %copy-start.9 = (f32[8,128,64]{2,0,1:T(8,128)S(1)}, f32[8,128,64]{2,0,1:T(8,128)}, u32[]{:S(2)}) copy-start(f32[8,128,64]{2,0,1:T(8,128)} %get-tuple-element.29) | copy-start | bytes 786436
  286.7 6.0 %copy-start.1 = (f32[128,8,8,8]{3,2,1,0:T(8,128)S(1)}, f32[128,8,8,8]{3,2,1,0:T(8,128)}, u32[]{:S(2)}) copy-start(f32[128,8,8,8]{3,2,1,0:T(8,128)} %copy.41) | copy-start | bytes 786436
  292.6 5.2 %copy-start.11 = (f32[128,64]{1,0:T(8,128)S(1)}, f32[128,64]{1,0:T(8,128)}, u32[]{:S(2)}) copy-start(f32[128,64]{1,0:T(8,128)} %get-tuple-element.7) | copy-start | bytes 98308
  292.6 5.2 %copy-start.7 = (f32[3,128,64]{2,1,0:T(8,128)S(1)}, f32[3,128,64]{2,1,0:T(8,128)}, u32[]{:S(2)}) copy-start(f32[3,128,64]{2,1,0:T(8,128)} %add_multiply_fusion) | copy-start | bytes 294916
  292.6 6.0 %copy-start.12 = (f32[8192]{0:T(1024)S(1)}, f32[8192]{0:T(1024)}, u32[]{:S(2)}) copy-start(f32[8192]{0:T(1024)} %multiply_negate_fusion) | copy-start | bytes 98308
  298.6 0.8 copy-start.14
where the time goes:
time: 301 us; the launch traced here: 299 us
  blocking collectives  178 us (59%)
  local copies, waits for them, and re-layouts  39.6 us (13%)
  starting transfers between devices  33.8 us (11%)
  matrix products  24 us (8%)
  other arithmetic  21.1 us (7%)
    unnamed x2, blocking collectives  178 us
    ppermute x6, starting transfers between devices, shifted(): return lax.ppermute(value, axis, pairs)  33.8 us
    reshape x6, local copies, waits for them, and re-layouts, as_rows(): return view.reshape(-1, view.shape[-1])  8.44 us
  transfers between devices with their start and end apart: 6, of which 0 were waited for; matrix products, arithmetic and copies ran while one was open for 14% of the time, Pallas kernels for 0%

commit v1 on v0

--- a/solution.py
+++ b/solution.py
@@ -124,9 +124,12 @@
         moments.reshape(2, half_tiles, 2, half_tiles, 2, half_tiles).sum(axis=(1, 3, 5)).reshape(8)
     )
     coarse = coarse / math.sqrt(tile_points * half_tiles**3)
-    column = lax.all_gather(coarse, "gz", axis=0, tiled=True)
+    lines = lax.axis_size("gz")
+    column = lax.all_to_all(jnp.broadcast_to(coarse[None], (lines, 8)), "gz", 0, 0, tiled=True)
+    column = column.reshape(lines * 8)
     partial_value = jnp.dot(top_kernel, column, precision=HIGHEST_PRECISION)
-    return lax.psum_scatter(partial_value, ("gx", "gy"), scatter_dimension=0, tiled=True)
+    parts = lax.all_to_all(partial_value.reshape(-1, 8), ("gx", "gy"), 0, 0, tiled=True)
+    return parts.sum(axis=0)
 
 
 def shards(

time: 301 us -> 153 us (0.51)
  the two profiles are of different devices: /device:TPU:2 before, /device:TPU:1 now
where the time goes in v1:
time: 153 us; the launch traced here: 151 us
  starting transfers between devices  54.4 us (36%)
  local copies, waits for them, and re-layouts  38.3 us (25%)
  matrix products  24.8 us (16%)
  other arithmetic  23.2 us (15%)
  waiting for transfers between devices  8.98 us (6%)
  between operations  1.87 us (1%)
    ppermute x6, starting transfers between devices, shifted(): return lax.ppermute(value, axis, pairs)  39.8 us
    all_to_all x1, starting transfers between devices, coarse_field(): lax.all_to_all(partial_value.reshape(-1, 8), ('gx', 'gy'), 0, 0, tiled=True)  10.1 us
    all_to_all x1, waiting for transfers between devices, coarse_field(): lax.all_to_all(partial_value.reshape(-1, 8), ('gx', 'gy'), 0, 0, tiled=True)  8.96 us
    reshape x6, local copies, waits for them, and re-layouts, as_rows(): return view.reshape(-1, view.shape[-1])  8.44 us
    dot_general x1, matrix products, forces_virial(): jnp.einsum('cijk,kcn->ijcn', cluster_field, slope_z, precision=HIGHEST_PR...  5.88 us
    dot_general x1, matrix products, spread(): jnp.einsum('ijcn,kcn->cijk', plane_weights, weight_z, precision=HIGHEST_P...  5.38 us
    dot_general x7, matrix products, apply_block(): lax.dot_general(rows, block, (contract_dims, ((), ())), preferred_element...  5.01 us
    dot_general x1, matrix products, forces_virial(): jnp.einsum('cijk,kcn->ijcn', cluster_field, weight_z, precision=HIGHEST_P...  4.84 us
  transfers between devices with their start and end apart: 8, of which 1 were waited for; matrix products, arithmetic and copies ran while one was open for 29% of the time, Pallas kernels for 0%

profile of v1, /device:TPU:1, one launch (start us, length us, event | category | flops | bytes accessed | tf_op | source)
XLA Modules:
  0.0 151.5 jit_solution(17569844823113724908)
XLA Ops:
  1.9 1.4 reduce.20
  3.4 1.0 slice_reduce_fusion
  4.6 0.9 negate_multiply_fusion
  5.6 0.7 fusion.58
  6.3 1.1 negate_multiply_fusion.1
  7.5 5.4 %fusion.3 = f32[128,8,8,8]{3,2,1,0:T(8,128)} fusion(f32[8,128,64]{2,0,1:T(8,128)S(1)} %get-tuple-element.31, f32[8,128,64]{2,0,1:T(8,128)S(1)} %get-tuple-element.28, f32[128,64]{1,0:T(8,128)S(1)} %sub.101), kind=kOutput, calls=%fused_computation.7 | convolution fusion | flops 51052544 | bytes 819200 | tf_op jit(solution)/shard_map/ijcn,kcn->cijk/dot_general | solution.py:35
  12.9 3.9 %copy.34 = f32[128,8,8,8]{0,3,2,1:T(8,128)S(1)} copy(f32[128,8,8,8]{3,2,1,0:T(8,128)} %fusion.3) | data formatting | bytes 524288 | tf_op jit(solution)/shard_map/ijcn,kcn->cijk/dot_general | solution.py:35
  16.8 1.2 fusion.64
  18.0 0.6 squeeze.21
  18.7 8.8 %collective-permute-start = (bf16[6,6,512]{2,1,0:T(8,128)(2,1)}, bf16[6,6,512]{2,1,0:T(8,128)(2,1)}, u32[]{:S(2)}, u32[]{:S(2)}) collective-permute-start(bf16[6,6,512]{2,1,0:T(8,128)(2,1)} %squeeze.21), channel_id=1, source_target_pairs={{0,384},{128,0},{256,128},{384,256},{1,385},{129,1},{257,129},{385... | collective-permute-start | bytes 110600 | tf_op jit(solution)/shard_map/ppermute | solution.py:20
  27.4 0.6 squeeze.23
  28.1 10.0 %collective-permute-start.1 = (bf16[6,6,512]{2,1,0:T(8,128)(2,1)}, bf16[6,6,512]{2,1,0:T(8,128)(2,1)}, u32[]{:S(2)}, u32[]{:S(2)}) collective-permute-start(bf16[6,6,512]{2,1,0:T(8,128)(2,1)} %squeeze.23), channel_id=1, source_target_pairs={{0,128},{128,256},{256,384},{384,0},{1,129},{129,257},{257,385},{3... | collective-permute-start | bytes 110600 | tf_op jit(solution)/shard_map/ppermute | solution.py:20
  38.1 0.6 slice_bitcast_fusion
  38.8 4.4 %collective-permute-start.2 = (bf16[6,6,512]{2,1,0:T(8,128)(2,1)}, bf16[6,6,512]{2,1,0:T(8,128)(2,1)}, u32[]{:S(2)}, u32[]{:S(2)}) collective-permute-start(bf16[6,6,512]{2,1,0:T(8,128)(2,1)} %get-tuple-element.20), channel_id=1, source_target_pairs={{0,96},{32,0},{64,32},{96,64},{1,97},{33,1},{65,33},{97,65},{2,98}... | collective-permute-start | bytes 110600 | tf_op jit(solution)/shard_map/ppermute | solution.py:20
  43.2 1.9 %collective-permute-start.3 = (bf16[6,6,512]{2,1,0:T(8,128)(2,1)}, bf16[6,6,512]{2,1,0:T(8,128)(2,1)}, u32[]{:S(2)}, u32[]{:S(2)}) collective-permute-start(bf16[6,6,512]{2,1,0:T(8,128)(2,1)} %get-tuple-element.19), channel_id=1, source_target_pairs={{0,32},{32,64},{64,96},{96,0},{1,33},{33,65},{65,97},{97,1},{2,34}... | collective-permute-start | bytes 110600 | tf_op jit(solution)/shard_map/ppermute | solution.py:20
  45.2 0.6 copy.54
  45.8 11.7 %collective-permute-start.4 = (bf16[6,6,512]{2,1,0:T(8,128)(2,1)}, bf16[6,6,512]{2,1,0:T(8,128)(2,1)}, u32[]{:S(2)}, u32[]{:S(2)}) collective-permute-start(bf16[6,6,512]{2,1,0:T(8,128)(2,1)} %bitcast.119), channel_id=1, source_target_pairs={{0,31},{1,0},{2,1},{3,2},{4,3},{5,4},{6,5},{7,6},{8,7},{9,8},{10,9... | collective-permute-start | bytes 110600 | tf_op jit(solution)/shard_map/ppermute | solution.py:20
  57.5 1.5 fusion.65
  59.4 0.6 broadcast_in_dim.65
  60.0 4.5 %all-to-all-start = ((f32[32,1,8]{2,1,0:T(1,128)}), f32[32,1,8]{2,1,0:T(1,128)}, u32[]{:S(2)}, u32[]{:S(2)}) async-start(f32[32,1,8]{2,1,0:T(1,128)} %broadcast_in_dim.65), calls=%async_computation | async-start | bytes 32768 | tf_op jit(solution)/shard_map/all_to_all | solution.py:128
  64.5 0.8 fusion.63
  65.2 0.9 fusion.61
  66.1 0.9 fusion.60
  68.2 0.9 reduce.6
  69.4 1.1 reshape.447
  70.5 1.3 mul.231
  71.8 1.5 %mul.232 = f32[8192]{0:T(1024)} reshape(f32[128,1,64]{2,0,1:T(8,128)} %mul.231) | data formatting | bytes 65536 | tf_op jit(solution)/shard_map/mul | solution.py:147
  73.3 0.7 fusion.50
  74.0 0.8 add_multiply_fusion
  74.8 1.4 multiply_negate_fusion
  76.2 1.2 compare_and_fusion
  77.5 1.4 reduce.21
  78.9 1.0 fusion.42
  80.0 0.7 copy.41
  80.7 10.1 %all-to-all-start.1 = ((f32[16,1,8]{2,1,0:T(1,128)}), f32[16,1,8]{2,1,0:T(1,128)S(1)}, u32[]{:S(2)}, u32[]{:S(2)}) async-start(f32[16,1,8]{2,1,0:T(1,128)} %copy.41), calls=%async_computation.1 | async-start | bytes 16384 | tf_op jit(solution)/shard_map/all_to_all | solution.py:131
  90.8 1.2 pad_clamp_fusion
  92.0 1.7 %slice.103 = bf16[5,6,6,512]{3,2,1,0:T(8,128)(2,1)} reshape(bf16[180,512]{1,0:T(8,128)(2,1)} %get-tuple-element.26) | data formatting | bytes 368640 | tf_op jit(solution)/shard_map/slice | solution.py:99
  93.7 1.7 %slice.108 = bf16[5,6,6,512]{3,2,1,0:T(8,128)(2,1)} reshape(bf16[180,512]{1,0:T(8,128)(2,1)} %get-tuple-element.25) | data formatting | bytes 368640 | tf_op jit(solution)/shard_map/slice | solution.py:100
  95.4 0.6 copy.53
  96.0 9.0 %all-to-all-done.1 = f32[16,1,8]{2,1,0:T(1,128)S(1)} async-done(((f32[16,1,8]{2,1,0:T(1,128)}), f32[16,1,8]{2,1,0:T(1,128)S(1)}, u32[]{:S(2)}, u32[]{:S(2)}) %all-to-all-start.1) | async-done | bytes 544 | tf_op jit(solution)/shard_map/all_to_all | solution.py:131
  105.2 0.7 broadcast_in_dim.68
  105.9 3.1 %collective-permute-start.5 = (bf16[6,6,512]{2,1,0:T(8,128)(2,1)}, bf16[6,6,512]{2,1,0:T(8,128)(2,1)}, u32[]{:S(2)}, u32[]{:S(2)}) collective-permute-start(bf16[6,6,512]{2,1,0:T(8,128)(2,1)} %bitcast.118), channel_id=1, source_target_pairs={{0,1},{1,2},{2,3},{3,4},{4,5},{5,6},{6,7},{7,8},{8,9},{9,10},{10,1... | collective-permute-start | bytes 110600 | tf_op jit(solution)/shard_map/ppermute | solution.py:20
  109.0 1.0 pad_maximum_fusion
  110.1 1.7 %pad_maximum_fusion.1 = bf16[6,6,6,512]{3,2,1,0:T(8,128)(2,1)} fusion(bf16[5,6,6,512]{3,2,1,0:T(8,128)(2,1)} %slice.108, bf16[1,6,6,512]{3,2,1,0:T(8,128)(2,1)} %bitcast.10), kind=kLoop, calls=%fused_computation.51 | loop fusion | flops 110592 | bytes 442368 | tf_op jit(solution)/shard_map/concatenate | solution.py:100
  111.8 1.7 %pad_maximum_fusion.2 = bf16[6,6,6,512]{3,2,1,0:T(8,128)(2,1)} fusion(bf16[6,1,6,512]{3,2,1,0:T(8,128)(2,1)} %bitcast.13, bf16[6,5,6,512]{3,2,1,0:T(8,128)(2,1)} %get-tuple-element.22), kind=kLoop, calls=%fused_computation.52 | loop fusion | flops 110592 | bytes 442368 | tf_op jit(solution)/shard_map/concatenate | solution.py:101
  113.5 0.9 copy.38
  114.4 1.7 %pad_maximum_fusion.3 = bf16[6,6,6,512]{3,2,1,0:T(8,128)(2,1)} fusion(bf16[6,5,6,512]{3,2,1,0:T(8,128)(2,1)} %get-tuple-element.21, bf16[6,1,6,512]{3,2,1,0:T(8,128)(2,1)} %bitcast.16), kind=kLoop, calls=%fused_computation.53 | loop fusion | flops 110592 | bytes 442368 | tf_op jit(solution)/shard_map/concatenate | solution.py:102
  116.2 1.8 %pad_maximum_fusion.4 = bf16[6,6,6,512]{3,2,1,0:T(8,128)(2,1)} fusion(bf16[6,6,1,512]{3,2,1,0:T(2,128)(2,1)S(1)} %copy.38, bf16[6,6,5,512]{3,2,1,0:T(8,128)(2,1)} %get-tuple-element.18), kind=kLoop, calls=%fused_computation.54 | loop fusion | flops 442368 | bytes 442368 | tf_op jit(solution)/shard_map/concatenate | solution.py:103
  118.0 0.8 reshape.436
  118.7 1.7 %reshape.437 = bf16[216,512]{1,0:T(8,128)(2,1)} reshape(bf16[6,6,6,512]{3,2,1,0:T(8,128)(2,1)} %pad_maximum_fusion.1) | data formatting | bytes 442368 | tf_op jit(solution)/shard_map/reshape | solution.py:89
  120.4 1.7 %reshape.439 = bf16[216,512]{1,0:T(8,128)(2,1)} reshape(bf16[6,6,6,512]{3,2,1,0:T(8,128)(2,1)} %pad_maximum_fusion.2) | data formatting | bytes 442368 | tf_op jit(solution)/shard_map/reshape | solution.py:89
  122.2 1.7 %reshape.440 = bf16[216,512]{1,0:T(8,128)(2,1)} reshape(bf16[6,6,6,512]{3,2,1,0:T(8,128)(2,1)} %pad_maximum_fusion.3) | data formatting | bytes 442368 | tf_op jit(solution)/shard_map/reshape | solution.py:89
  123.9 1.7 %reshape.441 = bf16[216,512]{1,0:T(8,128)(2,1)} reshape(bf16[6,6,6,512]{3,2,1,0:T(8,128)(2,1)} %pad_maximum_fusion.4) | data formatting | bytes 442368 | tf_op jit(solution)/shard_map/reshape | solution.py:89
  125.6 0.9 copy.40
  126.5 1.1 pad_maximum_fusion.5
  127.6 0.8 reshape.442
  128.4 1.3 convolution_add_fusion.5
  129.7 1.2 convolution_add_fusion.4
  130.9 1.3 convolution_add_fusion.3
  133.2 1.0 gather_fusion
  134.4 4.4 %copy.43 = f32[128,8,8,8]{3,2,1,0:T(8,128)} copy(f32[128,8,8,8]{0,3,2,1:T(8,128)S(1)} %broadcast_select_fusion) | data formatting | bytes 524288 | tf_op jit(solution)/shard_map/jit(_take)/select_n | solution.py:54
  138.8 5.9 %fusion = f32[128,64]{1,0:T(8,128)S(1)} fusion(f32[128,8,8,8]{3,2,1,0:T(8,128)} %copy.43, f32[8,128,64]{2,0,1:T(8,128)S(1)} %copy-done.3, f32[8,128,64]{2,0,1:T(8,128)S(1)} %get-tuple-element.28, f32[128,64]{1,0:T(8,128)S(1)} %sub.101), kind=kOutput, calls=%fused_computation.2 | convolution fusion | flops 52224000 | bytes 851968 | tf_op jit(solution)/shard_map/cijk,kcn->ijcn/dot_general | solution.py:58
  144.7 4.8 %fusion.1 = (f32[128,64]{1,0:T(8,128)S(1)}, f32[128,64]{1,0:T(8,128)S(1)}) fusion(f32[8,128,64]{2,0,1:T(8,128)S(1)} %get-tuple-element.28, f32[8,128,64]{2,0,1:T(8,128)S(1)} %copy-done.9, f32[8,128,64]{2,0,1:T(8,128)S(1)} %copy-done.8, f32[8,128,64]{2,0,1:T(8,128)S(1)} %copy-done.3, f32[128,8,8,8]{3,2,1,0:T(8,128)S(1)} %copy-done.1, f32[128,64]{1,0:T(8,128)S(1)} %sub.101), kind=kOutput, calls=%fused_computation.5 | convolution fusion | flops 53657600 | bytes 1409024 | tf_op jit(solution)/shard_map/cijk,kcn->ijcn/dot_general | solution.py:57
  150.7 0.8 maximum_multiply_fusion.1
  (90 shorter events, 5.4 us)
Async XLA Ops:
  0.6 78.3 %copy-start = (f32[128,256]{1,0:T(8,128)S(1)}, f32[128,256]{1,0:T(8,128)}, u32[]{:S(2)}) copy-start(f32[128,256]{1,0:T(8,128)} %param.13) | copy-start | bytes 393220
  1.3 6.1 %copy-start.17 = (f32[128]{0:T(128)}, f32[128]{0:T(128)S(1)}, u32[]{:S(2)}) copy-start(f32[128]{0:T(128)S(1)} %get-tuple-element.38) | copy-start | bytes 1540
  7.5 9.3 %copy-start.18 = (s32[1,1,1,128]{3,2,1,0:T(1,128)S(1)}, s32[1,1,1,128]{3,2,1,0:T(1,128)}, u32[]{:S(2)}) copy-start(s32[1,1,1,128]{3,2,1,0:T(1,128)} %param.9) | copy-start | bytes 1540
  12.9 44.6 %copy-start.13 = (f32[512]{0:T(512)S(1)}, f32[512]{0:T(512)}, u32[]{:S(2)}) copy-start(f32[512]{0:T(512)} %param.12) | copy-start | bytes 6148
  12.9 55.3 %copy-start.10 = (f32[3,1,1,1,8192]{4,3,2,1,0:T(1,128)S(1)}, f32[3,1,1,1,8192]{4,3,2,1,0:T(1,128)}, u32[]{:S(2)}) copy-start(f32[3,1,1,1,8192]{4,3,2,1,0:T(1,128)} %param.7) | copy-start | bytes 294916
  12.9 56.2 %copy-start.2 = (bf16[4,512,512]{2,1,0:T(8,128)(2,1)S(1)}, bf16[4,512,512]{2,1,0:T(8,128)(2,1)}, u32[]{:S(2)}) copy-start(bf16[4,512,512]{2,1,0:T(8,128)(2,1)} %param.11) | copy-start | bytes 6291460
  18.7 87.2 %collective-permute-start = (bf16[6,6,512]{2,1,0:T(8,128)(2,1)}, bf16[6,6,512]{2,1,0:T(8,128)(2,1)}, u32[]{:S(2)}, u32[]{:S(2)}) collective-permute-start(bf16[6,6,512]{2,1,0:T(8,128)(2,1)} %squeeze.21), channel_id=1, source_target_pairs={{0,384},{128,0},{256,128},{384,256},{1,385},{129,1},{257,129},{385... | collective-permute-start | bytes 110600 | tf_op jit(solution)/shard_map/ppermute | solution.py:20
  28.1 82.0 %collective-permute-start.1 = (bf16[6,6,512]{2,1,0:T(8,128)(2,1)}, bf16[6,6,512]{2,1,0:T(8,128)(2,1)}, u32[]{:S(2)}, u32[]{:S(2)}) collective-permute-start(bf16[6,6,512]{2,1,0:T(8,128)(2,1)} %squeeze.23), channel_id=1, source_target_pairs={{0,128},{128,256},{256,384},{384,0},{1,129},{129,257},{257,385},{3... | collective-permute-start | bytes 110600 | tf_op jit(solution)/shard_map/ppermute | solution.py:20
  38.8 73.0 %collective-permute-start.2 = (bf16[6,6,512]{2,1,0:T(8,128)(2,1)}, bf16[6,6,512]{2,1,0:T(8,128)(2,1)}, u32[]{:S(2)}, u32[]{:S(2)}) collective-permute-start(bf16[6,6,512]{2,1,0:T(8,128)(2,1)} %get-tuple-element.20), channel_id=1, source_target_pairs={{0,96},{32,0},{64,32},{96,64},{1,97},{33,1},{65,33},{97,65},{2,98}... | collective-permute-start | bytes 110600 | tf_op jit(solution)/shard_map/ppermute | solution.py:20
  43.2 71.3 %collective-permute-start.3 = (bf16[6,6,512]{2,1,0:T(8,128)(2,1)}, bf16[6,6,512]{2,1,0:T(8,128)(2,1)}, u32[]{:S(2)}, u32[]{:S(2)}) collective-permute-start(bf16[6,6,512]{2,1,0:T(8,128)(2,1)} %get-tuple-element.19), channel_id=1, source_target_pairs={{0,32},{32,64},{64,96},{96,0},{1,33},{33,65},{65,97},{97,1},{2,34}... | collective-permute-start | bytes 110600 | tf_op jit(solution)/shard_map/ppermute | solution.py:20
  45.8 67.7 %collective-permute-start.4 = (bf16[6,6,512]{2,1,0:T(8,128)(2,1)}, bf16[6,6,512]{2,1,0:T(8,128)(2,1)}, u32[]{:S(2)}, u32[]{:S(2)}) collective-permute-start(bf16[6,6,512]{2,1,0:T(8,128)(2,1)} %bitcast.119), channel_id=1, source_target_pairs={{0,31},{1,0},{2,1},{3,2},{4,3},{5,4},{6,5},{7,6},{8,7},{9,8},{10,9... | collective-permute-start | bytes 110600 | tf_op jit(solution)/shard_map/ppermute | solution.py:20
  60.0 17.5 %all-to-all-start = ((f32[32,1,8]{2,1,0:T(1,128)}), f32[32,1,8]{2,1,0:T(1,128)}, u32[]{:S(2)}, u32[]{:S(2)}) async-start(f32[32,1,8]{2,1,0:T(1,128)} %broadcast_in_dim.65), calls=%async_computation | async-start | bytes 32768 | tf_op jit(solution)/shard_map/all_to_all | solution.py:128
  80.7 24.3 %all-to-all-start.1 = ((f32[16,1,8]{2,1,0:T(1,128)}), f32[16,1,8]{2,1,0:T(1,128)S(1)}, u32[]{:S(2)}, u32[]{:S(2)}) async-start(f32[16,1,8]{2,1,0:T(1,128)} %copy.41), calls=%async_computation.1 | async-start | bytes 16384 | tf_op jit(solution)/shard_map/all_to_all | solution.py:131
  105.9 19.7 %collective-permute-start.5 = (bf16[6,6,512]{2,1,0:T(8,128)(2,1)}, bf16[6,6,512]{2,1,0:T(8,128)(2,1)}, u32[]{:S(2)}, u32[]{:S(2)}) collective-permute-start(bf16[6,6,512]{2,1,0:T(8,128)(2,1)} %bitcast.118), channel_id=1, source_target_pairs={{0,1},{1,2},{2,3},{3,4},{4,5},{5,6},{6,7},{7,8},{8,9},{9,10},{10,1... | collective-permute-start | bytes 110600 | tf_op jit(solution)/shard_map/ppermute | solution.py:20
  128.4 3.8 %copy-start.5 = (bf16[216,512]{1,0:T(8,128)(2,1)S(1)}, bf16[216,512]{1,0:T(8,128)(2,1)}, u32[]{:S(2)}) copy-start(bf16[216,512]{1,0:T(8,128)(2,1)} %reshape.440) | copy-start | bytes 663556
  128.4 4.1 %copy-start.4 = (bf16[216,512]{1,0:T(8,128)(2,1)S(1)}, bf16[216,512]{1,0:T(8,128)(2,1)}, u32[]{:S(2)}) copy-start(bf16[216,512]{1,0:T(8,128)(2,1)} %reshape.441) | copy-start | bytes 663556
  128.4 4.5 %copy-start.6 = (bf16[216,512]{1,0:T(8,128)(2,1)S(1)}, bf16[216,512]{1,0:T(8,128)(2,1)}, u32[]{:S(2)}) copy-start(bf16[216,512]{1,0:T(8,128)(2,1)} %reshape.442) | copy-start | bytes 663556
  128.4 4.5 %copy-start.14 = (f32[512]{0:T(512)S(1)}, f32[512]{0:T(512)}, u32[]{:S(2)}) copy-start(f32[512]{0:T(512)} %param.12) | copy-start | bytes 6148
  128.4 4.5 %copy-start.16 = (f32[216]{0:T(256)S(1)}, f32[216]{0:T(256)}, u32[]{:S(2)}) copy-start(f32[216]{0:T(256)} %broadcast_in_dim.68) | copy-start | bytes 2596
  132.2 2.1 %copy-start.19 = (pred[128]{0:T(512)(128)(4,1)S(1)}, pred[128]{0:T(512)(128)(4,1)}, u32[]{:S(2)}) copy-start(pred[128]{0:T(512)(128)(4,1)} %compare_and_fusion) | copy-start | bytes 388
  133.2 5.6 %copy-start.3 = (f32[8,128,64]{2,0,1:T(8,128)S(1)}, f32[8,128,64]{2,0,1:T(8,128)}, u32[]{:S(2)}) copy-start(f32[8,128,64]{2,0,1:T(8,128)} %get-tuple-element.30) | copy-start | bytes 786436
  134.4 10.3 %copy-start.8 = (f32[8,128,64]{2,0,1:T(8,128)S(1)}, f32[8,128,64]{2,0,1:T(8,128)}, u32[]{:S(2)}) copy-start(f32[8,128,64]{2,0,1:T(8,128)} %get-tuple-element.27) | copy-start | bytes 786436
  134.4 10.3 %copy-start.9 = (f32[8,128,64]{2,0,1:T(8,128)S(1)}, f32[8,128,64]{2,0,1:T(8,128)}, u32[]{:S(2)}) copy-start(f32[8,128,64]{2,0,1:T(8,128)} %get-tuple-element.29) | copy-start | bytes 786436
  138.8 5.9 %copy-start.1 = (f32[128,8,8,8]{3,2,1,0:T(8,128)S(1)}, f32[128,8,8,8]{3,2,1,0:T(8,128)}, u32[]{:S(2)}) copy-start(f32[128,8,8,8]{3,2,1,0:T(8,128)} %copy.43) | copy-start | bytes 786436
  144.7 5.2 %copy-start.11 = (f32[128,64]{1,0:T(8,128)S(1)}, f32[128,64]{1,0:T(8,128)}, u32[]{:S(2)}) copy-start(f32[128,64]{1,0:T(8,128)} %get-tuple-element.7) | copy-start | bytes 98308
  144.7 5.2 %copy-start.7 = (f32[3,128,64]{2,1,0:T(8,128)S(1)}, f32[3,128,64]{2,1,0:T(8,128)}, u32[]{:S(2)}) copy-start(f32[3,128,64]{2,1,0:T(8,128)} %add_multiply_fusion) | copy-start | bytes 294916
  144.7 6.0 %copy-start.12 = (f32[8192]{0:T(1024)S(1)}, f32[8192]{0:T(1024)}, u32[]{:S(2)}) copy-start(f32[8192]{0:T(1024)} %multiply_negate_fusion) | copy-start | bytes 98308
  150.7 0.8 copy-start.15

commit v2 on v0

v2 whole, which is shorter than its diff:
```python
import math

import jax
import jax.numpy as jnp
from jax import lax
from jax.experimental import pallas as pl
from jax.experimental.pallas import tpu as pltpu
from jax.sharding import PartitionSpec as P

TL = 8
TP = 512
CS = 64
TD = 6
CUBES = TD**3
FACE = 48
GRID_ROWS = 256
EXT_ROWS = 640
HALF = CS
LANES = 128


def iota(shape, axis):
    return lax.broadcasted_iota(jnp.int32, shape, axis)


def tile_coords(tile):
    plane = (tile * 10923) >> 16
    tx = (tile * 1821) >> 16
    return tx, plane - tx * TD, tile - plane * TD


def to_clusters(upper, lower):
    both = jnp.concatenate([upper, lower], axis=0).T
    even, odd = both[:HALF], both[HALF:]
    left = iota((HALF, LANES), 1) < HALF
    return (
        jnp.where(left, even, pltpu.roll(odd, HALF, 1)),
        jnp.where(left, pltpu.roll(even, HALF, 1), odd),
    )


def to_atoms(upper, lower):
    left = iota((HALF, LANES), 1) < HALF
    even = jnp.where(left, upper, pltpu.roll(lower, HALF, 1))
    odd = jnp.where(left, pltpu.roll(upper, HALF, 1), lower)
    both = jnp.concatenate([even, odd], axis=0).T
    return both[:HALF], both[HALF:]


def bump(offset):
    return jnp.exp(-0.5 * offset * offset)


def face_tile(face, row):
    if face < 2:
        tile = row + face * 180
    elif face < 4:
        line = (row * 10923) >> 16
        tile = line * 36 + (row - line * TD) + (face - 2) * 30
    else:
        tile = row * TD + (face - 4) * 5
    return jnp.where(row < TD * TD, tile, -1)


def spread_kernel(
    live_ref, pos_ref, charge_ref, tile_ref, weights_ref,
    grid_ref, face_x_ref, face_y_ref, low_z_ref, high_z_ref, coarse_ref, coord_ref, tiles_ref, charge_out_ref,
    wx_ref, wy_ref, wz_ref, cell_ref,
):
    cluster = 2 * iota((HALF, LANES), 0) + (iota((HALF, LANES), 1) >> 6)
    charge = charge_ref[...] * (cluster < live_ref[0, 0]).astype(jnp.float32)
    charge_out_ref[...] = charge
    x, y = to_clusters(pos_ref[0], pos_ref[1])
    z, q = to_clusters(pos_ref[2], charge)
    coord_ref[0], coord_ref[1], coord_ref[2] = x, y, z
    for node in range(TL):
        wx_ref[node] = q * bump(x - node)
        wy_ref[node] = bump(y - node)
    nodes = iota((TL, LANES), 0).astype(jnp.float32)
    for atom in range(CS):
        wz_ref[atom] = bump(z[atom : atom + 1] - nodes)

    own = iota((LANES, LANES), 0)
    at = iota((LANES, LANES), 1)
    order = (own == jnp.where(at < HALF, 2 * at, 2 * at - 127)).astype(jnp.bfloat16)
    ids = jnp.broadcast_to(tile_ref[...].astype(jnp.float32), (8, LANES)).astype(jnp.bfloat16)
    tiles = jnp.dot(ids, order, preferred_element_type=jnp.float32)
    tiles_ref[...] = tiles
    tiles = tiles[:1].astype(jnp.int32)

    for half in range(2):

        def step(atom, total, half=half):
            row = pl.ds(atom, 1)
            wz = wz_ref[atom]
            line = [wy_ref[j, row, :] * wz for j in range(TL)]
            new = []
            for i in range(4):
                wx = jnp.broadcast_to(wx_ref[4 * half + i, row, :], (TL, LANES))
                new += [total[8 * i + j] + wx * line[j] for j in range(TL)]
            return tuple(new)

        start = tuple(jnp.zeros((TL, LANES), jnp.float32) for _ in range(32))
        total = lax.fori_loop(0, CS, step, start, unroll=4)
        for slot in range(32):
            cell_ref[pl.ds((32 * half + slot) * TL, TL), :] = total[slot]

    cell = cell_ref[...]
    high = cell.astype(jnp.bfloat16)
    low = (cell - high.astype(jnp.float32)).astype(jnp.bfloat16)
    cells = jnp.concatenate([high, low], axis=1)

    def gathered(rows_tile):
        hot = (rows_tile == tiles).astype(jnp.bfloat16)
        return lax.dot_general(
            jnp.concatenate([hot, hot], axis=1), cells, (((1,), (1,)), ((), ())), preferred_element_type=jnp.float32
        )

    fine = gathered(iota((GRID_ROWS, LANES), 0))
    grid_ref[...] = fine.astype(jnp.bfloat16)
    faces = gathered(jnp.concatenate([face_tile(f, iota((FACE, LANES), 0)) for f in range(6)], axis=0))
    faces = faces.astype(jnp.bfloat16)
    low_z_ref[...] = faces[4 * FACE : 5 * FACE]
    high_z_ref[...] = faces[5 * FACE :]
    for ref, axis, first in ((face_x_ref, "gx", 0), (face_y_ref, "gy", 2)):
        me, count = lax.axis_index(axis), lax.axis_size(axis)
        ref[lax.rem(me + count - 1, count)] = faces[first * FACE : (first + 1) * FACE]
        ref[lax.rem(me + 1, count)] = faces[(first + 1) * FACE : (first + 2) * FACE]

    moments = jnp.sum(fine * weights_ref[...], axis=1, keepdims=True)
    tx, ty, tz = tile_coords(iota((GRID_ROWS, LANES), 0))
    corner = ((tx >= 3).astype(jnp.int32) * 2 + (ty >= 3).astype(jnp.int32)) * 2 + (tz >= 3).astype(jnp.int32)
    mine = corner == (iota((GRID_ROWS, LANES), 1) & 7)
    coarse = jnp.sum(jnp.where(mine, moments, 0.0), axis=0, keepdims=True)
    coarse = coarse * (1.0 / math.sqrt(TP * 27))
    for line in range(coarse_ref.shape[0]):
        coarse_ref[line] = coarse


def coarse_kernel(column_ref, top_ref, out_ref):
    lines = column_ref.shape[0]
    column = column_ref[...].reshape(lines, LANES)
    column = jnp.concatenate([column] * (lines * 8 // LANES), axis=1)
    shape = column.shape
    column = jnp.sum(jnp.where((iota(shape, 1) >> 3) == iota(shape, 0), column, 0.0), axis=0, keepdims=True)
    partial_value = jnp.sum(top_ref[...] * column, axis=1, keepdims=True)
    rows = partial_value.shape[0]
    lanes = jnp.where((iota((rows, LANES), 1) & 7) == (iota((rows, LANES), 0) & 7), partial_value, 0.0)
    lanes = jnp.sum(lanes.reshape(rows // 8, 8, LANES), axis=1)
    for brick in range(rows // 8):
        out_ref[brick] = lanes[brick : brick + 1]


ATOM_ROWS = 16


def gradients(field_ref, wx, wy, wz, x, y, z):
    sums = [None] * 4
    for i in reversed(range(TL)):
        a = b = c = None
        for j in reversed(range(TL)):
            run = mean = None
            for k in reversed(range(TL)):
                term = wz[k] * field_ref[(i * TL + j) * TL + k : (i * TL + j) * TL + k + 1, :]
                run = term if run is None else run + term
                if k:
                    mean = run if mean is None else mean + run
            part = wy[j] * run
            cross = wy[j] * mean
            a = part if a is None else a + part
            c = cross if c is None else c + cross
            if j:
                b = a if b is None else b + a
        for at, value in enumerate((a, b, c)):
            term = wx[i] * value
            sums[at] = term if sums[at] is None else sums[at] + term
        if i:
            sums[3] = sums[0] if sums[3] is None else sums[3] + sums[0]
    total, with_y, with_z, with_x = sums
    return with_x - x * total, with_y - y * total, with_z - z * total


def near_kernel(
    tiles_ref, grid_ref, face_x_ref, face_y_ref, up_z_ref, down_z_ref, blocks_ref, coord_ref, weights_ref,
    near_ref, unit_ref,
    ext_ref, field_ref, flat_ref, grad_ref,
):
    ext_ref[0:GRID_ROWS] = grid_ref[...]
    faces = []
    for ref, axis in ((face_x_ref, "gx"), (face_y_ref, "gy")):
        me, count = lax.axis_index(axis), lax.axis_size(axis)
        faces += [ref[lax.rem(me + 1, count)], ref[lax.rem(me + count - 1, count)]]
    faces += [up_z_ref[...], down_z_ref[...]]
    for at, face in enumerate(faces):
        ext_ref[GRID_ROWS + at * FACE : GRID_ROWS + (at + 1) * FACE] = face
    ext_ref[GRID_ROWS + 6 * FACE :] = jnp.zeros((EXT_ROWS - GRID_ROWS - 6 * FACE, TP), jnp.bfloat16)

    tile = jnp.broadcast_to(tiles_ref[:1], (LANES, LANES)).T[:, :1].astype(jnp.int32)
    tx, ty, tz = tile_coords(tile)
    edges = ((tx, 36, ty * TD + tz), (ty, TD, tx * TD + tz), (tz, 1, tx * TD + ty))
    targets = [tile]
    for at, (place, stride, row) in enumerate(edges):
        base = GRID_ROWS + 2 * at * FACE
        targets.append(jnp.where(place < TD - 1, tile + stride, base + row))
        targets.append(jnp.where(place > 0, tile - stride, base + FACE + row))
    at_row = iota((LANES, EXT_ROWS), 1)
    field = None
    for at, target in enumerate(targets):
        hot = (at_row == target).astype(jnp.bfloat16)
        rows = jnp.dot(hot, ext_ref[...], preferred_element_type=jnp.float32).astype(jnp.bfloat16)
        flipped = at > 0 and at % 2 == 0
        term = lax.dot_general(
            rows, blocks_ref[(at + 1) // 2], (((1,), (0 if flipped else 1,)), ((), ())), preferred_element_type=jnp.float32
        )
        field = term if field is None else field + term
    for part in range(TP // LANES):
        field_ref[part * LANES : (part + 1) * LANES, :] = field[:, part * LANES : (part + 1) * LANES].T
        flat_ref[part * LANES : (part + 1) * LANES, :] = jnp.broadcast_to(
            weights_ref[:, part * LANES : (part + 1) * LANES], (LANES, LANES)
        ).T

    @pl.loop(0, CS // ATOM_ROWS)
    def _(group):
        rows = pl.ds(pl.multiple_of(group * ATOM_ROWS, ATOM_ROWS), ATOM_ROWS)
        x, y, z = coord_ref[0, rows, :], coord_ref[1, rows, :], coord_ref[2, rows, :]
        wx, wy, wz = ([bump(u - node) for node in range(TL)] for u in (x, y, z))
        for which, ref in enumerate((field_ref, flat_ref)):
            for axis, value in enumerate(gradients(ref, wx, wy, wz, x, y, z)):
                grad_ref[3 * which + axis, rows, :] = value

    near_ref[0], near_ref[1] = to_atoms(grad_ref[0], grad_ref[1])
    near_ref[2], unit_ref[0] = to_atoms(grad_ref[2], grad_ref[3])
    unit_ref[1], unit_ref[2] = to_atoms(grad_ref[4], grad_ref[5])


def final_kernel(parts_ref, tile_ref, near_ref, unit_ref, pos_ref, charge_ref, force_ref, virial_ref):
    bricks = parts_ref.shape[0]
    coarse = jnp.sum(parts_ref[...].reshape(bricks, LANES), axis=0, keepdims=True)
    tile_row = tile_ref[...].astype(jnp.float32)
    mine = ((iota((HALF, LANES), 1) >> 1) == iota((HALF, LANES), 0))
    rows = jnp.where(mine, tile_row, 0.0).astype(jnp.bfloat16)
    side = ((iota((LANES, LANES), 0) & 1) == (iota((LANES, LANES), 1) >> 6)).astype(jnp.bfloat16)
    tile = jnp.dot(rows, side, preferred_element_type=jnp.float32).astype(jnp.int32)
    coords = tile_coords(tile)
    corner = jnp.zeros((HALF, LANES), jnp.int32)
    for place in coords:
        corner = corner * 2 + (place >= 3).astype(jnp.int32)
    pot = jnp.zeros((HALF, LANES), jnp.float32)
    for at in range(8):
        pot = jnp.where(corner == at, coarse[:, at : at + 1], pot)
    charge = charge_ref[...]
    forces, fracs = [], []
    for axis in range(3):
        forces.append(-charge * (near_ref[axis] + pot * unit_ref[axis]))
        fracs.append((coords[axis].astype(jnp.float32) * TL + pos_ref[axis]) * (1.0 / (TL * TD)))
        force_ref[axis] = forces[axis]
        virial_ref[axis] = fracs[axis] * forces[axis]
    virial_ref[3] = fracs[0] * forces[1]
    virial_ref[4] = fracs[0] * forces[2]
    virial_ref[5] = fracs[1] * forces[2]


VMEM = pl.BlockSpec(memory_space=pltpu.VMEM)
SMEM = pl.BlockSpec(memory_space=pltpu.SMEM)


def f32(*shape):
    return jax.ShapeDtypeStruct(shape, jnp.float32)


def bf16(*shape):
    return jax.ShapeDtypeStruct(shape, jnp.bfloat16)


def shifted(value, axis, steps):
    count = lax.axis_size(axis)
    return lax.ppermute(value, axis, [(source, (source + steps) % count) for source in range(count)])


def shards(positions, charges, cluster_tile, live_clusters, kernel_blocks, restrict_weights, top_kernel):
    pos = positions.reshape(3, HALF, LANES)
    charge = charges.reshape(HALF, LANES)
    tile = cluster_tile.reshape(1, LANES)
    live = live_clusters.reshape(1, 1)
    weights = restrict_weights.reshape(1, TP)
    lines, wide, high = lax.axis_size("gz"), lax.axis_size("gx"), lax.axis_size("gy")

    grid, face_x, face_y, low_z, high_z, coarse, coords, tiles, charge = pl.pallas_call(
        spread_kernel,
        out_shape=(
            bf16(GRID_ROWS, TP), bf16(wide, FACE, TP), bf16(high, FACE, TP), bf16(FACE, TP), bf16(FACE, TP),
            f32(lines, 1, LANES), f32(3, CS, LANES), f32(8, LANES), f32(HALF, LANES),
        ),
        in_specs=[SMEM] + [VMEM] * 4,
        out_specs=[VMEM] * 9,
        scratch_shapes=[
            pltpu.VMEM((TL, CS, LANES), jnp.float32), pltpu.VMEM((TL, CS, LANES), jnp.float32),
            pltpu.VMEM((CS, TL, LANES), jnp.float32), pltpu.VMEM((TP, LANES), jnp.float32),
        ],
        compiler_params=pltpu.CompilerParams(vmem_limit_bytes=16 << 20),
        cost_estimate=pl.CostEstimate(flops=10_000_000, bytes_accessed=1_000_000, transcendentals=200_000),
        name="spread",
    )(live, pos, charge, tile, weights)

    column = lax.all_to_all(coarse, "gz", 0, 0, tiled=True)
    face_x = lax.all_to_all(face_x, "gx", 0, 0, tiled=True)
    face_y = lax.all_to_all(face_y, "gy", 0, 0, tiled=True)
    up_z = shifted(low_z, "gz", -1)
    down_z = shifted(high_z, "gz", 1)

    parts = pl.pallas_call(
        coarse_kernel,
        out_shape=f32(wide * high, 1, LANES),
        in_specs=[VMEM] * 2,
        out_specs=VMEM,
        cost_estimate=pl.CostEstimate(flops=70_000, bytes_accessed=200_000, transcendentals=0),
        name="coarse",
    )(column, top_kernel)
    parts = lax.all_to_all(parts, ("gx", "gy"), 0, 0, tiled=True)

    near, unit = pl.pallas_call(
        near_kernel,
        out_shape=(f32(3, HALF, LANES), f32(3, HALF, LANES)),
        in_specs=[VMEM] * 9,
        out_specs=[VMEM] * 2,
        scratch_shapes=[
            pltpu.VMEM((EXT_ROWS, TP), jnp.bfloat16), pltpu.VMEM((TP, LANES), jnp.float32),
            pltpu.VMEM((TP, LANES), jnp.float32), pltpu.VMEM((6, CS, LANES), jnp.float32),
        ],
        compiler_params=pltpu.CompilerParams(vmem_limit_bytes=24 << 20),
        cost_estimate=pl.CostEstimate(flops=1_000_000_000, bytes_accessed=4_000_000, transcendentals=200_000),
        name="near",
    )(tiles, grid, face_x, face_y, up_z, down_z, kernel_blocks, coords, weights)

    forces, virial = pl.pallas_call(
        final_kernel,
        out_shape=(f32(3, HALF, LANES), f32(6, HALF, LANES)),
        in_specs=[VMEM] * 6,
        out_specs=[VMEM] * 2,
        cost_estimate=pl.CostEstimate(flops=500_000, bytes_accessed=600_000, transcendentals=0),
        name="final",
    )(parts, tile, near, unit, pos, charge)
    return forces.reshape(3, 1, 1, 1, -1), virial.reshape(6, 1, 1, 1, -1)


def solution(mesh):
    placed = (
        P(None, "gx", "gy", "gz", None),
        P("gx", "gy", "gz", None),
        P("gx", "gy", "gz", None),
        P("gx", "gy", "gz"),
        P(),
        P(),
        P("gz", ("gx", "gy")),
    )
    return jax.shard_map(
        shards,
        mesh=mesh,
        in_specs=placed,
        out_specs=(P(None, "gx", "gy", "gz", None), P(None, "gx", "gy", "gz", None)),
        check_vma=False,
    )
```

time: 301 us -> 93.2 us (0.31)
  the two profiles are of different devices: /device:TPU:2 before, /device:TPU:32 now
where the time goes in v2:
time: 93.2 us; the launch traced here: 92.6 us
  blocking collectives  36.9 us (40%)
  starting transfers between devices  16.9 us (18%)
  waiting for transfers between devices  16.7 us (18%)
  Pallas kernels  13.6 us (15%)
  local copies, waits for them, and re-layouts  7.13 us (8%)
  between operations  1.35 us (1%)
    all_to_all x1, blocking collectives, shards(): column = lax.all_to_all(coarse, 'gz', 0, 0, tiled=True)  26.5 us
    all_to_all x1, waiting for transfers between devices, shards(): face_x = lax.all_to_all(face_x, 'gx', 0, 0, tiled=True)  12.8 us
    all_to_all x1, blocking collectives, shards(): face_y = lax.all_to_all(face_y, 'gy', 0, 0, tiled=True)  10.4 us
    all_to_all x1, starting transfers between devices, shards(): face_x = lax.all_to_all(face_x, 'gx', 0, 0, tiled=True)  7.58 us
    pallas_call x1, Pallas kernels, shards(): pl.pallas_call(near_kernel, out_shape=(f32(3, HALF, LANES), f32(3, HALF,...  7.15 us
    unnamed x20, local copies, waits for them, and re-layouts  7.13 us
    ppermute x2, starting transfers between devices, shifted(): lax.ppermute(value, axis, [(source, (source + steps) % count) for source...  5.83 us
    all_to_all x1, waiting for transfers between devices, shards(): parts = lax.all_to_all(parts, ('gx', 'gy'), 0, 0, tiled=True)  3.93 us
  transfers between devices with their start and end apart: 4, of which 2 were waited for; matrix products, arithmetic and copies ran while one was open for 0% of the time, Pallas kernels for 9%

profile of v2, /device:TPU:32, one launch (start us, length us, event | category | flops | bytes accessed | tf_op | source)
XLA Modules:
  0.0 92.6 jit_solution(12248261226026495852)
XLA Ops:
  1.3 0.0 copy-start
  1.3 0.9 copy-done
  2.2 0.0 copy-start.4
  2.2 0.7 copy-done.4
  2.8 0.0 copy-start.6
  2.8 0.8 copy-done.6
  3.6 0.0 copy-start.7
  3.6 0.7 copy-done.7
  4.3 2.9 %spread.1 = (bf16[256,512]{1,0:T(8,128)(2,1)S(1)}, bf16[4,48,512]{2,1,0:T(8,128)(2,1)}, bf16[4,48,512]{2,1,0:T(8,128)(2,1)S(1)}, bf16[48,512]{1,0:T(8,128)(2,1)S...) custom-call(s32[1,1]{1,0:T(1,128)} %bitcast.7.live_ref, ...), custom_call_target="tpu_custom_call" | custom-call | flops 10000000 | bytes 1000000 | tf_op jit(solution)/shard_map/spread/pallas_call | solution.py:288
  7.2 0.0 copy-start.3
  7.2 26.5 %all_to_all.20.column_ref = f32[32,1,128]{2,1,0:T(1,128)} all-to-all(f32[32,1,128]{2,1,0:T(1,128)S(1)} %get-tuple-element.15), channel_id=1, replica_groups=mesh['gx'=4,'gy'=4,'gz'=32] {'gz'}, dimensions={0} | all-to-all | bytes 32768 | tf_op jit(solution)/shard_map/all_to_all | solution.py:305
  33.7 10.4 %all_to_all.21.face_y_ref = bf16[4,48,512]{2,1,0:T(8,128)(2,1)S(1)} all-to-all(bf16[4,48,512]{2,1,0:T(8,128)(2,1)S(1)} %get-tuple-element.19), channel_id=1, replica_groups=mesh['gx'=4,'gy'=4,'gz'=32] {'gy'}, dimensions={0} | all-to-all | bytes 393216 | tf_op jit(solution)/shard_map/all_to_all | solution.py:307
  44.1 0.0 copy-done.3
  44.1 7.6 %all-to-all-start.2 = ((bf16[4,48,512]{2,1,0:T(8,128)(2,1)}), bf16[4,48,512]{2,1,0:T(8,128)(2,1)S(1)}, u32[]{:S(2)}, u32[]{:S(2)}) async-start(bf16[4,48,512]{2,1,0:T(8,128)(2,1)} %get-tuple-element.18), calls=%async_computation.2 | async-start | bytes 393216 | tf_op jit(solution)/shard_map/all_to_all | solution.py:306
  51.7 3.3 %collective-permute-start = (bf16[48,512]{1,0:T(8,128)(2,1)S(1)}, bf16[48,512]{1,0:T(8,128)(2,1)S(1)}, u32[]{:S(2)}, u32[]{:S(2)}) collective-permute-start(bf16[48,512]{1,0:T(8,128)(2,1)S(1)} %get-tuple-element.20), channel_id=1, source_target_pairs={{0,31},{1,0},{2,1},{3,2},{4,3},{5,4},{6,5},{7,6},{8,7},{9,8},{10,9... | collective-permute-start | bytes 147464 | tf_op jit(solution)/shard_map/ppermute | solution.py:277
  55.0 2.5 %collective-permute-start.1 = (bf16[48,512]{1,0:T(8,128)(2,1)S(1)}, bf16[48,512]{1,0:T(8,128)(2,1)S(1)}, u32[]{:S(2)}, u32[]{:S(2)}) collective-permute-start(bf16[48,512]{1,0:T(8,128)(2,1)S(1)} %get-tuple-element.21), channel_id=1, source_target_pairs={{0,1},{1,2},{2,3},{3,4},{4,5},{5,6},{6,7},{7,8},{8,9},{9,10},{10,1... | collective-permute-start | bytes 147464 | tf_op jit(solution)/shard_map/ppermute | solution.py:277
  57.5 1.6 %coarse.1 = f32[16,1,128]{2,1,0:T(1,128)} custom-call(f32[32,1,128]{2,1,0:T(1,128)} %all_to_all.20.column_ref, f32[128,256]{1,0:T(8,128)} %top_ref.1), custom_call_target="tpu_custom_call" | custom-call | flops 70000 | bytes 200000 | tf_op jit(solution)/shard_map/coarse/pallas_call | solution.py:311
  59.2 12.8 %all-to-all-done.2.face_x_ref = bf16[4,48,512]{2,1,0:T(8,128)(2,1)S(1)} async-done(((bf16[4,48,512]{2,1,0:T(8,128)(2,1)}), bf16[4,48,512]{2,1,0:T(8,128)(2,1)S(1)}, u32[]{:S(2)}, u32[]{:S(2)}) %all-to-all-start.2) | async-done | bytes 196640 | tf_op jit(solution)/shard_map/all_to_all | solution.py:306
  71.9 3.5 %all-to-all-start.1 = ((f32[16,1,128]{2,1,0:T(1,128)}), f32[16,1,128]{2,1,0:T(1,128)S(1)}, u32[]{:S(2)}, u32[]{:S(2)}) async-start(f32[16,1,128]{2,1,0:T(1,128)} %coarse.1), calls=%async_computation.1 | async-start | bytes 16384 | tf_op jit(solution)/shard_map/all_to_all | solution.py:319
  75.4 0.0 collective-permute-done.up_z_ref
  75.4 0.0 collective-permute-done.1.down_z_ref
  75.4 0.0 copy-start.5
  75.5 1.6 %copy-done.5 = bf16[4,512,512]{2,1,0:T(8,128)(2,1)S(1)} copy-done((bf16[4,512,512]{2,1,0:T(8,128)(2,1)S(1)}, bf16[4,512,512]{2,1,0:T(8,128)(2,1)}, u32[]{:S(2)}) %copy-start.5) | copy-done | bytes 2097176
  77.0 0.0 copy-start.8
  77.0 0.7 copy-done.8
  77.7 7.1 %near.1 = (f32[3,64,128]{2,1,0:T(8,128)S(1)}, f32[3,64,128]{2,1,0:T(8,128)S(1)}) custom-call(f32[8,128]{1,0:T(8,128)S(1)} %get-tuple-element.16.tiles_ref, bf16[256,512]{1,0:T(8,128)(2,1)S(1)} %get-tuple-element.17.grid_ref, bf16[4,48,512]{2,1,0:T(8,128)(2,1)S(1)} %all-to-all-done.2.face_x_ref, bf16[4,48,512]{2,1,0:T(8,128)(2,1)S(1)} %all_to_all.21.face_y_ref, ...), custom_call_target="tpu_custom_call" | custom-call | flops 1000000000 | bytes 4000000 | tf_op jit(solution)/shard_map/near/pallas_call | solution.py:321
  84.9 0.0 copy-start.1
  84.9 0.6 copy-done.1
  85.5 0.0 copy-start.2
  85.5 0.6 copy-done.2
  86.2 3.9 %all-to-all-done.1.parts_ref = f32[16,1,128]{2,1,0:T(1,128)S(1)} async-done(((f32[16,1,128]{2,1,0:T(1,128)}), f32[16,1,128]{2,1,0:T(1,128)S(1)}, u32[]{:S(2)}, u32[]{:S(2)}) %all-to-all-start.1) | async-done | bytes 8224 | tf_op jit(solution)/shard_map/all_to_all | solution.py:319
  90.1 0.0 copy-start.9
  90.1 0.6 copy-done.9
  90.7 1.9 %final.1 = (f32[3,64,128]{2,1,0:T(8,128)}, f32[6,64,128]{2,1,0:T(8,128)}) custom-call(f32[16,1,128]{2,1,0:T(1,128)} %copy-done.9, s32[1,128]{1,0:T(1,128)} %bitcast.10, f32[3,64,128]{2,1,0:T(8,128)} %copy-done.1, f32[3,64,128]{2,1,0:T(8,128)} %copy-done.2, f32[3,64,128]{2,1,0:T(8,128)} %bitcast.8, f32[64,128]{1,0:T(8,128)} %copy-done.3), custom_call_target="tpu_custom_call" | custom-call | flops 500000 | bytes 600000 | tf_op jit(solution)/shard_map/final/pallas_call | solution.py:335
Async XLA Ops:
  1.3 0.9 copy-start
  2.2 0.7 copy-start.4
  2.8 0.8 copy-start.6
  3.6 0.7 copy-start.7
  7.2 36.9 %copy-start.3 = (f32[64,128]{1,0:T(8,128)}, f32[64,128]{1,0:T(8,128)S(1)}, u32[]{:S(2)}) copy-start(f32[64,128]{1,0:T(8,128)S(1)} %get-tuple-element.25.charge_ref) | copy-start | bytes 98308
  44.1 27.9 %all-to-all-start.2 = ((bf16[4,48,512]{2,1,0:T(8,128)(2,1)}), bf16[4,48,512]{2,1,0:T(8,128)(2,1)S(1)}, u32[]{:S(2)}, u32[]{:S(2)}) async-start(bf16[4,48,512]{2,1,0:T(8,128)(2,1)} %get-tuple-element.18), calls=%async_computation.2 | async-start | bytes 393216 | tf_op jit(solution)/shard_map/all_to_all | solution.py:306
  51.7 23.8 %collective-permute-start = (bf16[48,512]{1,0:T(8,128)(2,1)S(1)}, bf16[48,512]{1,0:T(8,128)(2,1)S(1)}, u32[]{:S(2)}, u32[]{:S(2)}) collective-permute-start(bf16[48,512]{1,0:T(8,128)(2,1)S(1)} %get-tuple-element.20), channel_id=1, source_target_pairs={{0,31},{1,0},{2,1},{3,2},{4,3},{5,4},{6,5},{7,6},{8,7},{9,8},{10,9... | collective-permute-start | bytes 147464 | tf_op jit(solution)/shard_map/ppermute | solution.py:277
  55.0 20.5 %collective-permute-start.1 = (bf16[48,512]{1,0:T(8,128)(2,1)S(1)}, bf16[48,512]{1,0:T(8,128)(2,1)S(1)}, u32[]{:S(2)}, u32[]{:S(2)}) collective-permute-start(bf16[48,512]{1,0:T(8,128)(2,1)S(1)} %get-tuple-element.21), channel_id=1, source_target_pairs={{0,1},{1,2},{2,3},{3,4},{4,5},{5,6},{6,7},{7,8},{8,9},{9,10},{10,1... | collective-permute-start | bytes 147464 | tf_op jit(solution)/shard_map/ppermute | solution.py:277
  71.9 18.1 %all-to-all-start.1 = ((f32[16,1,128]{2,1,0:T(1,128)}), f32[16,1,128]{2,1,0:T(1,128)S(1)}, u32[]{:S(2)}, u32[]{:S(2)}) async-start(f32[16,1,128]{2,1,0:T(1,128)} %coarse.1), calls=%async_computation.1 | async-start | bytes 16384 | tf_op jit(solution)/shard_map/all_to_all | solution.py:319
  75.4 1.6 %copy-start.5 = (bf16[4,512,512]{2,1,0:T(8,128)(2,1)S(1)}, bf16[4,512,512]{2,1,0:T(8,128)(2,1)}, u32[]{:S(2)}) copy-start(bf16[4,512,512]{2,1,0:T(8,128)(2,1)} %blocks_ref.1) | copy-start | bytes 6291460
  77.0 0.7 copy-start.8
  84.9 0.7 copy-start.1
  85.5 0.6 copy-start.2
  90.1 0.6 copy-start.9

commit v3 on v2

--- a/solution.py
+++ b/solution.py
@@ -47,29 +47,35 @@
     return both[:HALF], both[HALF:]
 
 
+def corner_of(places):
+    tx, ty, tz = ((place >= TD // 2).astype(jnp.int32) for place in places)
+    return (tx * 2 + ty) * 2 + tz
+
+
 def bump(offset):
     return jnp.exp(-0.5 * offset * offset)
 
 
-def face_tile(face, row):
-    if face < 2:
-        tile = row + face * 180
-    elif face < 4:
-        line = (row * 10923) >> 16
-        tile = line * 36 + (row - line * TD) + (face - 2) * 30
-    else:
-        tile = row * TD + (face - 4) * 5
-    return jnp.where(row < TD * TD, tile, -1)
-
-
 def spread_kernel(
-    live_ref, pos_ref, charge_ref, tile_ref, weights_ref,
-    grid_ref, face_x_ref, face_y_ref, low_z_ref, high_z_ref, coarse_ref, coord_ref, tiles_ref, charge_out_ref,
-    wx_ref, wy_ref, wz_ref, cell_ref,
+    live_ref, pos_any, charge_any, tile_any, weights_any, blocks_any, top_any,
+    grid_ref, coarse_ref, coord_ref, tiles_ref, drive_ref, frac_ref, corner_ref, weights_ref, blocks_ref, top_ref,
+    pos_ref, charge_ref, tile_ref, wx_ref, wy_ref, wz_ref, cell_ref, sems,
 ):
+    moves = [
+        pltpu.make_async_copy(source, target, sems.at[at])
+        for at, (source, target) in enumerate(
+            (
+                (pos_any, pos_ref), (charge_any, charge_ref), (tile_any, tile_ref),
+                (weights_any, weights_ref), (blocks_any, blocks_ref), (top_any, top_ref),
+            )
+        )
+    ]
+    for move in moves:
+        move.start()
+    for move in moves[:3]:
+        move.wait()
     cluster = 2 * iota((HALF, LANES), 0) + (iota((HALF, LANES), 1) >> 6)
     charge = charge_ref[...] * (cluster < live_ref[0, 0]).astype(jnp.float32)
-    charge_out_ref[...] = charge
     x, y = to_clusters(pos_ref[0], pos_ref[1])
     z, q = to_clusters(pos_ref[2], charge)
     coord_ref[0], coord_ref[1], coord_ref[2] = x, y, z
@@ -108,33 +114,53 @@
     cell = cell_ref[...]
     high = cell.astype(jnp.bfloat16)
     low = (cell - high.astype(jnp.float32)).astype(jnp.bfloat16)
-    cells = jnp.concatenate([high, low], axis=1)
-
-    def gathered(rows_tile):
-        hot = (rows_tile == tiles).astype(jnp.bfloat16)
-        return lax.dot_general(
-            jnp.concatenate([hot, hot], axis=1), cells, (((1,), (1,)), ((), ())), preferred_element_type=jnp.float32
-        )
-
-    fine = gathered(iota((GRID_ROWS, LANES), 0))
+    hot = (iota((GRID_ROWS, LANES), 0) == tiles).astype(jnp.bfloat16)
+    fine = lax.dot_general(
+        jnp.concatenate([hot, hot], axis=1), jnp.concatenate([high, low], axis=1), (((1,), (1,)), ((), ())),
+        preferred_element_type=jnp.float32,
+    )
     grid_ref[...] = fine.astype(jnp.bfloat16)
-    faces = gathered(jnp.concatenate([face_tile(f, iota((FACE, LANES), 0)) for f in range(6)], axis=0))
-    faces = faces.astype(jnp.bfloat16)
-    low_z_ref[...] = faces[4 * FACE : 5 * FACE]
-    high_z_ref[...] = faces[5 * FACE :]
-    for ref, axis, first in ((face_x_ref, "gx", 0), (face_y_ref, "gy", 2)):
-        me, count = lax.axis_index(axis), lax.axis_size(axis)
-        ref[lax.rem(me + count - 1, count)] = faces[first * FACE : (first + 1) * FACE]
-        ref[lax.rem(me + 1, count)] = faces[(first + 1) * FACE : (first + 2) * FACE]
-
+
+    moves[3].wait()
     moments = jnp.sum(fine * weights_ref[...], axis=1, keepdims=True)
     tx, ty, tz = tile_coords(iota((GRID_ROWS, LANES), 0))
-    corner = ((tx >= 3).astype(jnp.int32) * 2 + (ty >= 3).astype(jnp.int32)) * 2 + (tz >= 3).astype(jnp.int32)
-    mine = corner == (iota((GRID_ROWS, LANES), 1) & 7)
+    mine = corner_of((tx, ty, tz)) == (iota((GRID_ROWS, LANES), 1) & 7)
     coarse = jnp.sum(jnp.where(mine, moments, 0.0), axis=0, keepdims=True)
     coarse = coarse * (1.0 / math.sqrt(TP * 27))
     for line in range(coarse_ref.shape[0]):
         coarse_ref[line] = coarse
+
+    own_row = (iota((HALF, LANES), 1) >> 1) == iota((HALF, LANES), 0)
+    rows = jnp.where(own_row, tile_ref[...].astype(jnp.float32), 0.0).astype(jnp.bfloat16)
+    side = ((iota((LANES, LANES), 0) & 1) == (iota((LANES, LANES), 1) >> 6)).astype(jnp.bfloat16)
+    tile = jnp.dot(rows, side, preferred_element_type=jnp.float32).astype(jnp.int32)
+    places = tile_coords(tile)
+    corner_ref[...] = corner_of(places)
+    drive_ref[...] = -charge
+    for axis in range(3):
+        frac_ref[axis] = (places[axis].astype(jnp.float32) * TL + pos_ref[axis]) * (1.0 / (TL * TD))
+    for move in moves[4:]:
+        move.wait()
+
+
+def odd(axis):
+    return lax.axis_index(axis) & 1
+
+
+def face_kernel(grid_ref, near_x_ref, far_x_ref, near_y_ref, far_y_ref, near_z_ref, far_z_ref):
+    row = iota((FACE, GRID_ROWS), 0)
+    line = (row * 10923) >> 16
+    ids = []
+    for axis, (first, step) in zip(
+        ("gx", "gy", "gz"), ((row, 180), (line * 36 + (row - line * TD), 30), (row * TD, 5)), strict=True
+    ):
+        side = odd(axis)
+        ids += [first + step * (1 - side), first + step * side]
+    tile = jnp.where(jnp.concatenate([row] * 6, axis=0) < TD * TD, jnp.concatenate(ids, axis=0), -1)
+    hot = (iota((6 * FACE, GRID_ROWS), 1) == tile).astype(jnp.bfloat16)
+    faces = jnp.dot(hot, grid_ref[...], preferred_element_type=jnp.float32).astype(jnp.bfloat16)
+    for at, ref in enumerate((near_x_ref, far_x_ref, near_y_ref, far_y_ref, near_z_ref, far_z_ref)):
+        ref[...] = faces[at * FACE : (at + 1) * FACE]
 
 
 def coarse_kernel(column_ref, top_ref, out_ref):
@@ -181,18 +207,13 @@
 
 
 def near_kernel(
-    tiles_ref, grid_ref, face_x_ref, face_y_ref, up_z_ref, down_z_ref, blocks_ref, coord_ref, weights_ref,
+    tiles_ref, grid_ref, near_x_ref, far_x_ref, near_y_ref, far_y_ref, near_z_ref, far_z_ref, blocks_ref, coord_ref, weights_ref,
     near_ref, unit_ref,
     ext_ref, field_ref, flat_ref, grad_ref,
 ):
     ext_ref[0:GRID_ROWS] = grid_ref[...]
-    faces = []
-    for ref, axis in ((face_x_ref, "gx"), (face_y_ref, "gy")):
-        me, count = lax.axis_index(axis), lax.axis_size(axis)
-        faces += [ref[lax.rem(me + 1, count)], ref[lax.rem(me + count - 1, count)]]
-    faces += [up_z_ref[...], down_z_ref[...]]
-    for at, face in enumerate(faces):
-        ext_ref[GRID_ROWS + at * FACE : GRID_ROWS + (at + 1) * FACE] = face
+    for at, ref in enumerate((near_x_ref, far_x_ref, near_y_ref, far_y_ref, near_z_ref, far_z_ref)):
+        ext_ref[GRID_ROWS + at * FACE : GRID_ROWS + (at + 1) * FACE] = ref[...]
     ext_ref[GRID_ROWS + 6 * FACE :] = jnp.zeros((EXT_ROWS - GRID_ROWS - 6 * FACE, TP), jnp.bfloat16)
 
     tile = jnp.broadcast_to(tiles_ref[:1], (LANES, LANES)).T[:, :1].astype(jnp.int32)
@@ -200,9 +221,10 @@
     edges = ((tx, 36, ty * TD + tz), (ty, TD, tx * TD + tz), (tz, 1, tx * TD + ty))
     targets = [tile]
     for at, (place, stride, row) in enumerate(edges):
-        base = GRID_ROWS + 2 * at * FACE
-        targets.append(jnp.where(place < TD - 1, tile + stride, base + row))
-        targets.append(jnp.where(place > 0, tile - stride, base + FACE + row))
+        base = GRID_ROWS + 2 * at * FACE + row
+        side = odd(("gx", "gy", "gz")[at])
+        targets.append(jnp.where(place < TD - 1, tile + stride, base + side * FACE))
+        targets.append(jnp.where(place > 0, tile - stride, base + (1 - side) * FACE))
     at_row = iota((LANES, EXT_ROWS), 1)
     field = None
     for at, target in enumerate(targets):
@@ -233,35 +255,25 @@
     unit_ref[1], unit_ref[2] = to_atoms(grad_ref[4], grad_ref[5])
 
 
-def final_kernel(parts_ref, tile_ref, near_ref, unit_ref, pos_ref, charge_ref, force_ref, virial_ref):
-    bricks = parts_ref.shape[0]
-    coarse = jnp.sum(parts_ref[...].reshape(bricks, LANES), axis=0, keepdims=True)
-    tile_row = tile_ref[...].astype(jnp.float32)
-    mine = ((iota((HALF, LANES), 1) >> 1) == iota((HALF, LANES), 0))
-    rows = jnp.where(mine, tile_row, 0.0).astype(jnp.bfloat16)
-    side = ((iota((LANES, LANES), 0) & 1) == (iota((LANES, LANES), 1) >> 6)).astype(jnp.bfloat16)
-    tile = jnp.dot(rows, side, preferred_element_type=jnp.float32).astype(jnp.int32)
-    coords = tile_coords(tile)
-    corner = jnp.zeros((HALF, LANES), jnp.int32)
-    for place in coords:
-        corner = corner * 2 + (place >= 3).astype(jnp.int32)
+def final_kernel(parts_ref, corner_ref, near_ref, unit_ref, frac_ref, drive_ref, force_ref, virial_ref):
+    coarse = jnp.sum(parts_ref[...].reshape(parts_ref.shape[0], LANES), axis=0, keepdims=True)
+    corner = corner_ref[...]
     pot = jnp.zeros((HALF, LANES), jnp.float32)
     for at in range(8):
         pot = jnp.where(corner == at, coarse[:, at : at + 1], pot)
-    charge = charge_ref[...]
-    forces, fracs = [], []
+    drive = drive_ref[...]
+    forces = [drive * (near_ref[axis] + pot * unit_ref[axis]) for axis in range(3)]
     for axis in range(3):
-        forces.append(-charge * (near_ref[axis] + pot * unit_ref[axis]))
-        fracs.append((coords[axis].astype(jnp.float32) * TL + pos_ref[axis]) * (1.0 / (TL * TD)))
         force_ref[axis] = forces[axis]
-        virial_ref[axis] = fracs[axis] * forces[axis]
-    virial_ref[3] = fracs[0] * forces[1]
-    virial_ref[4] = fracs[0] * forces[2]
-    virial_ref[5] = fracs[1] * forces[2]
+        virial_ref[axis] = frac_ref[axis] * forces[axis]
+    virial_ref[3] = frac_ref[0] * forces[1]
+    virial_ref[4] = frac_ref[0] * forces[2]
+    virial_ref[5] = frac_ref[1] * forces[2]
 
 
 VMEM = pl.BlockSpec(memory_space=pltpu.VMEM)
 SMEM = pl.BlockSpec(memory_space=pltpu.SMEM)
+ANY = pl.BlockSpec(memory_space=pltpu.HBM)
 
 
 def f32(*shape):
@@ -272,9 +284,9 @@
     return jax.ShapeDtypeStruct(shape, jnp.bfloat16)
 
 
-def shifted(value, axis, steps):
+def exchanged(value, axis, far):
     count = lax.axis_size(axis)
-    return lax.ppermute(value, axis, [(source, (source + steps) % count) for source in range(count)])
+    return lax.ppermute(value, axis, [(i, (i + (1 if (i + far) % 2 == 0 else -1)) % count) for i in range(count)])
 
 
 def shards(positions, charges, cluster_tile, live_clusters, kernel_blocks, restrict_weights, top_kernel):
@@ -283,63 +295,75 @@
     tile = cluster_tile.reshape(1, LANES)
     live = live_clusters.reshape(1, 1)
     weights = restrict_weights.reshape(1, TP)
-    lines, wide, high = lax.axis_size("gz"), lax.axis_size("gx"), lax.axis_size("gy")
-
-    grid, face_x, face_y, low_z, high_z, coarse, coords, tiles, charge = pl.pallas_call(
+    lines, bricks = lax.axis_size("gz"), lax.axis_size(("gx", "gy"))
+
+    grid, coarse, coords, tiles, drive, frac, corner, weights, blocks, top = pl.pallas_call(
         spread_kernel,
         out_shape=(
-            bf16(GRID_ROWS, TP), bf16(wide, FACE, TP), bf16(high, FACE, TP), bf16(FACE, TP), bf16(FACE, TP),
-            f32(lines, 1, LANES), f32(3, CS, LANES), f32(8, LANES), f32(HALF, LANES),
+            bf16(GRID_ROWS, TP), f32(lines, 1, LANES), f32(3, CS, LANES), f32(8, LANES), f32(HALF, LANES),
+            f32(3, HALF, LANES), jax.ShapeDtypeStruct((HALF, LANES), jnp.int32), f32(1, TP),
+            bf16(*kernel_blocks.shape), f32(*top_kernel.shape),
         ),
-        in_specs=[SMEM] + [VMEM] * 4,
-        out_specs=[VMEM] * 9,
+        in_specs=[SMEM] + [ANY] * 6,
+        out_specs=[VMEM] * 10,
         scratch_shapes=[
+            pltpu.VMEM((3, HALF, LANES), jnp.float32), pltpu.VMEM((HALF, LANES), jnp.float32),
+            pltpu.VMEM((1, LANES), jnp.int32),
             pltpu.VMEM((TL, CS, LANES), jnp.float32), pltpu.VMEM((TL, CS, LANES), jnp.float32),
             pltpu.VMEM((CS, TL, LANES), jnp.float32), pltpu.VMEM((TP, LANES), jnp.float32),
+            pltpu.SemaphoreType.DMA((6,)),
         ],
-        compiler_params=pltpu.CompilerParams(vmem_limit_bytes=16 << 20),
+        compiler_params=pltpu.CompilerParams(vmem_limit_bytes=12 << 20),
         cost_estimate=pl.CostEstimate(flops=10_000_000, bytes_accessed=1_000_000, transcendentals=200_000),
         name="spread",
-    )(live, pos, charge, tile, weights)
-
+    )(live, *(pltpu.with_memory_space_constraint(a, pltpu.HBM) for a in (pos, charge, tile, weights, kernel_blocks, top_kernel)))
     column = lax.all_to_all(coarse, "gz", 0, 0, tiled=True)
-    face_x = lax.all_to_all(face_x, "gx", 0, 0, tiled=True)
-    face_y = lax.all_to_all(face_y, "gy", 0, 0, tiled=True)
-    up_z = shifted(low_z, "gz", -1)
-    down_z = shifted(high_z, "gz", 1)
+
+    faces = pl.pallas_call(
+        face_kernel,
+        out_shape=(bf16(FACE, TP),) * 6,
+        in_specs=[VMEM],
+        out_specs=[VMEM] * 6,
+        compiler_params=pltpu.CompilerParams(vmem_limit_bytes=8 << 20),
+        cost_estimate=pl.CostEstimate(flops=80_000_000, bytes_accessed=600_000, transcendentals=0),
+        name="faces",
+    )(grid)
+    faces = [exchanged(face, ("gx", "gy", "gz")[at // 2], at % 2) for at, face in enumerate(faces)]
 
     parts = pl.pallas_call(
         coarse_kernel,
-        out_shape=f32(wide * high, 1, LANES),
+        out_shape=f32(bricks, 1, LANES),
         in_specs=[VMEM] * 2,
         out_specs=VMEM,
+        compiler_params=pltpu.CompilerParams(vmem_limit_bytes=8 << 20),
         cost_estimate=pl.CostEstimate(flops=70_000, bytes_accessed=200_000, transcendentals=0),
         name="coarse",
-    )(column, top_kernel)
+    )(column, top)
     parts = lax.all_to_all(parts, ("gx", "gy"), 0, 0, tiled=True)
 
     near, unit = pl.pallas_call(
         near_kernel,
         out_shape=(f32(3, HALF, LANES), f32(3, HALF, LANES)),
-        in_specs=[VMEM] * 9,
+        in_specs=[VMEM] * 11,
         out_specs=[VMEM] * 2,
         scratch_shapes=[
             pltpu.VMEM((EXT_ROWS, TP), jnp.bfloat16), pltpu.VMEM((TP, LANES), jnp.float32),
             pltpu.VMEM((TP, LANES), jnp.float32), pltpu.VMEM((6, CS, LANES), jnp.float32),
         ],
-        compiler_params=pltpu.CompilerParams(vmem_limit_bytes=24 << 20),
+        compiler_params=pltpu.CompilerParams(vmem_limit_bytes=16 << 20),
         cost_estimate=pl.CostEstimate(flops=1_000_000_000, bytes_accessed=4_000_000, transcendentals=200_000),
         name="near",
-    )(tiles, grid, face_x, face_y, up_z, down_z, kernel_blocks, coords, weights)
+    )(tiles, grid, *faces, blocks, coords, weights)
 
     forces, virial = pl.pallas_call(
         final_kernel,
         out_shape=(f32(3, HALF, LANES), f32(6, HALF, LANES)),
         in_specs=[VMEM] * 6,
         out_specs=[VMEM] * 2,
+        compiler_params=pltpu.CompilerParams(vmem_limit_bytes=8 << 20),
         cost_estimate=pl.CostEstimate(flops=500_000, bytes_accessed=600_000, transcendentals=0),
         name="final",
-    )(parts, tile, near, unit, pos, charge)
+    )(parts, corner, near, unit, frac, drive)
     return forces.reshape(3, 1, 1, 1, -1), virial.reshape(6, 1, 1, 1, -1)
 
 

time: 93.2 us -> 77 us (0.83)
  the two profiles are of different devices: /device:TPU:32 before, /device:TPU:1 now
where the time goes in v3:
time: 77 us; the launch traced here: 76.6 us
  starting transfers between devices  55.4 us (72%)
  Pallas kernels  12.9 us (17%)
  waiting for transfers between devices  6.92 us (9%)
  between operations  1.4 us (2%)
    ppermute x6, starting transfers between devices, exchanged(): lax.ppermute(value, axis, [(i, (i + (1 if (i + far) % 2 == 0 else -1)) %...  38.2 us
    all_to_all x1, starting transfers between devices, shards(): column = lax.all_to_all(coarse, 'gz', 0, 0, tiled=True)  9.9 us
    all_to_all x1, starting transfers between devices, shards(): parts = lax.all_to_all(parts, ('gx', 'gy'), 0, 0, tiled=True)  7.35 us
    pallas_call x1, Pallas kernels, shards(): pl.pallas_call(near_kernel, out_shape=(f32(3, HALF, LANES), f32(3, HALF,...  7.16 us
    all_to_all x1, waiting for transfers between devices, shards(): parts = lax.all_to_all(parts, ('gx', 'gy'), 0, 0, tiled=True)  6.9 us
    pallas_call x1, Pallas kernels, shards(): pl.pallas_call(spread_kernel, out_shape=(bf16(GRID_ROWS, TP), f32(lines,...  3.94 us
  transfers between devices with their start and end apart: 8, of which 1 were waited for; matrix products, arithmetic and copies ran while one was open for 0% of the time, Pallas kernels for 10%

profile of v3, /device:TPU:1, one launch (start us, length us, event | category | flops | bytes accessed | tf_op | source)
XLA Modules:
  0.0 76.6 jit_solution(357497723922521558)
XLA Ops:
  1.3 3.9 %spread.1 = (bf16[256,512]{1,0:T(8,128)(2,1)S(1)}, f32[32,1,128]{2,1,0:T(1,128)}, f32[3,64,128]{2,1,0:T(8,128)S(1)}, f32[8,128]{1,0:T(8,128)S(1)}, f32[64,128]{1...) custom-call(s32[1,1]{1,0:T(1,128)} %bitcast.7.live_ref, ...), custom_call_target="tpu_custom_call" | custom-call | flops 10000000 | bytes 1000000 | tf_op jit(solution)/shard_map/spread/pallas_call | solution.py:300
  5.2 0.2 faces.1
  5.5 8.8 %collective-permute-start = (bf16[48,512]{1,0:T(8,128)(2,1)S(1)}, bf16[48,512]{1,0:T(8,128)(2,1)S(1)}, u32[]{:S(2)}, u32[]{:S(2)}) collective-permute-start(bf16[48,512]{1,0:T(8,128)(2,1)S(1)} %get-tuple-element.27), channel_id=1, source_target_pairs={{0,128},{128,0},{256,384},{384,256},{1,129},{129,1},{257,385},{385... | collective-permute-start | bytes 147464 | tf_op jit(solution)/shard_map/ppermute | solution.py:289
  14.3 9.9 %all-to-all-start = ((f32[32,1,128]{2,1,0:T(1,128)}), f32[32,1,128]{2,1,0:T(1,128)S(1)}, u32[]{:S(2)}, u32[]{:S(2)}) async-start(f32[32,1,128]{2,1,0:T(1,128)} %get-tuple-element.22), calls=%async_computation | async-start | bytes 32768 | tf_op jit(solution)/shard_map/all_to_all | solution.py:320
  24.2 8.1 %collective-permute-start.1 = (bf16[48,512]{1,0:T(8,128)(2,1)S(1)}, bf16[48,512]{1,0:T(8,128)(2,1)S(1)}, u32[]{:S(2)}, u32[]{:S(2)}) collective-permute-start(bf16[48,512]{1,0:T(8,128)(2,1)S(1)} %get-tuple-element.28), channel_id=1, source_target_pairs={{0,384},{128,256},{256,128},{384,0},{1,385},{129,257},{257,129},{3... | collective-permute-start | bytes 147464 | tf_op jit(solution)/shard_map/ppermute | solution.py:289
  32.3 3.1 %collective-permute-start.2 = (bf16[48,512]{1,0:T(8,128)(2,1)S(1)}, bf16[48,512]{1,0:T(8,128)(2,1)S(1)}, u32[]{:S(2)}, u32[]{:S(2)}) collective-permute-start(bf16[48,512]{1,0:T(8,128)(2,1)S(1)} %get-tuple-element.29), channel_id=1, source_target_pairs={{0,32},{32,0},{64,96},{96,64},{1,33},{33,1},{65,97},{97,65},{2,34}... | collective-permute-start | bytes 147464 | tf_op jit(solution)/shard_map/ppermute | solution.py:289
  35.4 3.7 %collective-permute-start.3 = (bf16[48,512]{1,0:T(8,128)(2,1)S(1)}, bf16[48,512]{1,0:T(8,128)(2,1)S(1)}, u32[]{:S(2)}, u32[]{:S(2)}) collective-permute-start(bf16[48,512]{1,0:T(8,128)(2,1)S(1)} %get-tuple-element.30), channel_id=1, source_target_pairs={{0,96},{32,64},{64,32},{96,0},{1,97},{33,65},{65,33},{97,1},{2,98}... | collective-permute-start | bytes 147464 | tf_op jit(solution)/shard_map/ppermute | solution.py:289
  39.2 3.4 %collective-permute-start.4 = (bf16[48,512]{1,0:T(8,128)(2,1)S(1)}, bf16[48,512]{1,0:T(8,128)(2,1)S(1)}, u32[]{:S(2)}, u32[]{:S(2)}) collective-permute-start(bf16[48,512]{1,0:T(8,128)(2,1)S(1)} %get-tuple-element.31), channel_id=1, source_target_pairs={{0,1},{1,0},{2,3},{3,2},{4,5},{5,4},{6,7},{7,6},{8,9},{9,8},{10,11... | collective-permute-start | bytes 147464 | tf_op jit(solution)/shard_map/ppermute | solution.py:289
  42.6 0.0 collective-permute-done.near_x_ref
  42.6 11.0 %collective-permute-start.5 = (bf16[48,512]{1,0:T(8,128)(2,1)S(1)}, bf16[48,512]{1,0:T(8,128)(2,1)S(1)}, u32[]{:S(2)}, u32[]{:S(2)}) collective-permute-start(bf16[48,512]{1,0:T(8,128)(2,1)S(1)} %get-tuple-element.32), channel_id=1, source_target_pairs={{0,31},{1,2},{2,1},{3,4},{4,3},{5,6},{6,5},{7,8},{8,7},{9,10},{10,... | collective-permute-start | bytes 147464 | tf_op jit(solution)/shard_map/ppermute | solution.py:289
  53.6 0.0 all-to-all-done.column_ref
  53.6 0.7 coarse.1
  54.3 7.4 %all-to-all-start.1 = ((f32[16,1,128]{2,1,0:T(1,128)}), f32[16,1,128]{2,1,0:T(1,128)S(1)}, u32[]{:S(2)}, u32[]{:S(2)}) async-start(f32[16,1,128]{2,1,0:T(1,128)} %coarse.1), calls=%async_computation.1 | async-start | bytes 16384 | tf_op jit(solution)/shard_map/all_to_all | solution.py:342
  61.7 0.0 collective-permute-done.1.far_x_ref
  61.7 0.0 collective-permute-done.2.near_y_ref
  61.7 0.0 collective-permute-done.3.far_y_ref
  61.7 0.0 collective-permute-done.4.near_z_ref
  61.7 0.0 collective-permute-done.5.far_z_ref
  61.7 7.2 %near.1 = (f32[3,64,128]{2,1,0:T(8,128)S(1)}, f32[3,64,128]{2,1,0:T(8,128)S(1)}) custom-call(f32[8,128]{1,0:T(8,128)S(1)} %get-tuple-element.25.tiles_ref, bf16[256,512]{1,0:T(8,128)(2,1)S(1)} %get-tuple-element.26.grid_ref, bf16[48,512]{1,0:T(8,128)(2,1)S(1)} %collective-permute-done.near_x_ref, bf16[48,512]{1,0:T(8,128)(2,1)S(1)} %collective-permute-done.1.far_x_ref, ...), custom_call_target="tpu_custom_call" | custom-call | flops 1000000000 | bytes 4000000 | tf_op jit(solution)/shard_map/near/pallas_call | solution.py:344
  68.9 6.9 %all-to-all-done.1.parts_ref = f32[16,1,128]{2,1,0:T(1,128)S(1)} async-done(((f32[16,1,128]{2,1,0:T(1,128)}), f32[16,1,128]{2,1,0:T(1,128)S(1)}, u32[]{:S(2)}, u32[]{:S(2)}) %all-to-all-start.1) | async-done | bytes 8224 | tf_op jit(solution)/shard_map/all_to_all | solution.py:342
  75.8 0.8 %final.1 = (f32[3,64,128]{2,1,0:T(8,128)}, f32[6,64,128]{2,1,0:T(8,128)}) custom-call(f32[16,1,128]{2,1,0:T(1,128)S(1)} %all-to-all-done.1.parts_ref, s32[64,128]{1,0:T(8,128)S(1)} %get-tuple-element.24.corner_ref, f32[3,64,128]{2,1,0:T(8,128)S(1)} %get-tuple-element.36.near_ref, f32[3,64,128]{2,1,0:T(8,128)S(1)} %get-tuple-element.37.unit_ref, ...), custom_call_target="tpu_custom_call" | custom-call | flops 500000 | bytes 600000 | tf_op jit(solution)/shard_map/final/pallas_call | solution.py:358
Async XLA Ops:
  5.5 37.1 %collective-permute-start = (bf16[48,512]{1,0:T(8,128)(2,1)S(1)}, bf16[48,512]{1,0:T(8,128)(2,1)S(1)}, u32[]{:S(2)}, u32[]{:S(2)}) collective-permute-start(bf16[48,512]{1,0:T(8,128)(2,1)S(1)} %get-tuple-element.27), channel_id=1, source_target_pairs={{0,128},{128,0},{256,384},{384,256},{1,129},{129,1},{257,385},{385... | collective-permute-start | bytes 147464 | tf_op jit(solution)/shard_map/ppermute | solution.py:289
  14.3 39.3 %all-to-all-start = ((f32[32,1,128]{2,1,0:T(1,128)}), f32[32,1,128]{2,1,0:T(1,128)S(1)}, u32[]{:S(2)}, u32[]{:S(2)}) async-start(f32[32,1,128]{2,1,0:T(1,128)} %get-tuple-element.22), calls=%async_computation | async-start | bytes 32768 | tf_op jit(solution)/shard_map/all_to_all | solution.py:320
  24.2 37.5 %collective-permute-start.1 = (bf16[48,512]{1,0:T(8,128)(2,1)S(1)}, bf16[48,512]{1,0:T(8,128)(2,1)S(1)}, u32[]{:S(2)}, u32[]{:S(2)}) collective-permute-start(bf16[48,512]{1,0:T(8,128)(2,1)S(1)} %get-tuple-element.28), channel_id=1, source_target_pairs={{0,384},{128,256},{256,128},{384,0},{1,385},{129,257},{257,129},{3... | collective-permute-start | bytes 147464 | tf_op jit(solution)/shard_map/ppermute | solution.py:289
  32.3 29.4 %collective-permute-start.2 = (bf16[48,512]{1,0:T(8,128)(2,1)S(1)}, bf16[48,512]{1,0:T(8,128)(2,1)S(1)}, u32[]{:S(2)}, u32[]{:S(2)}) collective-permute-start(bf16[48,512]{1,0:T(8,128)(2,1)S(1)} %get-tuple-element.29), channel_id=1, source_target_pairs={{0,32},{32,0},{64,96},{96,64},{1,33},{33,1},{65,97},{97,65},{2,34}... | collective-permute-start | bytes 147464 | tf_op jit(solution)/shard_map/ppermute | solution.py:289
  35.4 26.3 %collective-permute-start.3 = (bf16[48,512]{1,0:T(8,128)(2,1)S(1)}, bf16[48,512]{1,0:T(8,128)(2,1)S(1)}, u32[]{:S(2)}, u32[]{:S(2)}) collective-permute-start(bf16[48,512]{1,0:T(8,128)(2,1)S(1)} %get-tuple-element.30), channel_id=1, source_target_pairs={{0,96},{32,64},{64,32},{96,0},{1,97},{33,65},{65,33},{97,1},{2,98}... | collective-permute-start | bytes 147464 | tf_op jit(solution)/shard_map/ppermute | solution.py:289
  39.2 22.6 %collective-permute-start.4 = (bf16[48,512]{1,0:T(8,128)(2,1)S(1)}, bf16[48,512]{1,0:T(8,128)(2,1)S(1)}, u32[]{:S(2)}, u32[]{:S(2)}) collective-permute-start(bf16[48,512]{1,0:T(8,128)(2,1)S(1)} %get-tuple-element.31), channel_id=1, source_target_pairs={{0,1},{1,0},{2,3},{3,2},{4,5},{5,4},{6,7},{7,6},{8,9},{9,8},{10,11... | collective-permute-start | bytes 147464 | tf_op jit(solution)/shard_map/ppermute | solution.py:289
  42.6 19.1 %collective-permute-start.5 = (bf16[48,512]{1,0:T(8,128)(2,1)S(1)}, bf16[48,512]{1,0:T(8,128)(2,1)S(1)}, u32[]{:S(2)}, u32[]{:S(2)}) collective-permute-start(bf16[48,512]{1,0:T(8,128)(2,1)S(1)} %get-tuple-element.32), channel_id=1, source_target_pairs={{0,31},{1,2},{2,1},{3,4},{4,3},{5,6},{6,5},{7,8},{8,7},{9,10},{10,... | collective-permute-start | bytes 147464 | tf_op jit(solution)/shard_map/ppermute | solution.py:289
  54.3 21.5 %all-to-all-start.1 = ((f32[16,1,128]{2,1,0:T(1,128)}), f32[16,1,128]{2,1,0:T(1,128)S(1)}, u32[]{:S(2)}, u32[]{:S(2)}) async-start(f32[16,1,128]{2,1,0:T(1,128)} %coarse.1), calls=%async_computation.1 | async-start | bytes 16384 | tf_op jit(solution)/shard_map/all_to_all | solution.py:342

commit v4 on v3

--- a/solution.py
+++ b/solution.py
@@ -1,3 +1,4 @@
+import itertools
 import math
 
 import jax
@@ -14,7 +15,7 @@
 CUBES = TD**3
 FACE = 48
 GRID_ROWS = 256
-EXT_ROWS = 640
+EXT_ROWS = 768
 HALF = CS
 LANES = 128
 
@@ -58,7 +59,7 @@
 
 def spread_kernel(
     live_ref, pos_any, charge_any, tile_any, weights_any, blocks_any, top_any,
-    grid_ref, coarse_ref, coord_ref, tiles_ref, drive_ref, frac_ref, corner_ref, weights_ref, blocks_ref, top_ref,
+    grid_ref, coarse_ref, coord_ref, tiles_ref, frac_ref, drive_ref, corner_ref, weights_ref, blocks_ref, top_ref,
     pos_ref, charge_ref, tile_ref, wx_ref, wy_ref, wz_ref, cell_ref, sems,
 ):
     moves = [
@@ -70,10 +71,12 @@
             )
         )
     ]
-    for move in moves:
+    for move in moves[:4]:
         move.start()
     for move in moves[:3]:
         move.wait()
+    for move in moves[4:]:
+        move.start()
     cluster = 2 * iota((HALF, LANES), 0) + (iota((HALF, LANES), 1) >> 6)
     charge = charge_ref[...] * (cluster < live_ref[0, 0]).astype(jnp.float32)
     x, y = to_clusters(pos_ref[0], pos_ref[1])
@@ -147,20 +150,37 @@
     return lax.axis_index(axis) & 1
 
 
-def face_kernel(grid_ref, near_x_ref, far_x_ref, near_y_ref, far_y_ref, near_z_ref, far_z_ref):
+def face_kernel(grid_ref, pre_ref, keep_ref):
     row = iota((FACE, GRID_ROWS), 0)
     line = (row * 10923) >> 16
-    ids = []
-    for axis, (first, step) in zip(
-        ("gx", "gy", "gz"), ((row, 180), (line * 36 + (row - line * TD), 30), (row * TD, 5)), strict=True
-    ):
-        side = odd(axis)
-        ids += [first + step * (1 - side), first + step * side]
-    tile = jnp.where(jnp.concatenate([row] * 6, axis=0) < TD * TD, jnp.concatenate(ids, axis=0), -1)
-    hot = (iota((6 * FACE, GRID_ROWS), 1) == tile).astype(jnp.bfloat16)
+    core, side_y, side_z = odd("gx"), odd("gy"), odd("gz")
+    low_y, low_z = line * 36 + (row - line * TD), row * TD
+    near_x, far_x = row + 180 * (1 - core), row + 180 * core
+    own_y, own_z = core ^ side_y ^ 1, core ^ side_z ^ 1
+    ids = [
+        near_x, low_y + 30 * (1 - own_y), low_z + 5 * (1 - own_z), far_x,
+        low_y + 30 * own_y, low_z + 5 * own_z, far_x,
+    ]
+    tile = jnp.where(jnp.concatenate([row] * 7, axis=0) < TD * TD, jnp.concatenate(ids, axis=0), -1)
+    hot = (iota((7 * FACE, GRID_ROWS), 1) == tile).astype(jnp.bfloat16)
     faces = jnp.dot(hot, grid_ref[...], preferred_element_type=jnp.float32).astype(jnp.bfloat16)
-    for at, ref in enumerate((near_x_ref, far_x_ref, near_y_ref, far_y_ref, near_z_ref, far_z_ref)):
-        ref[...] = faces[at * FACE : (at + 1) * FACE]
+    for at in range(4):
+        pre_ref[at] = faces[at * FACE : (at + 1) * FACE]
+    for at in range(3):
+        keep_ref[at] = faces[(at + 4) * FACE : (at + 5) * FACE]
+
+
+def relay_kernel(keep_ref, got_ref, first_ref, second_ref, third_ref):
+    core = odd("gx")
+    first_ref[0], first_ref[1] = keep_ref[2 - core], got_ref[3 - core]
+    second_ref[0], second_ref[1] = keep_ref[0], got_ref[1]
+    third_ref[0], third_ref[1] = keep_ref[1], got_ref[2]
+
+
+def return_kernel(first_ref, second_ref, third_ref, post_ref):
+    post_ref[0] = first_ref[odd("gx")]
+    post_ref[1] = second_ref[1]
+    post_ref[2] = third_ref[1]
 
 
 def coarse_kernel(column_ref, top_ref, out_ref):
@@ -191,14 +211,16 @@
                 run = term if run is None else run + term
                 if k:
                     mean = run if mean is None else mean + run
-            part = wy[j] * run
-            cross = wy[j] * mean
+            weight = wy(j)
+            part = weight * run
+            cross = weight * mean
             a = part if a is None else a + part
             c = cross if c is None else c + cross
             if j:
                 b = a if b is None else b + a
+        weight = wx(i)
         for at, value in enumerate((a, b, c)):
-            term = wx[i] * value
+            term = weight * value
             sums[at] = term if sums[at] is None else sums[at] + term
         if i:
             sums[3] = sums[0] if sums[3] is None else sums[3] + sums[0]
@@ -207,24 +229,37 @@
 
 
 def near_kernel(
-    tiles_ref, grid_ref, near_x_ref, far_x_ref, near_y_ref, far_y_ref, near_z_ref, far_z_ref, blocks_ref, coord_ref, weights_ref,
+    tiles_ref, grid_ref, got_ref, first_ref, second_ref, third_ref, post_ref, blocks_ref, coord_any, weights_ref,
     near_ref, unit_ref,
-    ext_ref, field_ref, flat_ref, grad_ref,
+    ext_ref, field_ref, flat_ref, grad_ref, coord_ref, sem,
 ):
+    move = pltpu.make_async_copy(coord_any, coord_ref, sem)
+    move.start()
     ext_ref[0:GRID_ROWS] = grid_ref[...]
-    for at, ref in enumerate((near_x_ref, far_x_ref, near_y_ref, far_y_ref, near_z_ref, far_z_ref)):
-        ext_ref[GRID_ROWS + at * FACE : GRID_ROWS + (at + 1) * FACE] = ref[...]
-    ext_ref[GRID_ROWS + 6 * FACE :] = jnp.zeros((EXT_ROWS - GRID_ROWS - 6 * FACE, TP), jnp.bfloat16)
+    base = GRID_ROWS
+    for ref, count in ((got_ref, 1), (first_ref, 2), (second_ref, 2), (third_ref, 2), (post_ref, 3)):
+        for at in range(count):
+            ext_ref[base : base + FACE] = ref[at]
+            base += FACE
+    ext_ref[base:] = jnp.zeros((EXT_ROWS - base, TP), jnp.bfloat16)
+
+    core = odd("gx")
+
+    def at_row_of(on_core_0, on_core_1):
+        return GRID_ROWS + FACE * (on_core_0 + (on_core_1 - on_core_0) * core)
 
     tile = jnp.broadcast_to(tiles_ref[:1], (LANES, LANES)).T[:, :1].astype(jnp.int32)
     tx, ty, tz = tile_coords(tile)
-    edges = ((tx, 36, ty * TD + tz), (ty, TD, tx * TD + tz), (tz, 1, tx * TD + ty))
+    edges = (
+        ("gx", tx, 36, ty * TD + tz, at_row_of(0, 0), at_row_of(2, 7)),
+        ("gy", ty, TD, tx * TD + tz, at_row_of(3, 8), at_row_of(8, 3)),
+        ("gz", tz, 1, tx * TD + ty, at_row_of(5, 9), at_row_of(7, 1)),
+    )
     targets = [tile]
-    for at, (place, stride, row) in enumerate(edges):
-        base = GRID_ROWS + 2 * at * FACE + row
-        side = odd(("gx", "gy", "gz")[at])
-        targets.append(jnp.where(place < TD - 1, tile + stride, base + side * FACE))
-        targets.append(jnp.where(place > 0, tile - stride, base + (1 - side) * FACE))
+    for axis, place, stride, row, near, far in edges:
+        side = odd(axis)
+        targets.append(jnp.where(place < TD - 1, tile + stride, row + near + (far - near) * side))
+        targets.append(jnp.where(place > 0, tile - stride, row + far + (near - far) * side))
     at_row = iota((LANES, EXT_ROWS), 1)
     field = None
     for at, target in enumerate(targets):
@@ -241,13 +276,16 @@
             weights_ref[:, part * LANES : (part + 1) * LANES], (LANES, LANES)
         ).T
 
+    move.wait()
+
     @pl.loop(0, CS // ATOM_ROWS)
     def _(group):
         rows = pl.ds(pl.multiple_of(group * ATOM_ROWS, ATOM_ROWS), ATOM_ROWS)
         x, y, z = coord_ref[0, rows, :], coord_ref[1, rows, :], coord_ref[2, rows, :]
         wx, wy, wz = ([bump(u - node) for node in range(TL)] for u in (x, y, z))
         for which, ref in enumerate((field_ref, flat_ref)):
-            for axis, value in enumerate(gradients(ref, wx, wy, wz, x, y, z)):
+            sums = gradients(ref, wx.__getitem__, wy.__getitem__, wz, x, y, z)
+            for axis, value in enumerate(sums):
                 grad_ref[3 * which + axis, rows, :] = value
 
     near_ref[0], near_ref[1] = to_atoms(grad_ref[0], grad_ref[1])
@@ -284,9 +322,18 @@
     return jax.ShapeDtypeStruct(shape, jnp.bfloat16)
 
 
-def exchanged(value, axis, far):
-    count = lax.axis_size(axis)
-    return lax.ppermute(value, axis, [(i, (i + (1 if (i + far) % 2 == 0 else -1)) % count) for i in range(count)])
+def exchanged(value, partner):
+    wide, high, deep = (lax.axis_size(axis) for axis in ("gx", "gy", "gz"))
+    pairs = []
+    for x, y, z in itertools.product(range(wide), range(high), range(deep)):
+        to = partner(x, y, z)
+        if to is not None:
+            pairs.append(((x * high + y) * deep + z, ((to[0] % wide) * high + to[1] % high) * deep + to[2] % deep))
+    return lax.ppermute(value, ("gx", "gy", "gz"), pairs)
+
+
+def far(i):
+    return i + (1 if i % 2 else -1)
 
 
 def shards(positions, charges, cluster_tile, live_clusters, kernel_blocks, restrict_weights, top_kernel):
@@ -297,11 +344,11 @@
     weights = restrict_weights.reshape(1, TP)
     lines, bricks = lax.axis_size("gz"), lax.axis_size(("gx", "gy"))
 
-    grid, coarse, coords, tiles, drive, frac, corner, weights, blocks, top = pl.pallas_call(
+    grid, coarse, coords, tiles, frac, drive, corner, weights, blocks, top = pl.pallas_call(
         spread_kernel,
         out_shape=(
-            bf16(GRID_ROWS, TP), f32(lines, 1, LANES), f32(3, CS, LANES), f32(8, LANES), f32(HALF, LANES),
-            f32(3, HALF, LANES), jax.ShapeDtypeStruct((HALF, LANES), jnp.int32), f32(1, TP),
+            bf16(GRID_ROWS, TP), f32(lines, 1, LANES), f32(3, CS, LANES), f32(8, LANES),
+            f32(3, HALF, LANES), f32(HALF, LANES), jax.ShapeDtypeStruct((HALF, LANES), jnp.int32), f32(1, TP),
             bf16(*kernel_blocks.shape), f32(*top_kernel.shape),
         ),
         in_specs=[SMEM] + [ANY] * 6,
@@ -319,16 +366,38 @@
     )(live, *(pltpu.with_memory_space_constraint(a, pltpu.HBM) for a in (pos, charge, tile, weights, kernel_blocks, top_kernel)))
     column = lax.all_to_all(coarse, "gz", 0, 0, tiled=True)
 
-    faces = pl.pallas_call(
+    pre, keep = pl.pallas_call(
         face_kernel,
-        out_shape=(bf16(FACE, TP),) * 6,
+        out_shape=(bf16(4, FACE, TP), bf16(3, FACE, TP)),
         in_specs=[VMEM],
-        out_specs=[VMEM] * 6,
+        out_specs=[VMEM] * 2,
         compiler_params=pltpu.CompilerParams(vmem_limit_bytes=8 << 20),
         cost_estimate=pl.CostEstimate(flops=80_000_000, bytes_accessed=600_000, transcendentals=0),
         name="faces",
     )(grid)
-    faces = [exchanged(face, ("gx", "gy", "gz")[at // 2], at % 2) for at, face in enumerate(faces)]
+    got = exchanged(pre, lambda x, y, z: (x ^ 1, y, z))
+    first, second, third = pl.pallas_call(
+        relay_kernel,
+        out_shape=(bf16(2, FACE, TP),) * 3,
+        in_specs=[VMEM] * 2,
+        out_specs=[VMEM] * 3,
+        compiler_params=pltpu.CompilerParams(vmem_limit_bytes=4 << 20),
+        cost_estimate=pl.CostEstimate(flops=100_000, bytes_accessed=600_000, transcendentals=0),
+        name="relay",
+    )(keep, got)
+    first = exchanged(first, lambda x, y, z: (x, y, far(z)) if x % 2 else (x + 2, y, z))
+    second = exchanged(second, lambda x, y, z: (x, far(y), z) if x % 2 else (x, y ^ 1, z))
+    third = exchanged(third, lambda x, y, z: None if x % 2 else (x, y, z ^ 1))
+    post = pl.pallas_call(
+        return_kernel,
+        out_shape=bf16(3, FACE, TP),
+        in_specs=[VMEM] * 3,
+        out_specs=VMEM,
+        compiler_params=pltpu.CompilerParams(vmem_limit_bytes=4 << 20),
+        cost_estimate=pl.CostEstimate(flops=100_000, bytes_accessed=300_000, transcendentals=0),
+        name="back",
+    )(first, second, third)
+    post = exchanged(post, lambda x, y, z: (x ^ 1, y, z))
 
     parts = pl.pallas_call(
         coarse_kernel,
@@ -336,7 +405,7 @@
         in_specs=[VMEM] * 2,
         out_specs=VMEM,
         compiler_params=pltpu.CompilerParams(vmem_limit_bytes=8 << 20),
-        cost_estimate=pl.CostEstimate(flops=70_000, bytes_accessed=200_000, transcendentals=0),
+        cost_estimate=pl.CostEstimate(flops=3_000_000_000, bytes_accessed=200_000, transcendentals=0),
         name="coarse",
     )(column, top)
     parts = lax.all_to_all(parts, ("gx", "gy"), 0, 0, tiled=True)
@@ -344,16 +413,17 @@
     near, unit = pl.pallas_call(
         near_kernel,
         out_shape=(f32(3, HALF, LANES), f32(3, HALF, LANES)),
-        in_specs=[VMEM] * 11,
+        in_specs=[VMEM] * 8 + [ANY, VMEM],
         out_specs=[VMEM] * 2,
         scratch_shapes=[
             pltpu.VMEM((EXT_ROWS, TP), jnp.bfloat16), pltpu.VMEM((TP, LANES), jnp.float32),
             pltpu.VMEM((TP, LANES), jnp.float32), pltpu.VMEM((6, CS, LANES), jnp.float32),
+            pltpu.VMEM((3, CS, LANES), jnp.float32), pltpu.SemaphoreType.DMA,
         ],
         compiler_params=pltpu.CompilerParams(vmem_limit_bytes=16 << 20),
         cost_estimate=pl.CostEstimate(flops=1_000_000_000, bytes_accessed=4_000_000, transcendentals=200_000),
         name="near",
-    )(tiles, grid, *faces, blocks, coords, weights)
+    )(tiles, grid, got, first, second, third, post, blocks, pltpu.with_memory_space_constraint(coords, pltpu.HBM), weights)
 
     forces, virial = pl.pallas_call(
         final_kernel,

time: 77 us -> 77.1 us (level)
  starting transfers between devices: 55.4 us -> 50.6 us
  waiting for transfers between devices: 6.92 us -> 10.4 us
  Pallas kernels: 12.9 us -> 14.2 us
    all_to_all x1, starting transfers between devices: 7.35 us -> 14.8 us  [shards(): parts = lax.all_to_all(parts, ('gx', 'gy'), 0, 0, tiled=True)]
    ppermute x6 -> x5, starting transfers between devices: 38.2 us -> 32 us  [exchanged(): return lax.ppermute(value, ('gx', 'gy', 'gz'), pairs)]
    all_to_all x1, starting transfers between devices: 9.9 us -> 3.82 us  [shards(): column = lax.all_to_all(coarse, 'gz', 0, 0, tiled=True)]
    all_to_all x1, waiting for transfers between devices: 0.01 us -> 3.1 us  [shards(): column = lax.all_to_all(coarse, 'gz', 0, 0, tiled=True)]
    ppermute x6 -> x5, waiting for transfers between devices: 0.02 us -> 1.06 us  [exchanged(): return lax.ppermute(value, ('gx', 'gy', 'gz'), pairs)]
  transfers between devices with their start and end apart: 8 -> 7, of which waited for: 1 -> 3; matrix products, arithmetic and copies ran while one was open for 0% -> 0% of each run, Pallas kernels for 10% -> 11%
where the time goes in v4:
time: 77.1 us; the launch traced here: 76.7 us
  starting transfers between devices  50.6 us (66%)
  Pallas kernels  14.2 us (18%)
  waiting for transfers between devices  10.4 us (13%)
  between operations  1.4 us (2%)
    ppermute x5, starting transfers between devices, exchanged(): return lax.ppermute(value, ('gx', 'gy', 'gz'), pairs)  32 us
    all_to_all x1, starting transfers between devices, shards(): parts = lax.all_to_all(parts, ('gx', 'gy'), 0, 0, tiled=True)  14.8 us
    pallas_call x1, Pallas kernels, shards(): pl.pallas_call(near_kernel, out_shape=(f32(3, HALF, LANES), f32(3, HALF,...  7.85 us
    all_to_all x1, waiting for transfers between devices, shards(): parts = lax.all_to_all(parts, ('gx', 'gy'), 0, 0, tiled=True)  6.24 us
    pallas_call x1, Pallas kernels, shards(): pl.pallas_call(spread_kernel, out_shape=(bf16(GRID_ROWS, TP), f32(lines,...  3.93 us
    all_to_all x1, starting transfers between devices, shards(): column = lax.all_to_all(coarse, 'gz', 0, 0, tiled=True)  3.82 us
    all_to_all x1, waiting for transfers between devices, shards(): column = lax.all_to_all(coarse, 'gz', 0, 0, tiled=True)  3.1 us
  transfers between devices with their start and end apart: 7, of which 3 were waited for; matrix products, arithmetic and copies ran while one was open for 0% of the time, Pallas kernels for 11%

profile of v4, /device:TPU:1, one launch (start us, length us, event | category | flops | bytes accessed | tf_op | source)
XLA Modules:
  0.0 76.7 jit_solution(5982994942328689948)
XLA Ops:
  1.3 3.9 %spread.1 = (bf16[256,512]{1,0:T(8,128)(2,1)S(1)}, f32[32,1,128]{2,1,0:T(1,128)}, f32[3,64,128]{2,1,0:T(8,128)S(1)}, f32[8,128]{1,0:T(8,128)S(1)}, f32[3,64,128]...) custom-call(s32[1,1]{1,0:T(1,128)} %bitcast.7.live_ref, ...), custom_call_target="tpu_custom_call" | custom-call | flops 10000000 | bytes 1000000 | tf_op jit(solution)/shard_map/spread/pallas_call | solution.py:347
  5.2 0.0 copy-start
  5.2 0.2 faces.1
  5.5 8.8 %collective-permute-start = (bf16[4,48,512]{2,1,0:T(8,128)(2,1)S(1)}, bf16[4,48,512]{2,1,0:T(8,128)(2,1)S(1)}, u32[]{:S(2)}, u32[]{:S(2)}) collective-permute-start(bf16[4,48,512]{2,1,0:T(8,128)(2,1)S(1)} %get-tuple-element.26), channel_id=1, source_target_pairs={{0,128},{1,129},{2,130},{3,131},{4,132},{5,133},{6,134},{7,135},{8... | collective-permute-start | bytes 589832 | tf_op jit(solution)/shard_map/ppermute | solution.py:332
  14.3 1.0 %collective-permute-done.got_ref = bf16[4,48,512]{2,1,0:T(8,128)(2,1)S(1)} collective-permute-done((bf16[4,48,512]{2,1,0:T(8,128)(2,1)S(1)}, bf16[4,48,512]{2,1,0:T(8,128)(2,1)S(1)}, u32[]{:S(2)}, u32[]{:S(2)}) %collective-permute-start) | collective-permute-done | bytes 196640 | tf_op jit(solution)/shard_map/ppermute | solution.py:332
  15.3 0.7 relay.1
  16.0 9.9 %collective-permute-start.1 = (bf16[2,48,512]{2,1,0:T(8,128)(2,1)}, bf16[2,48,512]{2,1,0:T(8,128)(2,1)S(1)}, u32[]{:S(2)}, u32[]{:S(2)}) collective-permute-start(bf16[2,48,512]{2,1,0:T(8,128)(2,1)} %get-tuple-element.28), channel_id=1, source_target_pairs={{0,256},{1,257},{2,258},{3,259},{4,260},{5,261},{6,262},{7,263},{8... | collective-permute-start | bytes 294920 | tf_op jit(solution)/shard_map/ppermute | solution.py:332
  25.9 4.4 %collective-permute-start.2 = (bf16[2,48,512]{2,1,0:T(8,128)(2,1)S(1)}, bf16[2,48,512]{2,1,0:T(8,128)(2,1)S(1)}, u32[]{:S(2)}, u32[]{:S(2)}) collective-permute-start(bf16[2,48,512]{2,1,0:T(8,128)(2,1)S(1)} %get-tuple-element.29), channel_id=1, source_target_pairs={{0,32},{1,33},{2,34},{3,35},{4,36},{5,37},{6,38},{7,39},{8,40},{9,... | collective-permute-start | bytes 294920 | tf_op jit(solution)/shard_map/ppermute | solution.py:332
  30.3 0.0 copy-done
  30.3 0.7 collective-permute-start.3
  31.0 3.8 %all-to-all-start = ((f32[32,1,128]{2,1,0:T(1,128)}), f32[32,1,128]{2,1,0:T(1,128)S(1)}, u32[]{:S(2)}, u32[]{:S(2)}) async-start(f32[32,1,128]{2,1,0:T(1,128)} %get-tuple-element.21), calls=%async_computation | async-start | bytes 32768 | tf_op jit(solution)/shard_map/all_to_all | solution.py:367
  34.9 0.0 collective-permute-done.1.first_ref
  34.9 0.0 collective-permute-done.2.second_ref
  34.9 0.0 collective-permute-done.3.third_ref
  34.9 8.2 %collective-permute-start.4 = (bf16[3,48,512]{2,1,0:T(8,128)(2,1)S(1)}, bf16[3,48,512]{2,1,0:T(8,128)(2,1)S(1)}, u32[]{:S(2)}, u32[]{:S(2)}) collective-permute-start(bf16[3,48,512]{2,1,0:T(8,128)(2,1)S(1)} %back.1), channel_id=1, source_target_pairs={{0,128},{1,129},{2,130},{3,131},{4,132},{5,133},{6,134},{7,135},{8... | collective-permute-start | bytes 442376 | tf_op jit(solution)/shard_map/ppermute | solution.py:332
  43.1 3.1 %all-to-all-done.column_ref = f32[32,1,128]{2,1,0:T(1,128)S(1)} async-done(((f32[32,1,128]{2,1,0:T(1,128)}), f32[32,1,128]{2,1,0:T(1,128)S(1)}, u32[]{:S(2)}, u32[]{:S(2)}) %all-to-all-start) | async-done | bytes 16416 | tf_op jit(solution)/shard_map/all_to_all | solution.py:367
  46.2 0.7 coarse.1
  46.9 14.8 %all-to-all-start.1 = ((f32[16,1,128]{2,1,0:T(1,128)}), f32[16,1,128]{2,1,0:T(1,128)S(1)}, u32[]{:S(2)}, u32[]{:S(2)}) async-start(f32[16,1,128]{2,1,0:T(1,128)} %coarse.1), calls=%async_computation.1 | async-start | bytes 16384 | tf_op jit(solution)/shard_map/all_to_all | solution.py:411
  61.8 0.0 collective-permute-done.4.post_ref
  61.8 7.9 %near.1 = (f32[3,64,128]{2,1,0:T(8,128)S(1)}, f32[3,64,128]{2,1,0:T(8,128)S(1)}) custom-call(f32[8,128]{1,0:T(8,128)S(1)} %get-tuple-element.24.tiles_ref, bf16[256,512]{1,0:T(8,128)(2,1)S(1)} %get-tuple-element.25.grid_ref, bf16[4,48,512]{2,1,0:T(8,128)(2,1)S(1)} %collective-permute-done.got_ref, bf16[2,48,512]{2,1,0:T(8,128)(2,1)S(1)} %collective-permute-done.1.first_ref, ...), custom_call_target="tpu_custom_call" | custom-call | flops 1000000000 | bytes 4000000 | tf_op jit(solution)/shard_map/near/pallas_call | solution.py:413
  69.6 6.2 %all-to-all-done.1.parts_ref = f32[16,1,128]{2,1,0:T(1,128)S(1)} async-done(((f32[16,1,128]{2,1,0:T(1,128)}), f32[16,1,128]{2,1,0:T(1,128)S(1)}, u32[]{:S(2)}, u32[]{:S(2)}) %all-to-all-start.1) | async-done | bytes 8224 | tf_op jit(solution)/shard_map/all_to_all | solution.py:411
  75.9 0.8 %final.1 = (f32[3,64,128]{2,1,0:T(8,128)}, f32[6,64,128]{2,1,0:T(8,128)}) custom-call(f32[16,1,128]{2,1,0:T(1,128)S(1)} %all-to-all-done.1.parts_ref, s32[64,128]{1,0:T(8,128)S(1)} %get-tuple-element.23.corner_ref, f32[3,64,128]{2,1,0:T(8,128)S(1)} %get-tuple-element.34.near_ref, f32[3,64,128]{2,1,0:T(8,128)S(1)} %get-tuple-element.35.unit_ref, ...), custom_call_target="tpu_custom_call" | custom-call | flops 500000 | bytes 600000 | tf_op jit(solution)/shard_map/final/pallas_call | solution.py:428
  (1 shorter events, 0.0 us)
Async XLA Ops:
  5.2 25.1 %copy-start = (f32[3,64,128]{2,1,0:T(8,128)}, f32[3,64,128]{2,1,0:T(8,128)S(1)}, u32[]{:S(2)}) copy-start(f32[3,64,128]{2,1,0:T(8,128)S(1)} %get-tuple-element.32.coord_any) | copy-start | bytes 294916
  5.5 9.9 %collective-permute-start = (bf16[4,48,512]{2,1,0:T(8,128)(2,1)S(1)}, bf16[4,48,512]{2,1,0:T(8,128)(2,1)S(1)}, u32[]{:S(2)}, u32[]{:S(2)}) collective-permute-start(bf16[4,48,512]{2,1,0:T(8,128)(2,1)S(1)} %get-tuple-element.26), channel_id=1, source_target_pairs={{0,128},{1,129},{2,130},{3,131},{4,132},{5,133},{6,134},{7,135},{8... | collective-permute-start | bytes 589832 | tf_op jit(solution)/shard_map/ppermute | solution.py:332
  16.0 18.9 %collective-permute-start.1 = (bf16[2,48,512]{2,1,0:T(8,128)(2,1)}, bf16[2,48,512]{2,1,0:T(8,128)(2,1)S(1)}, u32[]{:S(2)}, u32[]{:S(2)}) collective-permute-start(bf16[2,48,512]{2,1,0:T(8,128)(2,1)} %get-tuple-element.28), channel_id=1, source_target_pairs={{0,256},{1,257},{2,258},{3,259},{4,260},{5,261},{6,262},{7,263},{8... | collective-permute-start | bytes 294920 | tf_op jit(solution)/shard_map/ppermute | solution.py:332
  25.9 8.9 %collective-permute-start.2 = (bf16[2,48,512]{2,1,0:T(8,128)(2,1)S(1)}, bf16[2,48,512]{2,1,0:T(8,128)(2,1)S(1)}, u32[]{:S(2)}, u32[]{:S(2)}) collective-permute-start(bf16[2,48,512]{2,1,0:T(8,128)(2,1)S(1)} %get-tuple-element.29), channel_id=1, source_target_pairs={{0,32},{1,33},{2,34},{3,35},{4,36},{5,37},{6,38},{7,39},{8,40},{9,... | collective-permute-start | bytes 294920 | tf_op jit(solution)/shard_map/ppermute | solution.py:332
  30.3 4.5 %collective-permute-start.3 = (bf16[2,48,512]{2,1,0:T(8,128)(2,1)S(1)}, bf16[2,48,512]{2,1,0:T(8,128)(2,1)S(1)}, u32[]{:S(2)}, u32[]{:S(2)}) collective-permute-start(bf16[2,48,512]{2,1,0:T(8,128)(2,1)S(1)} %get-tuple-element.30), channel_id=1, source_target_pairs={{0,1},{1,0},{2,3},{3,2},{4,5},{5,4},{6,7},{7,6},{8,9},{9,8},{10,11... | collective-permute-start | bytes 294920 | tf_op jit(solution)/shard_map/ppermute | solution.py:332
  31.0 15.2 %all-to-all-start = ((f32[32,1,128]{2,1,0:T(1,128)}), f32[32,1,128]{2,1,0:T(1,128)S(1)}, u32[]{:S(2)}, u32[]{:S(2)}) async-start(f32[32,1,128]{2,1,0:T(1,128)} %get-tuple-element.21), calls=%async_computation | async-start | bytes 32768 | tf_op jit(solution)/shard_map/all_to_all | solution.py:367
  34.9 26.9 %collective-permute-start.4 = (bf16[3,48,512]{2,1,0:T(8,128)(2,1)S(1)}, bf16[3,48,512]{2,1,0:T(8,128)(2,1)S(1)}, u32[]{:S(2)}, u32[]{:S(2)}) collective-permute-start(bf16[3,48,512]{2,1,0:T(8,128)(2,1)S(1)} %back.1), channel_id=1, source_target_pairs={{0,128},{1,129},{2,130},{3,131},{4,132},{5,133},{6,134},{7,135},{8... | collective-permute-start | bytes 442376 | tf_op jit(solution)/shard_map/ppermute | solution.py:332
  46.9 29.0 %all-to-all-start.1 = ((f32[16,1,128]{2,1,0:T(1,128)}), f32[16,1,128]{2,1,0:T(1,128)S(1)}, u32[]{:S(2)}, u32[]{:S(2)}) async-start(f32[16,1,128]{2,1,0:T(1,128)} %coarse.1), calls=%async_computation.1 | async-start | bytes 16384 | tf_op jit(solution)/shard_map/all_to_all | solution.py:411

commit v5 on v3

--- a/solution.py
+++ b/solution.py
@@ -144,7 +144,7 @@
 
 
 def odd(axis):
-    return lax.axis_index(axis) & 1
+    return lax.axis_index("cx" if axis == "gx" else axis) & 1
 
 
 def face_kernel(grid_ref, near_x_ref, far_x_ref, near_y_ref, far_y_ref, near_z_ref, far_z_ref):
@@ -163,7 +163,7 @@
         ref[...] = faces[at * FACE : (at + 1) * FACE]
 
 
-def coarse_kernel(column_ref, top_ref, out_ref):
+def coarse_kernel(column_ref, top_ref, face_ref, own_ref, send_ref):
     lines = column_ref.shape[0]
     column = column_ref[...].reshape(lines, LANES)
     column = jnp.concatenate([column] * (lines * 8 // LANES), axis=1)
@@ -173,8 +173,23 @@
     rows = partial_value.shape[0]
     lanes = jnp.where((iota((rows, LANES), 1) & 7) == (iota((rows, LANES), 0) & 7), partial_value, 0.0)
     lanes = jnp.sum(lanes.reshape(rows // 8, 8, LANES), axis=1)
-    for brick in range(rows // 8):
-        out_ref[brick] = lanes[brick : brick + 1]
+    half = jnp.broadcast_to(lax.axis_index("hx"), (8, LANES)) == 0
+    own_ref[...] = jnp.where(half, lanes[:8], lanes[8:])
+    rest = jnp.where(half, lanes[8:], lanes[:8])
+    parts = []
+    for _ in range(3):
+        parts.append(rest.astype(jnp.bfloat16).astype(jnp.float32))
+        rest = rest - parts[-1]
+    tail = jnp.concatenate(parts + [jnp.zeros((8, LANES), jnp.float32)], axis=1)
+    send_ref[:32] = face_ref[:32]
+    send_ref[32:] = jnp.concatenate([face_ref[32:].astype(jnp.float32)[:8], tail], axis=0).astype(jnp.bfloat16)
+
+
+def merge_kernel(own_ref, far_ref, field_any, out_ref):
+    tail = far_ref[32:].astype(jnp.float32)[8:]
+    total = own_ref[...] + ((tail[:, :LANES] + tail[:, LANES : 2 * LANES]) + tail[:, 2 * LANES : 3 * LANES])
+    for brick in range(8):
+        out_ref[brick] = total[brick : brick + 1]
 
 
 ATOM_ROWS = 16
@@ -206,25 +221,35 @@
     return with_x - x * total, with_y - y * total, with_z - z * total
 
 
+def tile_column(tiles_ref):
+    return jnp.broadcast_to(tiles_ref[:1], (LANES, LANES)).T[:, :1].astype(jnp.int32)
+
+
 def near_kernel(
-    tiles_ref, grid_ref, near_x_ref, far_x_ref, near_y_ref, far_y_ref, near_z_ref, far_z_ref, blocks_ref, coord_ref, weights_ref,
-    near_ref, unit_ref,
-    ext_ref, field_ref, flat_ref, grad_ref,
+    tiles_ref, grid_ref, near_x_ref, near_y_ref, far_y_ref, near_z_ref, far_z_ref, blocks_ref, coord_ref, weights_ref,
+    field_ref, unit_ref,
+    ext_ref, flat_ref, grad_ref,
 ):
     ext_ref[0:GRID_ROWS] = grid_ref[...]
-    for at, ref in enumerate((near_x_ref, far_x_ref, near_y_ref, far_y_ref, near_z_ref, far_z_ref)):
+    for at, ref in enumerate((near_x_ref, near_y_ref, far_y_ref, near_z_ref, far_z_ref)):
         ext_ref[GRID_ROWS + at * FACE : GRID_ROWS + (at + 1) * FACE] = ref[...]
-    ext_ref[GRID_ROWS + 6 * FACE :] = jnp.zeros((EXT_ROWS - GRID_ROWS - 6 * FACE, TP), jnp.bfloat16)
-
-    tile = jnp.broadcast_to(tiles_ref[:1], (LANES, LANES)).T[:, :1].astype(jnp.int32)
+    nothing = GRID_ROWS + 5 * FACE
+    ext_ref[nothing:] = jnp.zeros((EXT_ROWS - nothing, TP), jnp.bfloat16)
+
+    tile = tile_column(tiles_ref)
     tx, ty, tz = tile_coords(tile)
-    edges = ((tx, 36, ty * TD + tz), (ty, TD, tx * TD + tz), (tz, 1, tx * TD + ty))
+    row_x, row_y, row_z = ty * TD + tz, tx * TD + tz, tx * TD + ty
+    base = GRID_ROWS
+    edges = (
+        ("gx", tx, 36, base + row_x, nothing + 0 * row_x),
+        ("gy", ty, TD, base + FACE + row_y, base + 2 * FACE + row_y),
+        ("gz", tz, 1, base + 3 * FACE + row_z, base + 4 * FACE + row_z),
+    )
     targets = [tile]
-    for at, (place, stride, row) in enumerate(edges):
-        base = GRID_ROWS + 2 * at * FACE + row
-        side = odd(("gx", "gy", "gz")[at])
-        targets.append(jnp.where(place < TD - 1, tile + stride, base + side * FACE))
-        targets.append(jnp.where(place > 0, tile - stride, base + (1 - side) * FACE))
+    for axis, place, stride, near, far in edges:
+        side = jnp.broadcast_to(odd(axis), near.shape) == 1
+        targets.append(jnp.where(place < TD - 1, tile + stride, jnp.where(side, far, near)))
+        targets.append(jnp.where(place > 0, tile - stride, jnp.where(side, near, far)))
     at_row = iota((LANES, EXT_ROWS), 1)
     field = None
     for at, target in enumerate(targets):
@@ -235,24 +260,49 @@
             rows, blocks_ref[(at + 1) // 2], (((1,), (0 if flipped else 1,)), ((), ())), preferred_element_type=jnp.float32
         )
         field = term if field is None else field + term
+    field_ref[...] = field
     for part in range(TP // LANES):
-        field_ref[part * LANES : (part + 1) * LANES, :] = field[:, part * LANES : (part + 1) * LANES].T
         flat_ref[part * LANES : (part + 1) * LANES, :] = jnp.broadcast_to(
             weights_ref[:, part * LANES : (part + 1) * LANES], (LANES, LANES)
         ).T
-
+    all_gradients(flat_ref, coord_ref, grad_ref)
+    unit_ref[0], unit_ref[1] = to_atoms(grad_ref[0], grad_ref[1])
+    unit_ref[2], _ = to_atoms(grad_ref[2], grad_ref[2])
+
+
+def all_gradients(field_ref, coord_ref, grad_ref):
     @pl.loop(0, CS // ATOM_ROWS)
     def _(group):
         rows = pl.ds(pl.multiple_of(group * ATOM_ROWS, ATOM_ROWS), ATOM_ROWS)
         x, y, z = coord_ref[0, rows, :], coord_ref[1, rows, :], coord_ref[2, rows, :]
         wx, wy, wz = ([bump(u - node) for node in range(TL)] for u in (x, y, z))
-        for which, ref in enumerate((field_ref, flat_ref)):
-            for axis, value in enumerate(gradients(ref, wx, wy, wz, x, y, z)):
-                grad_ref[3 * which + axis, rows, :] = value
-
+        for axis, value in enumerate(gradients(field_ref, wx, wy, wz, x, y, z)):
+            grad_ref[axis, rows, :] = value
+
+
+def far_kernel(
+    tiles_ref, part_ref, far_x_ref, block_ref, coord_ref,
+    near_ref,
+    sum_ref, field_ref, grad_ref,
+):
+    tx, ty, tz = tile_coords(tile_column(tiles_ref))
+    core = odd("gx")
+    target = jnp.where(tx == (TD - 1) * core, ty * TD + tz, -1)
+    hot = (iota((LANES, FACE), 1) == target).astype(jnp.bfloat16)
+    rows = jnp.dot(hot, far_x_ref[...], preferred_element_type=jnp.float32).astype(jnp.bfloat16)
+    for side in range(2):
+
+        @pl.when(core == side)
+        def _(side=side):
+            sum_ref[...] = part_ref[...] + lax.dot_general(
+                rows, block_ref[1], (((1,), (side,)), ((), ())), preferred_element_type=jnp.float32
+            )
+
+    for part in range(TP // LANES):
+        field_ref[part * LANES : (part + 1) * LANES, :] = sum_ref[:, part * LANES : (part + 1) * LANES].T
+    all_gradients(field_ref, coord_ref, grad_ref)
     near_ref[0], near_ref[1] = to_atoms(grad_ref[0], grad_ref[1])
-    near_ref[2], unit_ref[0] = to_atoms(grad_ref[2], grad_ref[3])
-    unit_ref[1], unit_ref[2] = to_atoms(grad_ref[4], grad_ref[5])
+    near_ref[2], _ = to_atoms(grad_ref[2], grad_ref[2])
 
 
 def final_kernel(parts_ref, corner_ref, near_ref, unit_ref, frac_ref, drive_ref, force_ref, virial_ref):
@@ -273,7 +323,7 @@
 
 VMEM = pl.BlockSpec(memory_space=pltpu.VMEM)
 SMEM = pl.BlockSpec(memory_space=pltpu.SMEM)
-ANY = pl.BlockSpec(memory_space=pltpu.HBM)
+ANY = pl.BlockSpec(memory_space=pl.ANY)
 
 
 def f32(*shape):
@@ -295,7 +345,7 @@
     tile = cluster_tile.reshape(1, LANES)
     live = live_clusters.reshape(1, 1)
     weights = restrict_weights.reshape(1, TP)
-    lines, bricks = lax.axis_size("gz"), lax.axis_size(("gx", "gy"))
+    lines = lax.axis_size("gz")
 
     grid, coarse, coords, tiles, drive, frac, corner, weights, blocks, top = pl.pallas_call(
         spread_kernel,
@@ -328,32 +378,60 @@
         cost_estimate=pl.CostEstimate(flops=80_000_000, bytes_accessed=600_000, transcendentals=0),
         name="faces",
     )(grid)
-    faces = [exchanged(face, ("gx", "gy", "gz")[at // 2], at % 2) for at, face in enumerate(faces)]
-
-    parts = pl.pallas_call(
+    near_x, far_x, near_y, far_y, near_z, far_z = faces
+    near_x = exchanged(near_x, ("hx", "cx"), 0)
+    near_y, far_y = exchanged(near_y, "gy", 0), exchanged(far_y, "gy", 1)
+    near_z, far_z = exchanged(near_z, "gz", 0), exchanged(far_z, "gz", 1)
+
+    own, far_x = pl.pallas_call(
         coarse_kernel,
-        out_shape=f32(bricks, 1, LANES),
-        in_specs=[VMEM] * 2,
-        out_specs=VMEM,
+        out_shape=(f32(8, LANES), bf16(FACE, TP)),
+        in_specs=[VMEM] * 3,
+        out_specs=[VMEM] * 2,
         compiler_params=pltpu.CompilerParams(vmem_limit_bytes=8 << 20),
         cost_estimate=pl.CostEstimate(flops=70_000, bytes_accessed=200_000, transcendentals=0),
         name="coarse",
-    )(column, top)
-    parts = lax.all_to_all(parts, ("gx", "gy"), 0, 0, tiled=True)
-
-    near, unit = pl.pallas_call(
+    )(column, top, far_x)
+    far_x = exchanged(far_x, ("hx", "cx"), 1)
+
+    field, unit = pl.pallas_call(
         near_kernel,
-        out_shape=(f32(3, HALF, LANES), f32(3, HALF, LANES)),
-        in_specs=[VMEM] * 11,
+        out_shape=(f32(LANES, TP), f32(3, HALF, LANES)),
+        in_specs=[VMEM] * 10,
         out_specs=[VMEM] * 2,
         scratch_shapes=[
             pltpu.VMEM((EXT_ROWS, TP), jnp.bfloat16), pltpu.VMEM((TP, LANES), jnp.float32),
-            pltpu.VMEM((TP, LANES), jnp.float32), pltpu.VMEM((6, CS, LANES), jnp.float32),
+            pltpu.VMEM((3, CS, LANES), jnp.float32),
         ],
         compiler_params=pltpu.CompilerParams(vmem_limit_bytes=16 << 20),
         cost_estimate=pl.CostEstimate(flops=1_000_000_000, bytes_accessed=4_000_000, transcendentals=200_000),
         name="near",
-    )(tiles, grid, *faces, blocks, coords, weights)
+    )(tiles, grid, near_x, near_y, far_y, near_z, far_z, blocks, coords, weights)
+
+    parts = pl.pallas_call(
+        merge_kernel,
+        out_shape=f32(8, 1, LANES),
+        in_specs=[VMEM] * 2 + [ANY],
+        out_specs=VMEM,
+        compiler_params=pltpu.CompilerParams(vmem_limit_bytes=4 << 20),
+        cost_estimate=pl.CostEstimate(flops=10_000, bytes_accessed=60_000, transcendentals=0),
+        name="merge",
+    )(own, far_x, field)
+    parts = lax.all_to_all(parts, ("cx", "gy"), 0, 0, tiled=True)
+
+    near = pl.pallas_call(
+        far_kernel,
+        out_shape=f32(3, HALF, LANES),
+        in_specs=[VMEM] * 5,
+        out_specs=VMEM,
+        scratch_shapes=[
+            pltpu.VMEM((LANES, TP), jnp.float32), pltpu.VMEM((TP, LANES), jnp.float32),
+            pltpu.VMEM((3, CS, LANES), jnp.float32),
+        ],
+        compiler_params=pltpu.CompilerParams(vmem_limit_bytes=16 << 20),
+        cost_estimate=pl.CostEstimate(flops=1_000_000_000, bytes_accessed=4_000_000, transcendentals=200_000),
+        name="far",
+    )(tiles, field, far_x, blocks, coords)
 
     forces, virial = pl.pallas_call(
         final_kernel,
@@ -368,19 +446,22 @@
 
 
 def solution(mesh):
+    wide, high, deep = (mesh.shape[axis] for axis in ("gx", "gy", "gz"))
+    split = jax.sharding.Mesh(mesh.devices.reshape(wide // 2, 2, high, deep), ("hx", "cx", "gy", "gz"))
+    x = ("hx", "cx")
     placed = (
-        P(None, "gx", "gy", "gz", None),
-        P("gx", "gy", "gz", None),
-        P("gx", "gy", "gz", None),
-        P("gx", "gy", "gz"),
+        P(None, x, "gy", "gz", None),
+        P(x, "gy", "gz", None),
+        P(x, "gy", "gz", None),
+        P(x, "gy", "gz"),
         P(),
         P(),
-        P("gz", ("gx", "gy")),
+        P("gz", ("hx", "cx", "gy")),
     )
     return jax.shard_map(
         shards,
-        mesh=mesh,
+        mesh=split,
         in_specs=placed,
-        out_specs=(P(None, "gx", "gy", "gz", None), P(None, "gx", "gy", "gz", None)),
+        out_specs=(P(None, x, "gy", "gz", None), P(None, x, "gy", "gz", None)),
         check_vma=False,
     )

time: 77 us -> 71.6 us (0.930)
  waiting for transfers between devices: 6.92 us -> 3.27 us
  starting transfers between devices: 55.4 us -> 52.9 us
  Pallas kernels: 12.9 us -> 13.7 us
    all_to_all x1, starting transfers between devices: 9.9 us -> 16.1 us  [shards(): column = lax.all_to_all(coarse, 'gz', 0, 0, tiled=True)]
    all_to_all x1, waiting for transfers between devices: 6.9 us -> 1.32 us  [shards(): parts = lax.all_to_all(parts, ('cx', 'gy'), 0, 0, tiled=True)]
    ppermute x6, starting transfers between devices: 38.2 us -> 33.1 us  [exchanged(): lax.ppermute(value, axis, [(i, (i + (1 if (i + far) % 2 == 0 else -1)) %...]
    all_to_all x1, starting transfers between devices: 7.35 us -> 3.67 us  [shards(): parts = lax.all_to_all(parts, ('cx', 'gy'), 0, 0, tiled=True)]
    ppermute x6, waiting for transfers between devices: 0.02 us -> 1.94 us  [exchanged(): lax.ppermute(value, axis, [(i, (i + (1 if (i + far) % 2 == 0 else -1)) %...]
    pallas_call x2 -> x4, Pallas kernels: 7.88 us -> 8.73 us  [the longest x1 4.85 us: shards(): pl.pallas_call(near_kernel, out_shape=(f32(LANES, TP), f32(3, HALF, LANES...]
  transfers between devices with their start and end apart: 8 -> 8, of which waited for: 1 -> 2; matrix products, arithmetic and copies ran while one was open for 0% -> 0% of each run, Pallas kernels for 10% -> 12%
where the time goes in v5:
time: 71.6 us; the launch traced here: 71.3 us
  starting transfers between devices  52.9 us (74%)
  Pallas kernels  13.7 us (19%)
  waiting for transfers between devices  3.27 us (5%)
  between operations  1.42 us (2%)
    ppermute x6, starting transfers between devices, exchanged(): lax.ppermute(value, axis, [(i, (i + (1 if (i + far) % 2 == 0 else -1)) %...  33.1 us
    all_to_all x1, starting transfers between devices, shards(): column = lax.all_to_all(coarse, 'gz', 0, 0, tiled=True)  16.1 us
    pallas_call x1, Pallas kernels, shards(): pl.pallas_call(near_kernel, out_shape=(f32(LANES, TP), f32(3, HALF, LANES...  4.85 us
    pallas_call x1, Pallas kernels, shards(): pl.pallas_call(spread_kernel, out_shape=(bf16(GRID_ROWS, TP), f32(lines,...  3.94 us
    all_to_all x1, starting transfers between devices, shards(): parts = lax.all_to_all(parts, ('cx', 'gy'), 0, 0, tiled=True)  3.67 us
    pallas_call x1, Pallas kernels, shards(): pl.pallas_call(far_kernel, out_shape=f32(3, HALF, LANES), in_specs=[VMEM]...  3.15 us
    ppermute x6, waiting for transfers between devices, exchanged(): lax.ppermute(value, axis, [(i, (i + (1 if (i + far) % 2 == 0 else -1)) %...  1.94 us
  transfers between devices with their start and end apart: 8, of which 2 were waited for; matrix products, arithmetic and copies ran while one was open for 0% of the time, Pallas kernels for 12%

profile of v5, /device:TPU:1, one launch (start us, length us, event | category | flops | bytes accessed | tf_op | source)
XLA Modules:
  0.0 71.3 jit_solution(11404114277336382182)
XLA Ops:
  1.3 3.9 %spread.1 = (bf16[256,512]{1,0:T(8,128)(2,1)S(1)}, f32[32,1,128]{2,1,0:T(1,128)}, f32[3,64,128]{2,1,0:T(8,128)S(1)}, f32[8,128]{1,0:T(8,128)S(1)}, f32[64,128]{1...) custom-call(s32[1,1]{1,0:T(1,128)} %bitcast.7.live_ref, ...), custom_call_target="tpu_custom_call" | custom-call | flops 10000000 | bytes 1000000 | tf_op jit(solution)/shard_map/spread/pallas_call | solution.py:350
  5.2 16.1 %all-to-all-start = ((f32[32,1,128]{2,1,0:T(1,128)}), f32[32,1,128]{2,1,0:T(1,128)S(1)}, u32[]{:S(2)}, u32[]{:S(2)}) async-start(f32[32,1,128]{2,1,0:T(1,128)} %get-tuple-element.24), calls=%async_computation | async-start | bytes 32768 | tf_op jit(solution)/shard_map/all_to_all | solution.py:370
  21.3 0.2 faces.1
  21.6 2.9 %collective-permute-start.1 = (bf16[48,512]{1,0:T(8,128)(2,1)S(1)}, bf16[48,512]{1,0:T(8,128)(2,1)S(1)}, u32[]{:S(2)}, u32[]{:S(2)}) collective-permute-start(bf16[48,512]{1,0:T(8,128)(2,1)S(1)} %get-tuple-element.31), channel_id=1, source_target_pairs={{0,128},{128,0},{256,384},{384,256},{1,129},{129,1},{257,385},{385... | collective-permute-start | bytes 147464 | tf_op jit(solution)/shard_map/ppermute | solution.py:339
  24.4 3.1 %collective-permute-start.2 = (bf16[48,512]{1,0:T(8,128)(2,1)S(1)}, bf16[48,512]{1,0:T(8,128)(2,1)S(1)}, u32[]{:S(2)}, u32[]{:S(2)}) collective-permute-start(bf16[48,512]{1,0:T(8,128)(2,1)S(1)} %get-tuple-element.32), channel_id=1, source_target_pairs={{0,32},{32,0},{64,96},{96,64},{1,33},{33,1},{65,97},{97,65},{2,34}... | collective-permute-start | bytes 147464 | tf_op jit(solution)/shard_map/ppermute | solution.py:339
  27.6 3.7 %collective-permute-start.3 = (bf16[48,512]{1,0:T(8,128)(2,1)S(1)}, bf16[48,512]{1,0:T(8,128)(2,1)S(1)}, u32[]{:S(2)}, u32[]{:S(2)}) collective-permute-start(bf16[48,512]{1,0:T(8,128)(2,1)S(1)} %get-tuple-element.33), channel_id=1, source_target_pairs={{0,96},{32,64},{64,32},{96,0},{1,97},{33,65},{65,33},{97,1},{2,98}... | collective-permute-start | bytes 147464 | tf_op jit(solution)/shard_map/ppermute | solution.py:339
  31.3 3.4 %collective-permute-start.4 = (bf16[48,512]{1,0:T(8,128)(2,1)S(1)}, bf16[48,512]{1,0:T(8,128)(2,1)S(1)}, u32[]{:S(2)}, u32[]{:S(2)}) collective-permute-start(bf16[48,512]{1,0:T(8,128)(2,1)S(1)} %get-tuple-element.34), channel_id=1, source_target_pairs={{0,1},{1,0},{2,3},{3,2},{4,5},{5,4},{6,7},{7,6},{8,9},{9,8},{10,11... | collective-permute-start | bytes 147464 | tf_op jit(solution)/shard_map/ppermute | solution.py:339
  34.7 11.0 %collective-permute-start.5 = (bf16[48,512]{1,0:T(8,128)(2,1)S(1)}, bf16[48,512]{1,0:T(8,128)(2,1)S(1)}, u32[]{:S(2)}, u32[]{:S(2)}) collective-permute-start(bf16[48,512]{1,0:T(8,128)(2,1)S(1)} %get-tuple-element.35), channel_id=1, source_target_pairs={{0,31},{1,2},{2,1},{3,4},{4,3},{5,6},{6,5},{7,8},{8,7},{9,10},{10,... | collective-permute-start | bytes 147464 | tf_op jit(solution)/shard_map/ppermute | solution.py:339
  45.7 0.0 all-to-all-done.column_ref
  45.8 0.1 coarse.1
  45.9 0.0 collective-permute-done.1.near_x_ref
  45.9 9.0 %collective-permute-start = (bf16[48,512]{1,0:T(8,128)(2,1)S(1)}, bf16[48,512]{1,0:T(8,128)(2,1)S(1)}, u32[]{:S(2)}, u32[]{:S(2)}) collective-permute-start(bf16[48,512]{1,0:T(8,128)(2,1)S(1)} %get-tuple-element.29), channel_id=1, source_target_pairs={{0,384},{128,256},{256,128},{384,0},{1,385},{129,257},{257,129},{3... | collective-permute-start | bytes 147464 | tf_op jit(solution)/shard_map/ppermute | solution.py:339
  54.9 0.0 collective-permute-done.2.near_y_ref
  54.9 0.0 collective-permute-done.3.far_y_ref
  54.9 0.0 collective-permute-done.4.near_z_ref
  54.9 0.0 collective-permute-done.5.far_z_ref
  54.9 4.8 %near.1 = (f32[128,512]{1,0:T(8,128)S(1)}, f32[3,64,128]{2,1,0:T(8,128)S(1)}) custom-call(f32[8,128]{1,0:T(8,128)S(1)} %get-tuple-element.30.tiles_ref, bf16[256,512]{1,0:T(8,128)(2,1)S(1)} %get-tuple-element.26.grid_ref, bf16[48,512]{1,0:T(8,128)(2,1)S(1)} %collective-permute-done.1.near_x_ref, bf16[48,512]{1,0:T(8,128)(2,1)S(1)} %collective-permute-done.2.near_y_ref, ...), custom_call_target="tpu_custom_call" | custom-call | flops 1000000000 | bytes 4000000 | tf_op jit(solution)/shard_map/near/pallas_call | solution.py:397
  59.8 1.9 %collective-permute-done.far_ref.far_x_ref = bf16[48,512]{1,0:T(8,128)(2,1)S(1)} collective-permute-done((bf16[48,512]{1,0:T(8,128)(2,1)S(1)}, bf16[48,512]{1,0:T(8,128)(2,1)S(1)}, u32[]{:S(2)}, u32[]{:S(2)}) %collective-permute-start) | collective-permute-done | bytes 49184 | tf_op jit(solution)/shard_map/ppermute | solution.py:339
  61.7 0.6 merge.1
  62.3 3.7 %all-to-all-start.1 = ((f32[8,1,128]{2,1,0:T(1,128)}), f32[8,1,128]{2,1,0:T(1,128)S(1)}, u32[]{:S(2)}, u32[]{:S(2)}) async-start(f32[8,1,128]{2,1,0:T(1,128)} %merge.1), calls=%async_computation.1 | async-start | bytes 8192 | tf_op jit(solution)/shard_map/all_to_all | solution.py:420
  66.0 3.1 %far.1.near_ref = f32[3,64,128]{2,1,0:T(8,128)S(1)} custom-call(f32[8,128]{1,0:T(8,128)S(1)} %get-tuple-element.30.tiles_ref, f32[128,512]{1,0:T(8,128)S(1)} %get-tuple-element.39.field_any.part_ref, bf16[48,512]{1,0:T(8,128)(2,1)S(1)} %collective-permute-done.far_ref.far_x_ref, bf16[4,512,512]{2,1,0:T(8,128)(2,1)S(1)} %get-tuple-element.36.blocks_ref.block_ref, ...), custom_call_target="tpu_custom_call" | custom-call | flops 1000000000 | bytes 4000000 | tf_op jit(solution)/shard_map/far/pallas_call | solution.py:422
  69.1 1.3 %all-to-all-done.1.parts_ref = f32[8,1,128]{2,1,0:T(1,128)S(1)} async-done(((f32[8,1,128]{2,1,0:T(1,128)}), f32[8,1,128]{2,1,0:T(1,128)S(1)}, u32[]{:S(2)}, u32[]{:S(2)}) %all-to-all-start.1) | async-done | bytes 4128 | tf_op jit(solution)/shard_map/all_to_all | solution.py:420
  70.4 0.8 %final.1 = (f32[3,64,128]{2,1,0:T(8,128)}, f32[6,64,128]{2,1,0:T(8,128)}) custom-call(f32[8,1,128]{2,1,0:T(1,128)S(1)} %all-to-all-done.1.parts_ref, s32[64,128]{1,0:T(8,128)S(1)} %get-tuple-element.40.corner_ref, f32[3,64,128]{2,1,0:T(8,128)S(1)} %far.1.near_ref, f32[3,64,128]{2,1,0:T(8,128)S(1)} %get-tuple-element.41.unit_ref, ...), custom_call_target="tpu_custom_call" | custom-call | flops 500000 | bytes 600000 | tf_op jit(solution)/shard_map/final/pallas_call | solution.py:436
Async XLA Ops:
  5.2 40.5 %all-to-all-start = ((f32[32,1,128]{2,1,0:T(1,128)}), f32[32,1,128]{2,1,0:T(1,128)S(1)}, u32[]{:S(2)}, u32[]{:S(2)}) async-start(f32[32,1,128]{2,1,0:T(1,128)} %get-tuple-element.24), calls=%async_computation | async-start | bytes 32768 | tf_op jit(solution)/shard_map/all_to_all | solution.py:370
  21.6 24.3 %collective-permute-start.1 = (bf16[48,512]{1,0:T(8,128)(2,1)S(1)}, bf16[48,512]{1,0:T(8,128)(2,1)S(1)}, u32[]{:S(2)}, u32[]{:S(2)}) collective-permute-start(bf16[48,512]{1,0:T(8,128)(2,1)S(1)} %get-tuple-element.31), channel_id=1, source_target_pairs={{0,128},{128,0},{256,384},{384,256},{1,129},{129,1},{257,385},{385... | collective-permute-start | bytes 147464 | tf_op jit(solution)/shard_map/ppermute | solution.py:339
  24.4 30.4 %collective-permute-start.2 = (bf16[48,512]{1,0:T(8,128)(2,1)S(1)}, bf16[48,512]{1,0:T(8,128)(2,1)S(1)}, u32[]{:S(2)}, u32[]{:S(2)}) collective-permute-start(bf16[48,512]{1,0:T(8,128)(2,1)S(1)} %get-tuple-element.32), channel_id=1, source_target_pairs={{0,32},{32,0},{64,96},{96,64},{1,33},{33,1},{65,97},{97,65},{2,34}... | collective-permute-start | bytes 147464 | tf_op jit(solution)/shard_map/ppermute | solution.py:339
  27.6 27.3 %collective-permute-start.3 = (bf16[48,512]{1,0:T(8,128)(2,1)S(1)}, bf16[48,512]{1,0:T(8,128)(2,1)S(1)}, u32[]{:S(2)}, u32[]{:S(2)}) collective-permute-start(bf16[48,512]{1,0:T(8,128)(2,1)S(1)} %get-tuple-element.33), channel_id=1, source_target_pairs={{0,96},{32,64},{64,32},{96,0},{1,97},{33,65},{65,33},{97,1},{2,98}... | collective-permute-start | bytes 147464 | tf_op jit(solution)/shard_map/ppermute | solution.py:339
  31.3 23.6 %collective-permute-start.4 = (bf16[48,512]{1,0:T(8,128)(2,1)S(1)}, bf16[48,512]{1,0:T(8,128)(2,1)S(1)}, u32[]{:S(2)}, u32[]{:S(2)}) collective-permute-start(bf16[48,512]{1,0:T(8,128)(2,1)S(1)} %get-tuple-element.34), channel_id=1, source_target_pairs={{0,1},{1,0},{2,3},{3,2},{4,5},{5,4},{6,7},{7,6},{8,9},{9,8},{10,11... | collective-permute-start | bytes 147464 | tf_op jit(solution)/shard_map/ppermute | solution.py:339
  34.7 20.2 %collective-permute-start.5 = (bf16[48,512]{1,0:T(8,128)(2,1)S(1)}, bf16[48,512]{1,0:T(8,128)(2,1)S(1)}, u32[]{:S(2)}, u32[]{:S(2)}) collective-permute-start(bf16[48,512]{1,0:T(8,128)(2,1)S(1)} %get-tuple-element.35), channel_id=1, source_target_pairs={{0,31},{1,2},{2,1},{3,4},{4,3},{5,6},{6,5},{7,8},{8,7},{9,10},{10,... | collective-permute-start | bytes 147464 | tf_op jit(solution)/shard_map/ppermute | solution.py:339
  45.9 15.8 %collective-permute-start = (bf16[48,512]{1,0:T(8,128)(2,1)S(1)}, bf16[48,512]{1,0:T(8,128)(2,1)S(1)}, u32[]{:S(2)}, u32[]{:S(2)}) collective-permute-start(bf16[48,512]{1,0:T(8,128)(2,1)S(1)} %get-tuple-element.29), channel_id=1, source_target_pairs={{0,384},{128,256},{256,128},{384,0},{1,385},{129,257},{257,129},{3... | collective-permute-start | bytes 147464 | tf_op jit(solution)/shard_map/ppermute | solution.py:339
  62.3 8.1 %all-to-all-start.1 = ((f32[8,1,128]{2,1,0:T(1,128)}), f32[8,1,128]{2,1,0:T(1,128)S(1)}, u32[]{:S(2)}, u32[]{:S(2)}) async-start(f32[8,1,128]{2,1,0:T(1,128)} %merge.1), calls=%async_computation.1 | async-start | bytes 8192 | tf_op jit(solution)/shard_map/all_to_all | solution.py:420

commit v6 on v5

--- a/solution.py
+++ b/solution.py
@@ -14,6 +14,7 @@
 CUBES = TD**3
 FACE = 48
 GRID_ROWS = 256
+FAR_ROWS = 40
 EXT_ROWS = 640
 HALF = CS
 LANES = 128
@@ -163,7 +164,7 @@
         ref[...] = faces[at * FACE : (at + 1) * FACE]
 
 
-def coarse_kernel(column_ref, top_ref, face_ref, own_ref, send_ref):
+def coarse_kernel(column_ref, top_ref, face_ref, face_y_ref, own_ref, send_ref, pass_ref):
     lines = column_ref.shape[0]
     column = column_ref[...].reshape(lines, LANES)
     column = jnp.concatenate([column] * (lines * 8 // LANES), axis=1)
@@ -173,23 +174,26 @@
     rows = partial_value.shape[0]
     lanes = jnp.where((iota((rows, LANES), 1) & 7) == (iota((rows, LANES), 0) & 7), partial_value, 0.0)
     lanes = jnp.sum(lanes.reshape(rows // 8, 8, LANES), axis=1)
-    half = jnp.broadcast_to(lax.axis_index("hx"), (8, LANES)) == 0
-    own_ref[...] = jnp.where(half, lanes[:8], lanes[8:])
-    rest = jnp.where(half, lanes[8:], lanes[:8])
+    mine = iota((8, LANES), 1) >> 3 == iota((8, LANES), 0)
+    lower, upper = (jnp.sum(jnp.where(mine, lanes[at : at + 8], 0.0), axis=0, keepdims=True) for at in (0, 8))
+    half = jnp.broadcast_to(lax.axis_index("hx"), (1, LANES)) == 0
+    own_ref[...] = jnp.where(half, lower, upper)
+    rest = jnp.where(half, upper, lower)
     parts = []
     for _ in range(3):
         parts.append(rest.astype(jnp.bfloat16).astype(jnp.float32))
         rest = rest - parts[-1]
-    tail = jnp.concatenate(parts + [jnp.zeros((8, LANES), jnp.float32)], axis=1)
-    send_ref[:32] = face_ref[:32]
-    send_ref[32:] = jnp.concatenate([face_ref[32:].astype(jnp.float32)[:8], tail], axis=0).astype(jnp.bfloat16)
+    sums = jnp.concatenate(parts + [jnp.zeros((1, LANES), jnp.float32)], axis=1)
+    rows = face_ref[...].astype(jnp.float32)[:FAR_ROWS]
+    send_ref[...] = jnp.where(iota((FAR_ROWS, TP), 0) == TD * TD, sums, rows).astype(jnp.bfloat16)
+    pass_ref[...] = face_y_ref[...].astype(jnp.float32)[: pass_ref.shape[0]].astype(jnp.bfloat16)
 
 
 def merge_kernel(own_ref, far_ref, field_any, out_ref):
-    tail = far_ref[32:].astype(jnp.float32)[8:]
-    total = own_ref[...] + ((tail[:, :LANES] + tail[:, LANES : 2 * LANES]) + tail[:, 2 * LANES : 3 * LANES])
+    sums = far_ref[...].astype(jnp.float32)[TD * TD : TD * TD + 1]
+    total = own_ref[...] + ((sums[:, :LANES] + sums[:, LANES : 2 * LANES]) + sums[:, 2 * LANES : 3 * LANES])
     for brick in range(8):
-        out_ref[brick] = total[brick : brick + 1]
+        out_ref[brick] = pltpu.roll(total, (LANES - 8 * brick) % LANES, 1) if brick else total
 
 
 ATOM_ROWS = 16
@@ -232,7 +236,11 @@
 ):
     ext_ref[0:GRID_ROWS] = grid_ref[...]
     for at, ref in enumerate((near_x_ref, near_y_ref, far_y_ref, near_z_ref, far_z_ref)):
-        ext_ref[GRID_ROWS + at * FACE : GRID_ROWS + (at + 1) * FACE] = ref[...]
+        face = ref[...]
+        if face.shape[0] < FACE:
+            rest = jnp.zeros((FACE - face.shape[0], TP), jnp.float32)
+            face = jnp.concatenate([face.astype(jnp.float32), rest], axis=0).astype(jnp.bfloat16)
+        ext_ref[GRID_ROWS + at * FACE : GRID_ROWS + (at + 1) * FACE] = face
     nothing = GRID_ROWS + 5 * FACE
     ext_ref[nothing:] = jnp.zeros((EXT_ROWS - nothing, TP), jnp.bfloat16)
 
@@ -288,7 +296,7 @@
     tx, ty, tz = tile_coords(tile_column(tiles_ref))
     core = odd("gx")
     target = jnp.where(tx == (TD - 1) * core, ty * TD + tz, -1)
-    hot = (iota((LANES, FACE), 1) == target).astype(jnp.bfloat16)
+    hot = (iota((LANES, FAR_ROWS), 1) == target).astype(jnp.bfloat16)
     rows = jnp.dot(hot, far_x_ref[...], preferred_element_type=jnp.float32).astype(jnp.bfloat16)
     for side in range(2):
 
@@ -379,20 +387,21 @@
         name="faces",
     )(grid)
     near_x, far_x, near_y, far_y, near_z, far_z = faces
+    far_z, near_z = exchanged(far_z, "gz", 1), exchanged(near_z, "gz", 0)
     near_x = exchanged(near_x, ("hx", "cx"), 0)
-    near_y, far_y = exchanged(near_y, "gy", 0), exchanged(far_y, "gy", 1)
-    near_z, far_z = exchanged(near_z, "gz", 0), exchanged(far_z, "gz", 1)
-
-    own, far_x = pl.pallas_call(
+    near_y = exchanged(near_y, "gy", 0)
+
+    own, far_x, far_y = pl.pallas_call(
         coarse_kernel,
-        out_shape=(f32(8, LANES), bf16(FACE, TP)),
-        in_specs=[VMEM] * 3,
-        out_specs=[VMEM] * 2,
+        out_shape=(f32(1, LANES), bf16(FAR_ROWS, TP), bf16(36, TP)),
+        in_specs=[VMEM] * 4,
+        out_specs=[VMEM] * 3,
         compiler_params=pltpu.CompilerParams(vmem_limit_bytes=8 << 20),
         cost_estimate=pl.CostEstimate(flops=70_000, bytes_accessed=200_000, transcendentals=0),
         name="coarse",
-    )(column, top, far_x)
+    )(column, top, far_x, far_y)
     far_x = exchanged(far_x, ("hx", "cx"), 1)
+    far_y = exchanged(far_y, "gy", 1)
 
     field, unit = pl.pallas_call(
         near_kernel,
@@ -404,7 +413,7 @@
             pltpu.VMEM((3, CS, LANES), jnp.float32),
         ],
         compiler_params=pltpu.CompilerParams(vmem_limit_bytes=16 << 20),
-        cost_estimate=pl.CostEstimate(flops=1_000_000_000, bytes_accessed=4_000_000, transcendentals=200_000),
+        cost_estimate=pl.CostEstimate(flops=1000, bytes_accessed=1000, transcendentals=0),
         name="near",
     )(tiles, grid, near_x, near_y, far_y, near_z, far_z, blocks, coords, weights)
 

time: 71.6 us -> 72.5 us (1.013)
  waiting for transfers between devices: 3.27 us -> 4.16 us
    ppermute x6, waiting for transfers between devices: 1.94 us -> 2.82 us  [exchanged(): lax.ppermute(value, axis, [(i, (i + (1 if (i + far) % 2 == 0 else -1)) %...]
where the time goes in v6:
time: 72.5 us; the launch traced here: 72.1 us
  starting transfers between devices  52.8 us (73%)
  Pallas kernels  13.8 us (19%)
  waiting for transfers between devices  4.16 us (6%)
  between operations  1.41 us (2%)
    ppermute x6, starting transfers between devices, exchanged(): lax.ppermute(value, axis, [(i, (i + (1 if (i + far) % 2 == 0 else -1)) %...  32.8 us
    all_to_all x1, starting transfers between devices, shards(): column = lax.all_to_all(coarse, 'gz', 0, 0, tiled=True)  16.1 us
    pallas_call x1, Pallas kernels, shards(): pl.pallas_call(near_kernel, out_shape=(f32(LANES, TP), f32(3, HALF, LANES...  4.81 us
    pallas_call x1, Pallas kernels, shards(): pl.pallas_call(spread_kernel, out_shape=(bf16(GRID_ROWS, TP), f32(lines,...  3.94 us
    all_to_all x1, starting transfers between devices, shards(): parts = lax.all_to_all(parts, ('cx', 'gy'), 0, 0, tiled=True)  3.88 us
    pallas_call x1, Pallas kernels, shards(): pl.pallas_call(far_kernel, out_shape=f32(3, HALF, LANES), in_specs=[VMEM]...  3.14 us
    ppermute x6, waiting for transfers between devices, exchanged(): lax.ppermute(value, axis, [(i, (i + (1 if (i + far) % 2 == 0 else -1)) %...  2.82 us
  transfers between devices with their start and end apart: 8, of which 2 were waited for; matrix products, arithmetic and copies ran while one was open for 0% of the time, Pallas kernels for 12%

profile of v6, /device:TPU:1, one launch (start us, length us, event | category | flops | bytes accessed | tf_op | source)
XLA Modules:
  0.0 72.1 jit_solution(15133502199992007557)
XLA Ops:
  1.3 3.9 %spread.1 = (bf16[256,512]{1,0:T(8,128)(2,1)S(1)}, f32[32,1,128]{2,1,0:T(1,128)}, f32[3,64,128]{2,1,0:T(8,128)S(1)}, f32[8,128]{1,0:T(8,128)S(1)}, f32[64,128]{1...) custom-call(s32[1,1]{1,0:T(1,128)} %bitcast.7.live_ref, ...), custom_call_target="tpu_custom_call" | custom-call | flops 10000000 | bytes 1000000 | tf_op jit(solution)/shard_map/spread/pallas_call | solution.py:358
  5.2 16.1 %all-to-all-start = ((f32[32,1,128]{2,1,0:T(1,128)}), f32[32,1,128]{2,1,0:T(1,128)S(1)}, u32[]{:S(2)}, u32[]{:S(2)}) async-start(f32[32,1,128]{2,1,0:T(1,128)} %get-tuple-element.25), calls=%async_computation | async-start | bytes 32768 | tf_op jit(solution)/shard_map/all_to_all | solution.py:378
  21.3 0.2 faces.1
  21.6 2.9 %collective-permute-start.1 = (bf16[48,512]{1,0:T(8,128)(2,1)S(1)}, bf16[48,512]{1,0:T(8,128)(2,1)S(1)}, u32[]{:S(2)}, u32[]{:S(2)}) collective-permute-start(bf16[48,512]{1,0:T(8,128)(2,1)S(1)} %get-tuple-element.33), channel_id=1, source_target_pairs={{0,128},{128,0},{256,384},{384,256},{1,129},{129,1},{257,385},{385... | collective-permute-start | bytes 147464 | tf_op jit(solution)/shard_map/ppermute | solution.py:347
  24.4 3.1 %collective-permute-start.2 = (bf16[48,512]{1,0:T(8,128)(2,1)S(1)}, bf16[48,512]{1,0:T(8,128)(2,1)S(1)}, u32[]{:S(2)}, u32[]{:S(2)}) collective-permute-start(bf16[48,512]{1,0:T(8,128)(2,1)S(1)} %get-tuple-element.34), channel_id=1, source_target_pairs={{0,32},{32,0},{64,96},{96,64},{1,33},{33,1},{65,97},{97,65},{2,34}... | collective-permute-start | bytes 147464 | tf_op jit(solution)/shard_map/ppermute | solution.py:347
  27.6 3.4 %collective-permute-start.4 = (bf16[48,512]{1,0:T(8,128)(2,1)S(1)}, bf16[48,512]{1,0:T(8,128)(2,1)S(1)}, u32[]{:S(2)}, u32[]{:S(2)}) collective-permute-start(bf16[48,512]{1,0:T(8,128)(2,1)S(1)} %get-tuple-element.36), channel_id=1, source_target_pairs={{0,1},{1,0},{2,3},{3,2},{4,5},{5,4},{6,7},{7,6},{8,9},{9,8},{10,11... | collective-permute-start | bytes 147464 | tf_op jit(solution)/shard_map/ppermute | solution.py:347
  31.0 11.0 %collective-permute-start.5 = (bf16[48,512]{1,0:T(8,128)(2,1)S(1)}, bf16[48,512]{1,0:T(8,128)(2,1)S(1)}, u32[]{:S(2)}, u32[]{:S(2)}) collective-permute-start(bf16[48,512]{1,0:T(8,128)(2,1)S(1)} %get-tuple-element.37), channel_id=1, source_target_pairs={{0,31},{1,2},{2,1},{3,4},{4,3},{5,6},{6,5},{7,8},{8,7},{9,10},{10,... | collective-permute-start | bytes 147464 | tf_op jit(solution)/shard_map/ppermute | solution.py:347
  42.0 0.0 all-to-all-done.column_ref
  42.0 0.1 coarse.1
  42.2 8.7 %collective-permute-start = (bf16[40,512]{1,0:T(8,128)(2,1)S(1)}, bf16[40,512]{1,0:T(8,128)(2,1)S(1)}, u32[]{:S(2)}, u32[]{:S(2)}) collective-permute-start(bf16[40,512]{1,0:T(8,128)(2,1)S(1)} %get-tuple-element.31), channel_id=1, source_target_pairs={{0,384},{128,256},{256,128},{384,0},{1,385},{129,257},{257,129},{3... | collective-permute-start | bytes 122888 | tf_op jit(solution)/shard_map/ppermute | solution.py:347
  50.8 0.0 collective-permute-done.1.near_x_ref
  50.9 3.7 %collective-permute-start.3 = (bf16[36,512]{1,0:T(8,128)(2,1)S(1)}, bf16[36,512]{1,0:T(8,128)(2,1)S(1)}, u32[]{:S(2)}, u32[]{:S(2)}) collective-permute-start(bf16[36,512]{1,0:T(8,128)(2,1)S(1)} %get-tuple-element.35), channel_id=1, source_target_pairs={{0,96},{32,64},{64,32},{96,0},{1,97},{33,65},{65,33},{97,1},{2,98}... | collective-permute-start | bytes 110600 | tf_op jit(solution)/shard_map/ppermute | solution.py:347
  54.6 0.0 collective-permute-done.2.near_y_ref
  54.6 0.0 collective-permute-done.4.near_z_ref
  54.6 0.0 collective-permute-done.5.far_z_ref
  54.6 2.8 %collective-permute-done.3.far_y_ref = bf16[36,512]{1,0:T(8,128)(2,1)S(1)} collective-permute-done((bf16[36,512]{1,0:T(8,128)(2,1)S(1)}, bf16[36,512]{1,0:T(8,128)(2,1)S(1)}, u32[]{:S(2)}, u32[]{:S(2)}) %collective-permute-start.3) | collective-permute-done | bytes 36896 | tf_op jit(solution)/shard_map/ppermute | solution.py:347
  57.4 4.8 %near.1 = (f32[128,512]{1,0:T(8,128)S(1)}, f32[3,64,128]{2,1,0:T(8,128)S(1)}) custom-call(f32[8,128]{1,0:T(8,128)S(1)} %get-tuple-element.32.tiles_ref, bf16[256,512]{1,0:T(8,128)(2,1)S(1)} %get-tuple-element.27.grid_ref, bf16[48,512]{1,0:T(8,128)(2,1)S(1)} %collective-permute-done.1.near_x_ref, bf16[48,512]{1,0:T(8,128)(2,1)S(1)} %collective-permute-done.2.near_y_ref, ...), custom_call_target="tpu_custom_call" | custom-call | flops 1000 | bytes 1000 | tf_op jit(solution)/shard_map/near/pallas_call | solution.py:406
  62.2 0.0 collective-permute-done.far_ref.far_x_ref
  62.3 0.7 merge.1
  62.9 3.9 %all-to-all-start.1 = ((f32[8,1,128]{2,1,0:T(1,128)}), f32[8,1,128]{2,1,0:T(1,128)S(1)}, u32[]{:S(2)}, u32[]{:S(2)}) async-start(f32[8,1,128]{2,1,0:T(1,128)} %merge.1), calls=%async_computation.1 | async-start | bytes 8192 | tf_op jit(solution)/shard_map/all_to_all | solution.py:429
  66.8 3.1 %far.1.near_ref = f32[3,64,128]{2,1,0:T(8,128)S(1)} custom-call(f32[8,128]{1,0:T(8,128)S(1)} %get-tuple-element.32.tiles_ref, f32[128,512]{1,0:T(8,128)S(1)} %get-tuple-element.41.field_any.part_ref, bf16[40,512]{1,0:T(8,128)(2,1)S(1)} %collective-permute-done.far_ref.far_x_ref, bf16[4,512,512]{2,1,0:T(8,128)(2,1)S(1)} %get-tuple-element.38.blocks_ref.block_ref, ...), custom_call_target="tpu_custom_call" | custom-call | flops 1000000000 | bytes 4000000 | tf_op jit(solution)/shard_map/far/pallas_call | solution.py:431
  70.0 1.3 %all-to-all-done.1.parts_ref = f32[8,1,128]{2,1,0:T(1,128)S(1)} async-done(((f32[8,1,128]{2,1,0:T(1,128)}), f32[8,1,128]{2,1,0:T(1,128)S(1)}, u32[]{:S(2)}, u32[]{:S(2)}) %all-to-all-start.1) | async-done | bytes 4128 | tf_op jit(solution)/shard_map/all_to_all | solution.py:429
  71.3 0.8 %final.1 = (f32[3,64,128]{2,1,0:T(8,128)}, f32[6,64,128]{2,1,0:T(8,128)}) custom-call(f32[8,1,128]{2,1,0:T(1,128)S(1)} %all-to-all-done.1.parts_ref, s32[64,128]{1,0:T(8,128)S(1)} %get-tuple-element.42.corner_ref, f32[3,64,128]{2,1,0:T(8,128)S(1)} %far.1.near_ref, f32[3,64,128]{2,1,0:T(8,128)S(1)} %get-tuple-element.43.unit_ref, ...), custom_call_target="tpu_custom_call" | custom-call | flops 500000 | bytes 600000 | tf_op jit(solution)/shard_map/final/pallas_call | solution.py:445
Async XLA Ops:
  5.2 36.8 %all-to-all-start = ((f32[32,1,128]{2,1,0:T(1,128)}), f32[32,1,128]{2,1,0:T(1,128)S(1)}, u32[]{:S(2)}, u32[]{:S(2)}) async-start(f32[32,1,128]{2,1,0:T(1,128)} %get-tuple-element.25), calls=%async_computation | async-start | bytes 32768 | tf_op jit(solution)/shard_map/all_to_all | solution.py:378
  21.6 29.3 %collective-permute-start.1 = (bf16[48,512]{1,0:T(8,128)(2,1)S(1)}, bf16[48,512]{1,0:T(8,128)(2,1)S(1)}, u32[]{:S(2)}, u32[]{:S(2)}) collective-permute-start(bf16[48,512]{1,0:T(8,128)(2,1)S(1)} %get-tuple-element.33), channel_id=1, source_target_pairs={{0,128},{128,0},{256,384},{384,256},{1,129},{129,1},{257,385},{385... | collective-permute-start | bytes 147464 | tf_op jit(solution)/shard_map/ppermute | solution.py:347
  24.4 30.1 %collective-permute-start.2 = (bf16[48,512]{1,0:T(8,128)(2,1)S(1)}, bf16[48,512]{1,0:T(8,128)(2,1)S(1)}, u32[]{:S(2)}, u32[]{:S(2)}) collective-permute-start(bf16[48,512]{1,0:T(8,128)(2,1)S(1)} %get-tuple-element.34), channel_id=1, source_target_pairs={{0,32},{32,0},{64,96},{96,64},{1,33},{33,1},{65,97},{97,65},{2,34}... | collective-permute-start | bytes 147464 | tf_op jit(solution)/shard_map/ppermute | solution.py:347
  27.6 27.0 %collective-permute-start.4 = (bf16[48,512]{1,0:T(8,128)(2,1)S(1)}, bf16[48,512]{1,0:T(8,128)(2,1)S(1)}, u32[]{:S(2)}, u32[]{:S(2)}) collective-permute-start(bf16[48,512]{1,0:T(8,128)(2,1)S(1)} %get-tuple-element.36), channel_id=1, source_target_pairs={{0,1},{1,0},{2,3},{3,2},{4,5},{5,4},{6,7},{7,6},{8,9},{9,8},{10,11... | collective-permute-start | bytes 147464 | tf_op jit(solution)/shard_map/ppermute | solution.py:347
  31.0 23.6 %collective-permute-start.5 = (bf16[48,512]{1,0:T(8,128)(2,1)S(1)}, bf16[48,512]{1,0:T(8,128)(2,1)S(1)}, u32[]{:S(2)}, u32[]{:S(2)}) collective-permute-start(bf16[48,512]{1,0:T(8,128)(2,1)S(1)} %get-tuple-element.37), channel_id=1, source_target_pairs={{0,31},{1,2},{2,1},{3,4},{4,3},{5,6},{6,5},{7,8},{8,7},{9,10},{10,... | collective-permute-start | bytes 147464 | tf_op jit(solution)/shard_map/ppermute | solution.py:347
  42.2 20.1 %collective-permute-start = (bf16[40,512]{1,0:T(8,128)(2,1)S(1)}, bf16[40,512]{1,0:T(8,128)(2,1)S(1)}, u32[]{:S(2)}, u32[]{:S(2)}) collective-permute-start(bf16[40,512]{1,0:T(8,128)(2,1)S(1)} %get-tuple-element.31), channel_id=1, source_target_pairs={{0,384},{128,256},{256,128},{384,0},{1,385},{129,257},{257,129},{3... | collective-permute-start | bytes 122888 | tf_op jit(solution)/shard_map/ppermute | solution.py:347
  50.9 6.6 %collective-permute-start.3 = (bf16[36,512]{1,0:T(8,128)(2,1)S(1)}, bf16[36,512]{1,0:T(8,128)(2,1)S(1)}, u32[]{:S(2)}, u32[]{:S(2)}) collective-permute-start(bf16[36,512]{1,0:T(8,128)(2,1)S(1)} %get-tuple-element.35), channel_id=1, source_target_pairs={{0,96},{32,64},{64,32},{96,0},{1,97},{33,65},{65,33},{97,1},{2,98}... | collective-permute-start | bytes 110600 | tf_op jit(solution)/shard_map/ppermute | solution.py:347
  62.9 8.4 %all-to-all-start.1 = ((f32[8,1,128]{2,1,0:T(1,128)}), f32[8,1,128]{2,1,0:T(1,128)S(1)}, u32[]{:S(2)}, u32[]{:S(2)}) async-start(f32[8,1,128]{2,1,0:T(1,128)} %merge.1), calls=%async_computation.1 | async-start | bytes 8192 | tf_op jit(solution)/shard_map/all_to_all | solution.py:429

commit v7 on v6

--- a/solution.py
+++ b/solution.py
@@ -15,7 +15,7 @@
 FACE = 48
 GRID_ROWS = 256
 FAR_ROWS = 40
-EXT_ROWS = 640
+EXT_ROWS = 512
 HALF = CS
 LANES = 128
 
@@ -230,18 +230,14 @@
 
 
 def near_kernel(
-    tiles_ref, grid_ref, near_x_ref, near_y_ref, far_y_ref, near_z_ref, far_z_ref, blocks_ref, coord_ref, weights_ref,
+    tiles_ref, grid_ref, near_x_ref, near_y_ref, near_z_ref, far_z_ref, blocks_ref, coord_ref, weights_ref,
     field_ref, unit_ref,
     ext_ref, flat_ref, grad_ref,
 ):
     ext_ref[0:GRID_ROWS] = grid_ref[...]
-    for at, ref in enumerate((near_x_ref, near_y_ref, far_y_ref, near_z_ref, far_z_ref)):
-        face = ref[...]
-        if face.shape[0] < FACE:
-            rest = jnp.zeros((FACE - face.shape[0], TP), jnp.float32)
-            face = jnp.concatenate([face.astype(jnp.float32), rest], axis=0).astype(jnp.bfloat16)
-        ext_ref[GRID_ROWS + at * FACE : GRID_ROWS + (at + 1) * FACE] = face
-    nothing = GRID_ROWS + 5 * FACE
+    for at, ref in enumerate((near_x_ref, near_y_ref, near_z_ref, far_z_ref)):
+        ext_ref[GRID_ROWS + at * FACE : GRID_ROWS + (at + 1) * FACE] = ref[...]
+    nothing = GRID_ROWS + 4 * FACE
     ext_ref[nothing:] = jnp.zeros((EXT_ROWS - nothing, TP), jnp.bfloat16)
 
     tile = tile_column(tiles_ref)
@@ -250,8 +246,8 @@
     base = GRID_ROWS
     edges = (
         ("gx", tx, 36, base + row_x, nothing + 0 * row_x),
-        ("gy", ty, TD, base + FACE + row_y, base + 2 * FACE + row_y),
-        ("gz", tz, 1, base + 3 * FACE + row_z, base + 4 * FACE + row_z),
+        ("gy", ty, TD, base + FACE + row_y, nothing + 0 * row_y),
+        ("gz", tz, 1, base + 2 * FACE + row_z, base + 3 * FACE + row_z),
     )
     targets = [tile]
     for axis, place, stride, near, far in edges:
@@ -289,22 +285,26 @@
 
 
 def far_kernel(
-    tiles_ref, part_ref, far_x_ref, block_ref, coord_ref,
+    tiles_ref, part_ref, far_x_ref, far_y_ref, block_ref, coord_ref,
     near_ref,
     sum_ref, field_ref, grad_ref,
 ):
     tx, ty, tz = tile_coords(tile_column(tiles_ref))
-    core = odd("gx")
-    target = jnp.where(tx == (TD - 1) * core, ty * TD + tz, -1)
-    hot = (iota((LANES, FAR_ROWS), 1) == target).astype(jnp.bfloat16)
-    rows = jnp.dot(hot, far_x_ref[...], preferred_element_type=jnp.float32).astype(jnp.bfloat16)
-    for side in range(2):
-
-        @pl.when(core == side)
-        def _(side=side):
-            sum_ref[...] = part_ref[...] + lax.dot_general(
-                rows, block_ref[1], (((1,), (side,)), ((), ())), preferred_element_type=jnp.float32
-            )
+    sum_ref[...] = part_ref[...]
+    for axis, ref, place, row, block in (("gx", far_x_ref, tx, ty * TD + tz, 1), ("gy", far_y_ref, ty, tx * TD + tz, 2)):
+        own_side = odd(axis)
+        target = jnp.where(place == (TD - 1) * own_side, row, -1)
+        hot = (iota((LANES, FACE), 1) == target).astype(jnp.bfloat16)
+        rest = jnp.zeros((FACE - ref.shape[0], TP), jnp.float32)
+        face = jnp.concatenate([ref[...].astype(jnp.float32), rest], axis=0).astype(jnp.bfloat16)
+        rows = jnp.dot(hot, face, preferred_element_type=jnp.float32).astype(jnp.bfloat16)
+        for side in range(2):
+
+            @pl.when(own_side == side)
+            def _(side=side, rows=rows, block=block):
+                sum_ref[...] += lax.dot_general(
+                    rows, block_ref[block], (((1,), (side,)), ((), ())), preferred_element_type=jnp.float32
+                )
 
     for part in range(TP // LANES):
         field_ref[part * LANES : (part + 1) * LANES, :] = sum_ref[:, part * LANES : (part + 1) * LANES].T
@@ -406,7 +406,7 @@
     field, unit = pl.pallas_call(
         near_kernel,
         out_shape=(f32(LANES, TP), f32(3, HALF, LANES)),
-        in_specs=[VMEM] * 10,
+        in_specs=[VMEM] * 9,
         out_specs=[VMEM] * 2,
         scratch_shapes=[
             pltpu.VMEM((EXT_ROWS, TP), jnp.bfloat16), pltpu.VMEM((TP, LANES), jnp.float32),
@@ -415,7 +415,7 @@
         compiler_params=pltpu.CompilerParams(vmem_limit_bytes=16 << 20),
         cost_estimate=pl.CostEstimate(flops=1000, bytes_accessed=1000, transcendentals=0),
         name="near",
-    )(tiles, grid, near_x, near_y, far_y, near_z, far_z, blocks, coords, weights)
+    )(tiles, grid, near_x, near_y, near_z, far_z, blocks, coords, weights)
 
     parts = pl.pallas_call(
         merge_kernel,
@@ -431,7 +431,7 @@
     near = pl.pallas_call(
         far_kernel,
         out_shape=f32(3, HALF, LANES),
-        in_specs=[VMEM] * 5,
+        in_specs=[VMEM] * 6,
         out_specs=VMEM,
         scratch_shapes=[
             pltpu.VMEM((LANES, TP), jnp.float32), pltpu.VMEM((TP, LANES), jnp.float32),
@@ -440,7 +440,7 @@
         compiler_params=pltpu.CompilerParams(vmem_limit_bytes=16 << 20),
         cost_estimate=pl.CostEstimate(flops=1_000_000_000, bytes_accessed=4_000_000, transcendentals=200_000),
         name="far",
-    )(tiles, field, far_x, blocks, coords)
+    )(tiles, field, far_x, far_y, blocks, coords)
 
     forces, virial = pl.pallas_call(
         final_kernel,

time: 72.5 us -> 68.7 us (0.948)
  waiting for transfers between devices: 4.16 us -> 0.77 us
    ppermute x6, waiting for transfers between devices: 2.82 us -> 0.02 us  [exchanged(): lax.ppermute(value, axis, [(i, (i + (1 if (i + far) % 2 == 0 else -1)) %...]
  transfers between devices with their start and end apart: 8 -> 8, of which waited for: 2 -> 1; matrix products, arithmetic and copies ran while one was open for 0% -> 0% of each run, Pallas kernels for 12% -> 14%
where the time goes in v7:
time: 68.7 us; the launch traced here: 68.4 us
  starting transfers between devices  52.2 us (76%)
  Pallas kernels  14 us (20%)
  between operations  1.43 us (2%)
  waiting for transfers between devices  0.77 us (1%)
    ppermute x6, starting transfers between devices, exchanged(): lax.ppermute(value, axis, [(i, (i + (1 if (i + far) % 2 == 0 else -1)) %...  32.8 us
    all_to_all x1, starting transfers between devices, shards(): column = lax.all_to_all(coarse, 'gz', 0, 0, tiled=True)  16.1 us
    pallas_call x1, Pallas kernels, shards(): pl.pallas_call(near_kernel, out_shape=(f32(LANES, TP), f32(3, HALF, LANES...  4.59 us
    pallas_call x1, Pallas kernels, shards(): pl.pallas_call(spread_kernel, out_shape=(bf16(GRID_ROWS, TP), f32(lines,...  3.94 us
    pallas_call x1, Pallas kernels, shards(): pl.pallas_call(far_kernel, out_shape=f32(3, HALF, LANES), in_specs=[VMEM]...  3.6 us
    all_to_all x1, starting transfers between devices, shards(): parts = lax.all_to_all(parts, ('cx', 'gy'), 0, 0, tiled=True)  3.26 us
  transfers between devices with their start and end apart: 8, of which 1 were waited for; matrix products, arithmetic and copies ran while one was open for 0% of the time, Pallas kernels for 14%

profile of v7, /device:TPU:1, one launch (start us, length us, event | category | flops | bytes accessed | tf_op | source)
XLA Modules:
  0.0 68.4 jit_solution(16337673037759975632)
XLA Ops:
  1.3 3.9 %spread.1 = (bf16[256,512]{1,0:T(8,128)(2,1)S(1)}, f32[32,1,128]{2,1,0:T(1,128)}, f32[3,64,128]{2,1,0:T(8,128)S(1)}, f32[8,128]{1,0:T(8,128)S(1)}, f32[64,128]{1...) custom-call(s32[1,1]{1,0:T(1,128)} %bitcast.7.live_ref, ...), custom_call_target="tpu_custom_call" | custom-call | flops 10000000 | bytes 1000000 | tf_op jit(solution)/shard_map/spread/pallas_call | solution.py:358
  5.2 16.1 %all-to-all-start = ((f32[32,1,128]{2,1,0:T(1,128)}), f32[32,1,128]{2,1,0:T(1,128)S(1)}, u32[]{:S(2)}, u32[]{:S(2)}) async-start(f32[32,1,128]{2,1,0:T(1,128)} %get-tuple-element.25), calls=%async_computation | async-start | bytes 32768 | tf_op jit(solution)/shard_map/all_to_all | solution.py:378
  21.3 0.2 faces.1
  21.6 2.9 %collective-permute-start.1 = (bf16[48,512]{1,0:T(8,128)(2,1)S(1)}, bf16[48,512]{1,0:T(8,128)(2,1)S(1)}, u32[]{:S(2)}, u32[]{:S(2)}) collective-permute-start(bf16[48,512]{1,0:T(8,128)(2,1)S(1)} %get-tuple-element.33), channel_id=1, source_target_pairs={{0,128},{128,0},{256,384},{384,256},{1,129},{129,1},{257,385},{385... | collective-permute-start | bytes 147464 | tf_op jit(solution)/shard_map/ppermute | solution.py:347
  24.4 3.1 %collective-permute-start.2 = (bf16[48,512]{1,0:T(8,128)(2,1)S(1)}, bf16[48,512]{1,0:T(8,128)(2,1)S(1)}, u32[]{:S(2)}, u32[]{:S(2)}) collective-permute-start(bf16[48,512]{1,0:T(8,128)(2,1)S(1)} %get-tuple-element.34), channel_id=1, source_target_pairs={{0,32},{32,0},{64,96},{96,64},{1,33},{33,1},{65,97},{97,65},{2,34}... | collective-permute-start | bytes 147464 | tf_op jit(solution)/shard_map/ppermute | solution.py:347
  27.6 3.4 %collective-permute-start.3 = (bf16[48,512]{1,0:T(8,128)(2,1)S(1)}, bf16[48,512]{1,0:T(8,128)(2,1)S(1)}, u32[]{:S(2)}, u32[]{:S(2)}) collective-permute-start(bf16[48,512]{1,0:T(8,128)(2,1)S(1)} %get-tuple-element.35), channel_id=1, source_target_pairs={{0,1},{1,0},{2,3},{3,2},{4,5},{5,4},{6,7},{7,6},{8,9},{9,8},{10,11... | collective-permute-start | bytes 147464 | tf_op jit(solution)/shard_map/ppermute | solution.py:347
  31.0 11.0 %collective-permute-start.4 = (bf16[48,512]{1,0:T(8,128)(2,1)S(1)}, bf16[48,512]{1,0:T(8,128)(2,1)S(1)}, u32[]{:S(2)}, u32[]{:S(2)}) collective-permute-start(bf16[48,512]{1,0:T(8,128)(2,1)S(1)} %get-tuple-element.36), channel_id=1, source_target_pairs={{0,31},{1,2},{2,1},{3,4},{4,3},{5,6},{6,5},{7,8},{8,7},{9,10},{10,... | collective-permute-start | bytes 147464 | tf_op jit(solution)/shard_map/ppermute | solution.py:347
  42.0 0.0 all-to-all-done.column_ref
  42.0 0.1 coarse.1
  42.2 8.7 %collective-permute-start = (bf16[40,512]{1,0:T(8,128)(2,1)S(1)}, bf16[40,512]{1,0:T(8,128)(2,1)S(1)}, u32[]{:S(2)}, u32[]{:S(2)}) collective-permute-start(bf16[40,512]{1,0:T(8,128)(2,1)S(1)} %get-tuple-element.31), channel_id=1, source_target_pairs={{0,384},{128,256},{256,128},{384,0},{1,385},{129,257},{257,129},{3... | collective-permute-start | bytes 122888 | tf_op jit(solution)/shard_map/ppermute | solution.py:347
  50.8 0.0 collective-permute-done.1.near_x_ref
  50.9 3.7 %collective-permute-start.5 = (bf16[36,512]{1,0:T(8,128)(2,1)S(1)}, bf16[36,512]{1,0:T(8,128)(2,1)S(1)}, u32[]{:S(2)}, u32[]{:S(2)}) collective-permute-start(bf16[36,512]{1,0:T(8,128)(2,1)S(1)} %get-tuple-element.42), channel_id=1, source_target_pairs={{0,96},{32,64},{64,32},{96,0},{1,97},{33,65},{65,33},{97,1},{2,98}... | collective-permute-start | bytes 110600 | tf_op jit(solution)/shard_map/ppermute | solution.py:347
  54.6 0.0 collective-permute-done.2.near_y_ref
  54.6 0.0 collective-permute-done.3.near_z_ref
  54.6 0.0 collective-permute-done.4.far_z_ref
  54.6 4.6 %near.1 = (f32[128,512]{1,0:T(8,128)S(1)}, f32[3,64,128]{2,1,0:T(8,128)S(1)}) custom-call(f32[8,128]{1,0:T(8,128)S(1)} %get-tuple-element.32.tiles_ref, bf16[256,512]{1,0:T(8,128)(2,1)S(1)} %get-tuple-element.27.grid_ref, bf16[48,512]{1,0:T(8,128)(2,1)S(1)} %collective-permute-done.1.near_x_ref, bf16[48,512]{1,0:T(8,128)(2,1)S(1)} %collective-permute-done.2.near_y_ref, ...), custom_call_target="tpu_custom_call" | custom-call | flops 1000 | bytes 1000 | tf_op jit(solution)/shard_map/near/pallas_call | solution.py:406
  59.2 0.0 collective-permute-done.far_ref.far_x_ref
  59.2 0.7 merge.1
  59.9 3.3 %all-to-all-start.1 = ((f32[8,1,128]{2,1,0:T(1,128)}), f32[8,1,128]{2,1,0:T(1,128)S(1)}, u32[]{:S(2)}, u32[]{:S(2)}) async-start(f32[8,1,128]{2,1,0:T(1,128)} %merge.1), calls=%async_computation.1 | async-start | bytes 8192 | tf_op jit(solution)/shard_map/all_to_all | solution.py:429
  63.2 0.0 collective-permute-done.5.far_y_ref
  63.2 3.6 %far.1.near_ref = f32[3,64,128]{2,1,0:T(8,128)S(1)} custom-call(f32[8,128]{1,0:T(8,128)S(1)} %get-tuple-element.32.tiles_ref, f32[128,512]{1,0:T(8,128)S(1)} %get-tuple-element.40.field_any.part_ref, bf16[40,512]{1,0:T(8,128)(2,1)S(1)} %collective-permute-done.far_ref.far_x_ref, bf16[36,512]{1,0:T(8,128)(2,1)S(1)} %collective-permute-done.5.far_y_ref, ...), custom_call_target="tpu_custom_call" | custom-call | flops 1000000000 | bytes 4000000 | tf_op jit(solution)/shard_map/far/pallas_call | solution.py:431
  66.8 0.8 %all-to-all-done.1.parts_ref = f32[8,1,128]{2,1,0:T(1,128)S(1)} async-done(((f32[8,1,128]{2,1,0:T(1,128)}), f32[8,1,128]{2,1,0:T(1,128)S(1)}, u32[]{:S(2)}, u32[]{:S(2)}) %all-to-all-start.1) | async-done | bytes 4128 | tf_op jit(solution)/shard_map/all_to_all | solution.py:429
  67.5 0.8 %final.1 = (f32[3,64,128]{2,1,0:T(8,128)}, f32[6,64,128]{2,1,0:T(8,128)}) custom-call(f32[8,1,128]{2,1,0:T(1,128)S(1)} %all-to-all-done.1.parts_ref, s32[64,128]{1,0:T(8,128)S(1)} %get-tuple-element.41.corner_ref, f32[3,64,128]{2,1,0:T(8,128)S(1)} %far.1.near_ref, f32[3,64,128]{2,1,0:T(8,128)S(1)} %get-tuple-element.43.unit_ref, ...), custom_call_target="tpu_custom_call" | custom-call | flops 500000 | bytes 600000 | tf_op jit(solution)/shard_map/final/pallas_call | solution.py:445
Async XLA Ops:
  5.2 36.8 %all-to-all-start = ((f32[32,1,128]{2,1,0:T(1,128)}), f32[32,1,128]{2,1,0:T(1,128)S(1)}, u32[]{:S(2)}, u32[]{:S(2)}) async-start(f32[32,1,128]{2,1,0:T(1,128)} %get-tuple-element.25), calls=%async_computation | async-start | bytes 32768 | tf_op jit(solution)/shard_map/all_to_all | solution.py:378
  21.6 29.3 %collective-permute-start.1 = (bf16[48,512]{1,0:T(8,128)(2,1)S(1)}, bf16[48,512]{1,0:T(8,128)(2,1)S(1)}, u32[]{:S(2)}, u32[]{:S(2)}) collective-permute-start(bf16[48,512]{1,0:T(8,128)(2,1)S(1)} %get-tuple-element.33), channel_id=1, source_target_pairs={{0,128},{128,0},{256,384},{384,256},{1,129},{129,1},{257,385},{385... | collective-permute-start | bytes 147464 | tf_op jit(solution)/shard_map/ppermute | solution.py:347
  24.4 30.1 %collective-permute-start.2 = (bf16[48,512]{1,0:T(8,128)(2,1)S(1)}, bf16[48,512]{1,0:T(8,128)(2,1)S(1)}, u32[]{:S(2)}, u32[]{:S(2)}) collective-permute-start(bf16[48,512]{1,0:T(8,128)(2,1)S(1)} %get-tuple-element.34), channel_id=1, source_target_pairs={{0,32},{32,0},{64,96},{96,64},{1,33},{33,1},{65,97},{97,65},{2,34}... | collective-permute-start | bytes 147464 | tf_op jit(solution)/shard_map/ppermute | solution.py:347
  27.6 27.0 %collective-permute-start.3 = (bf16[48,512]{1,0:T(8,128)(2,1)S(1)}, bf16[48,512]{1,0:T(8,128)(2,1)S(1)}, u32[]{:S(2)}, u32[]{:S(2)}) collective-permute-start(bf16[48,512]{1,0:T(8,128)(2,1)S(1)} %get-tuple-element.35), channel_id=1, source_target_pairs={{0,1},{1,0},{2,3},{3,2},{4,5},{5,4},{6,7},{7,6},{8,9},{9,8},{10,11... | collective-permute-start | bytes 147464 | tf_op jit(solution)/shard_map/ppermute | solution.py:347
  31.0 23.6 %collective-permute-start.4 = (bf16[48,512]{1,0:T(8,128)(2,1)S(1)}, bf16[48,512]{1,0:T(8,128)(2,1)S(1)}, u32[]{:S(2)}, u32[]{:S(2)}) collective-permute-start(bf16[48,512]{1,0:T(8,128)(2,1)S(1)} %get-tuple-element.36), channel_id=1, source_target_pairs={{0,31},{1,2},{2,1},{3,4},{4,3},{5,6},{6,5},{7,8},{8,7},{9,10},{10,... | collective-permute-start | bytes 147464 | tf_op jit(solution)/shard_map/ppermute | solution.py:347
  42.2 17.1 %collective-permute-start = (bf16[40,512]{1,0:T(8,128)(2,1)S(1)}, bf16[40,512]{1,0:T(8,128)(2,1)S(1)}, u32[]{:S(2)}, u32[]{:S(2)}) collective-permute-start(bf16[40,512]{1,0:T(8,128)(2,1)S(1)} %get-tuple-element.31), channel_id=1, source_target_pairs={{0,384},{128,256},{256,128},{384,0},{1,385},{129,257},{257,129},{3... | collective-permute-start | bytes 122888 | tf_op jit(solution)/shard_map/ppermute | solution.py:347
  50.9 12.3 %collective-permute-start.5 = (bf16[36,512]{1,0:T(8,128)(2,1)S(1)}, bf16[36,512]{1,0:T(8,128)(2,1)S(1)}, u32[]{:S(2)}, u32[]{:S(2)}) collective-permute-start(bf16[36,512]{1,0:T(8,128)(2,1)S(1)} %get-tuple-element.42), channel_id=1, source_target_pairs={{0,96},{32,64},{64,32},{96,0},{1,97},{33,65},{65,33},{97,1},{2,98}... | collective-permute-start | bytes 110600 | tf_op jit(solution)/shard_map/ppermute | solution.py:347
  59.9 7.6 %all-to-all-start.1 = ((f32[8,1,128]{2,1,0:T(1,128)}), f32[8,1,128]{2,1,0:T(1,128)S(1)}, u32[]{:S(2)}, u32[]{:S(2)}) async-start(f32[8,1,128]{2,1,0:T(1,128)} %merge.1), calls=%async_computation.1 | async-start | bytes 8192 | tf_op jit(solution)/shard_map/all_to_all | solution.py:429

commit v8 on v7

--- a/solution.py
+++ b/solution.py
@@ -15,7 +15,6 @@
 FACE = 48
 GRID_ROWS = 256
 FAR_ROWS = 40
-EXT_ROWS = 512
 HALF = CS
 LANES = 128
 
@@ -59,8 +58,8 @@
 
 def spread_kernel(
     live_ref, pos_any, charge_any, tile_any, weights_any, blocks_any, top_any,
-    grid_ref, coarse_ref, coord_ref, tiles_ref, drive_ref, frac_ref, corner_ref, weights_ref, blocks_ref, top_ref,
-    pos_ref, charge_ref, tile_ref, wx_ref, wy_ref, wz_ref, cell_ref, sems,
+    grid_ref, coarse_any, coord_ref, tiles_ref, frac_ref, corner_ref, weights_ref, blocks_ref, top_ref, wx_any, wy_any,
+    pos_ref, charge_ref, tile_ref, wx_ref, wy_ref, wz_ref, cell_ref, coarse_ref, sems,
 ):
     moves = [
         pltpu.make_async_copy(source, target, sems.at[at])
@@ -68,13 +67,16 @@
             (
                 (pos_any, pos_ref), (charge_any, charge_ref), (tile_any, tile_ref),
                 (weights_any, weights_ref), (blocks_any, blocks_ref), (top_any, top_ref),
+                (wx_ref, wx_any), (wy_ref, wy_any), (coarse_ref, coarse_any),
             )
         )
     ]
-    for move in moves:
+    for move in moves[:4]:
         move.start()
     for move in moves[:3]:
         move.wait()
+    for move in moves[4:6]:
+        move.start()
     cluster = 2 * iota((HALF, LANES), 0) + (iota((HALF, LANES), 1) >> 6)
     charge = charge_ref[...] * (cluster < live_ref[0, 0]).astype(jnp.float32)
     x, y = to_clusters(pos_ref[0], pos_ref[1])
@@ -83,6 +85,8 @@
     for node in range(TL):
         wx_ref[node] = q * bump(x - node)
         wy_ref[node] = bump(y - node)
+    moves[6].start()
+    moves[7].start()
     nodes = iota((TL, LANES), 0).astype(jnp.float32)
     for atom in range(CS):
         wz_ref[atom] = bump(z[atom : atom + 1] - nodes)
@@ -130,6 +134,7 @@
     coarse = coarse * (1.0 / math.sqrt(TP * 27))
     for line in range(coarse_ref.shape[0]):
         coarse_ref[line] = coarse
+    moves[8].start()
 
     own_row = (iota((HALF, LANES), 1) >> 1) == iota((HALF, LANES), 0)
     rows = jnp.where(own_row, tile_ref[...].astype(jnp.float32), 0.0).astype(jnp.bfloat16)
@@ -137,7 +142,6 @@
     tile = jnp.dot(rows, side, preferred_element_type=jnp.float32).astype(jnp.int32)
     places = tile_coords(tile)
     corner_ref[...] = corner_of(places)
-    drive_ref[...] = -charge
     for axis in range(3):
         frac_ref[axis] = (places[axis].astype(jnp.float32) * TL + pos_ref[axis]) * (1.0 / (TL * TD))
     for move in moves[4:]:
@@ -210,14 +214,16 @@
                 run = term if run is None else run + term
                 if k:
                     mean = run if mean is None else mean + run
-            part = wy[j] * run
-            cross = wy[j] * mean
+            weight = wy(j)
+            part = weight * run
+            cross = weight * mean
             a = part if a is None else a + part
             c = cross if c is None else c + cross
             if j:
                 b = a if b is None else b + a
+        weight = wx(i)
         for at, value in enumerate((a, b, c)):
-            term = wx[i] * value
+            term = weight * value
             sums[at] = term if sums[at] is None else sums[at] + term
         if i:
             sums[3] = sums[0] if sums[3] is None else sums[3] + sums[0]
@@ -230,65 +236,75 @@
 
 
 def near_kernel(
-    tiles_ref, grid_ref, near_x_ref, near_y_ref, near_z_ref, far_z_ref, blocks_ref, coord_ref, weights_ref,
+    tiles_ref, grid_ref, near_x_ref, near_y_ref, near_z_ref, far_z_ref, blocks_ref, coord_ref, weights_ref, wx_any, wy_any,
     field_ref, unit_ref,
-    ext_ref, flat_ref, grad_ref,
+    flat_ref, grad_ref, wx_ref, wy_ref, sems,
 ):
-    ext_ref[0:GRID_ROWS] = grid_ref[...]
-    for at, ref in enumerate((near_x_ref, near_y_ref, near_z_ref, far_z_ref)):
-        ext_ref[GRID_ROWS + at * FACE : GRID_ROWS + (at + 1) * FACE] = ref[...]
-    nothing = GRID_ROWS + 4 * FACE
-    ext_ref[nothing:] = jnp.zeros((EXT_ROWS - nothing, TP), jnp.bfloat16)
-
+    moves = read_weights(wx_any, wy_any, wx_ref, wy_ref, sems)
     tile = tile_column(tiles_ref)
     tx, ty, tz = tile_coords(tile)
     row_x, row_y, row_z = ty * TD + tz, tx * TD + tz, tx * TD + ty
-    base = GRID_ROWS
+
+    def picked(ref, row):
+        hot = (iota((LANES, ref.shape[0]), 1) == row).astype(jnp.bfloat16)
+        return jnp.dot(hot, ref[...], preferred_element_type=jnp.float32)
+
+    field = lax.dot_general(
+        picked(grid_ref, tile).astype(jnp.bfloat16), blocks_ref[0], (((1,), (1,)), ((), ())), preferred_element_type=jnp.float32
+    )
     edges = (
-        ("gx", tx, 36, base + row_x, nothing + 0 * row_x),
-        ("gy", ty, TD, base + FACE + row_y, nothing + 0 * row_y),
-        ("gz", tz, 1, base + 2 * FACE + row_z, base + 3 * FACE + row_z),
-    )
-    targets = [tile]
-    for axis, place, stride, near, far in edges:
-        side = jnp.broadcast_to(odd(axis), near.shape) == 1
-        targets.append(jnp.where(place < TD - 1, tile + stride, jnp.where(side, far, near)))
-        targets.append(jnp.where(place > 0, tile - stride, jnp.where(side, near, far)))
-    at_row = iota((LANES, EXT_ROWS), 1)
-    field = None
-    for at, target in enumerate(targets):
-        hot = (at_row == target).astype(jnp.bfloat16)
-        rows = jnp.dot(hot, ext_ref[...], preferred_element_type=jnp.float32).astype(jnp.bfloat16)
-        flipped = at > 0 and at % 2 == 0
-        term = lax.dot_general(
-            rows, blocks_ref[(at + 1) // 2], (((1,), (0 if flipped else 1,)), ((), ())), preferred_element_type=jnp.float32
-        )
-        field = term if field is None else field + term
+        ("gx", tx, 36, row_x, near_x_ref, None),
+        ("gy", ty, TD, row_y, near_y_ref, None),
+        ("gz", tz, 1, row_z, near_z_ref, far_z_ref),
+    )
+    for block, (axis, place, stride, row, near_face, far_face) in enumerate(edges, 1):
+        side = jnp.broadcast_to(odd(axis), row.shape)
+        for down in range(2):
+            edge = place == (TD - 1) * (1 - down)
+            rows = picked(grid_ref, jnp.where(edge, -1, tile + (1 - 2 * down) * stride))
+            rows += picked(near_face, jnp.where(edge & (side == down), row, -1))
+            if far_face is not None:
+                rows += picked(far_face, jnp.where(edge & (side != down), row, -1))
+            field += lax.dot_general(
+                rows.astype(jnp.bfloat16), blocks_ref[block], (((1,), (1 - down,)), ((), ())),
+                preferred_element_type=jnp.float32,
+            )
     field_ref[...] = field
     for part in range(TP // LANES):
         flat_ref[part * LANES : (part + 1) * LANES, :] = jnp.broadcast_to(
             weights_ref[:, part * LANES : (part + 1) * LANES], (LANES, LANES)
         ).T
-    all_gradients(flat_ref, coord_ref, grad_ref)
+    for move in moves:
+        move.wait()
+    all_gradients(flat_ref, coord_ref, wx_ref, wy_ref, grad_ref)
     unit_ref[0], unit_ref[1] = to_atoms(grad_ref[0], grad_ref[1])
     unit_ref[2], _ = to_atoms(grad_ref[2], grad_ref[2])
 
 
-def all_gradients(field_ref, coord_ref, grad_ref):
+def read_weights(wx_any, wy_any, wx_ref, wy_ref, sems):
+    moves = [pltpu.make_async_copy(wx_any, wx_ref, sems.at[0]), pltpu.make_async_copy(wy_any, wy_ref, sems.at[1])]
+    for move in moves:
+        move.start()
+    return moves
+
+
+def all_gradients(field_ref, coord_ref, wx_ref, wy_ref, grad_ref):
     @pl.loop(0, CS // ATOM_ROWS)
     def _(group):
         rows = pl.ds(pl.multiple_of(group * ATOM_ROWS, ATOM_ROWS), ATOM_ROWS)
         x, y, z = coord_ref[0, rows, :], coord_ref[1, rows, :], coord_ref[2, rows, :]
-        wx, wy, wz = ([bump(u - node) for node in range(TL)] for u in (x, y, z))
-        for axis, value in enumerate(gradients(field_ref, wx, wy, wz, x, y, z)):
-            grad_ref[axis, rows, :] = value
+        wz = [bump(z - node) for node in range(TL)]
+        values = gradients(field_ref, lambda i: wx_ref[i, rows, :], lambda j: wy_ref[j, rows, :], wz, x, y, z)
+        for axis, value in enumerate(values):
+            grad_ref[axis, rows, :] = -value
 
 
 def far_kernel(
-    tiles_ref, part_ref, far_x_ref, far_y_ref, block_ref, coord_ref,
+    tiles_ref, part_ref, far_x_ref, far_y_ref, block_ref, coord_ref, wx_any, wy_any,
     near_ref,
-    sum_ref, field_ref, grad_ref,
+    sum_ref, field_ref, grad_ref, wx_ref, wy_ref, sems,
 ):
+    moves = read_weights(wx_any, wy_any, wx_ref, wy_ref, sems)
     tx, ty, tz = tile_coords(tile_column(tiles_ref))
     sum_ref[...] = part_ref[...]
     for axis, ref, place, row, block in (("gx", far_x_ref, tx, ty * TD + tz, 1), ("gy", far_y_ref, ty, tx * TD + tz, 2)):
@@ -308,19 +324,20 @@
 
     for part in range(TP // LANES):
         field_ref[part * LANES : (part + 1) * LANES, :] = sum_ref[:, part * LANES : (part + 1) * LANES].T
-    all_gradients(field_ref, coord_ref, grad_ref)
+    for move in moves:
+        move.wait()
+    all_gradients(field_ref, coord_ref, wx_ref, wy_ref, grad_ref)
     near_ref[0], near_ref[1] = to_atoms(grad_ref[0], grad_ref[1])
     near_ref[2], _ = to_atoms(grad_ref[2], grad_ref[2])
 
 
-def final_kernel(parts_ref, corner_ref, near_ref, unit_ref, frac_ref, drive_ref, force_ref, virial_ref):
+def final_kernel(parts_ref, corner_ref, near_ref, unit_ref, frac_ref, force_ref, virial_ref):
     coarse = jnp.sum(parts_ref[...].reshape(parts_ref.shape[0], LANES), axis=0, keepdims=True)
     corner = corner_ref[...]
     pot = jnp.zeros((HALF, LANES), jnp.float32)
     for at in range(8):
         pot = jnp.where(corner == at, coarse[:, at : at + 1], pot)
-    drive = drive_ref[...]
-    forces = [drive * (near_ref[axis] + pot * unit_ref[axis]) for axis in range(3)]
+    forces = [near_ref[axis] + pot * unit_ref[axis] for axis in range(3)]
     for axis in range(3):
         force_ref[axis] = forces[axis]
         virial_ref[axis] = frac_ref[axis] * forces[axis]
@@ -332,6 +349,7 @@
 VMEM = pl.BlockSpec(memory_space=pltpu.VMEM)
 SMEM = pl.BlockSpec(memory_space=pltpu.SMEM)
 ANY = pl.BlockSpec(memory_space=pl.ANY)
+HBM = pl.BlockSpec(memory_space=pltpu.HBM)
 
 
 def f32(*shape):
@@ -355,26 +373,27 @@
     weights = restrict_weights.reshape(1, TP)
     lines = lax.axis_size("gz")
 
-    grid, coarse, coords, tiles, drive, frac, corner, weights, blocks, top = pl.pallas_call(
+    grid, coarse, coords, tiles, frac, corner, weights, blocks, top, wx, wy = pl.pallas_call(
         spread_kernel,
         out_shape=(
-            bf16(GRID_ROWS, TP), f32(lines, 1, LANES), f32(3, CS, LANES), f32(8, LANES), f32(HALF, LANES),
+            bf16(GRID_ROWS, TP), f32(lines, 1, LANES), f32(3, CS, LANES), f32(8, LANES),
             f32(3, HALF, LANES), jax.ShapeDtypeStruct((HALF, LANES), jnp.int32), f32(1, TP),
-            bf16(*kernel_blocks.shape), f32(*top_kernel.shape),
+            bf16(*kernel_blocks.shape), f32(*top_kernel.shape), pltpu.HBM((TL, CS, LANES), jnp.float32), pltpu.HBM((TL, CS, LANES), jnp.float32),
         ),
         in_specs=[SMEM] + [ANY] * 6,
-        out_specs=[VMEM] * 10,
+        out_specs=[VMEM, HBM] + [VMEM] * 7 + [HBM] * 2,
         scratch_shapes=[
             pltpu.VMEM((3, HALF, LANES), jnp.float32), pltpu.VMEM((HALF, LANES), jnp.float32),
             pltpu.VMEM((1, LANES), jnp.int32),
             pltpu.VMEM((TL, CS, LANES), jnp.float32), pltpu.VMEM((TL, CS, LANES), jnp.float32),
             pltpu.VMEM((CS, TL, LANES), jnp.float32), pltpu.VMEM((TP, LANES), jnp.float32),
-            pltpu.SemaphoreType.DMA((6,)),
+            pltpu.VMEM((lines, 1, LANES), jnp.float32), pltpu.SemaphoreType.DMA((9,)),
         ],
         compiler_params=pltpu.CompilerParams(vmem_limit_bytes=12 << 20),
         cost_estimate=pl.CostEstimate(flops=10_000_000, bytes_accessed=1_000_000, transcendentals=200_000),
         name="spread",
     )(live, *(pltpu.with_memory_space_constraint(a, pltpu.HBM) for a in (pos, charge, tile, weights, kernel_blocks, top_kernel)))
+    wx, wy = (pltpu.with_memory_space_constraint(a, pltpu.HBM) for a in (wx, wy))
     column = lax.all_to_all(coarse, "gz", 0, 0, tiled=True)
 
     faces = pl.pallas_call(
@@ -406,16 +425,16 @@
     field, unit = pl.pallas_call(
         near_kernel,
         out_shape=(f32(LANES, TP), f32(3, HALF, LANES)),
-        in_specs=[VMEM] * 9,
+        in_specs=[VMEM] * 9 + [HBM] * 2,
         out_specs=[VMEM] * 2,
         scratch_shapes=[
-            pltpu.VMEM((EXT_ROWS, TP), jnp.bfloat16), pltpu.VMEM((TP, LANES), jnp.float32),
-            pltpu.VMEM((3, CS, LANES), jnp.float32),
+            pltpu.VMEM((TP, LANES), jnp.float32), pltpu.VMEM((3, CS, LANES), jnp.float32),
+            pltpu.VMEM((TL, CS, LANES), jnp.float32), pltpu.VMEM((TL, CS, LANES), jnp.float32), pltpu.SemaphoreType.DMA((2,)),
         ],
         compiler_params=pltpu.CompilerParams(vmem_limit_bytes=16 << 20),
         cost_estimate=pl.CostEstimate(flops=1000, bytes_accessed=1000, transcendentals=0),
         name="near",
-    )(tiles, grid, near_x, near_y, near_z, far_z, blocks, coords, weights)
+    )(tiles, grid, near_x, near_y, near_z, far_z, blocks, coords, weights, wx, wy)
 
     parts = pl.pallas_call(
         merge_kernel,
@@ -431,26 +450,27 @@
     near = pl.pallas_call(
         far_kernel,
         out_shape=f32(3, HALF, LANES),
-        in_specs=[VMEM] * 6,
+        in_specs=[VMEM] * 6 + [HBM] * 2,
         out_specs=VMEM,
         scratch_shapes=[
             pltpu.VMEM((LANES, TP), jnp.float32), pltpu.VMEM((TP, LANES), jnp.float32),
             pltpu.VMEM((3, CS, LANES), jnp.float32),
+            pltpu.VMEM((TL, CS, LANES), jnp.float32), pltpu.VMEM((TL, CS, LANES), jnp.float32), pltpu.SemaphoreType.DMA((2,)),
         ],
         compiler_params=pltpu.CompilerParams(vmem_limit_bytes=16 << 20),
         cost_estimate=pl.CostEstimate(flops=1_000_000_000, bytes_accessed=4_000_000, transcendentals=200_000),
         name="far",
-    )(tiles, field, far_x, far_y, blocks, coords)
+    )(tiles, field, far_x, far_y, blocks, coords, wx, wy)
 
     forces, virial = pl.pallas_call(
         final_kernel,
         out_shape=(f32(3, HALF, LANES), f32(6, HALF, LANES)),
-        in_specs=[VMEM] * 6,
+        in_specs=[VMEM] * 5,
         out_specs=[VMEM] * 2,
         compiler_params=pltpu.CompilerParams(vmem_limit_bytes=8 << 20),
         cost_estimate=pl.CostEstimate(flops=500_000, bytes_accessed=600_000, transcendentals=0),
         name="final",
-    )(parts, corner, near, unit, frac, drive)
+    )(parts, corner, near, unit, frac)
     return forces.reshape(3, 1, 1, 1, -1), virial.reshape(6, 1, 1, 1, -1)
 
 

time: 68.7 us -> 69.7 us (1.015)
  Pallas kernels: 14 us -> 14.9 us
    pallas_call x1, Pallas kernels: 4.59 us -> 5.45 us  [shards(): pl.pallas_call(near_kernel, out_shape=(f32(LANES, TP), f32(3, HALF, LANES...]
  transfers between devices with their start and end apart: 8 -> 8, of which waited for: 1 -> 1; matrix products, arithmetic and copies ran while one was open for 0% -> 0% of each run, Pallas kernels for 14% -> 15%
where the time goes in v8:
time: 69.7 us; the launch traced here: 69.2 us
  starting transfers between devices  52.2 us (75%)
  Pallas kernels  14.9 us (21%)
  between operations  1.43 us (2%)
  waiting for transfers between devices  0.75 us (1%)
    ppermute x6, starting transfers between devices, exchanged(): lax.ppermute(value, axis, [(i, (i + (1 if (i + far) % 2 == 0 else -1)) %...  32.8 us
    all_to_all x1, starting transfers between devices, shards(): column = lax.all_to_all(coarse, 'gz', 0, 0, tiled=True)  16.1 us
    pallas_call x1, Pallas kernels, shards(): pl.pallas_call(near_kernel, out_shape=(f32(LANES, TP), f32(3, HALF, LANES...  5.45 us
    pallas_call x1, Pallas kernels, shards(): pl.pallas_call(spread_kernel, out_shape=(bf16(GRID_ROWS, TP), f32(lines,...  3.96 us
    pallas_call x1, Pallas kernels, shards(): pl.pallas_call(far_kernel, out_shape=f32(3, HALF, LANES), in_specs=[VMEM]...  3.62 us
    all_to_all x1, starting transfers between devices, shards(): parts = lax.all_to_all(parts, ('cx', 'gy'), 0, 0, tiled=True)  3.26 us
  transfers between devices with their start and end apart: 8, of which 1 were waited for; matrix products, arithmetic and copies ran while one was open for 0% of the time, Pallas kernels for 15%

profile of v8, /device:TPU:1, one launch (start us, length us, event | category | flops | bytes accessed | tf_op | source)
XLA Modules:
  0.0 69.2 jit_solution(5596863409277328058)
XLA Ops:
  1.3 4.0 %spread.1 = (bf16[256,512]{1,0:T(8,128)(2,1)S(1)}, f32[32,1,128]{2,1,0:T(1,128)}, f32[3,64,128]{2,1,0:T(8,128)S(1)}, f32[8,128]{1,0:T(8,128)S(1)}, f32[3,64,128]...) custom-call(s32[1,1]{1,0:T(1,128)} %bitcast.7.live_ref, ...), custom_call_target="tpu_custom_call" | custom-call | flops 10000000 | bytes 1000000 | tf_op jit(solution)/shard_map/spread/pallas_call | solution.py:376
  5.2 16.1 %all-to-all-start = ((f32[32,1,128]{2,1,0:T(1,128)}), f32[32,1,128]{2,1,0:T(1,128)S(1)}, u32[]{:S(2)}, u32[]{:S(2)}) async-start(f32[32,1,128]{2,1,0:T(1,128)} %get-tuple-element.26), calls=%async_computation | async-start | bytes 32768 | tf_op jit(solution)/shard_map/all_to_all | solution.py:397
  21.4 0.2 faces.1
  21.6 2.9 %collective-permute-start.1 = (bf16[48,512]{1,0:T(8,128)(2,1)S(1)}, bf16[48,512]{1,0:T(8,128)(2,1)S(1)}, u32[]{:S(2)}, u32[]{:S(2)}) collective-permute-start(bf16[48,512]{1,0:T(8,128)(2,1)S(1)} %get-tuple-element.34), channel_id=1, source_target_pairs={{0,128},{128,0},{256,384},{384,256},{1,129},{129,1},{257,385},{385... | collective-permute-start | bytes 147464 | tf_op jit(solution)/shard_map/ppermute | solution.py:365
  24.5 3.1 %collective-permute-start.2 = (bf16[48,512]{1,0:T(8,128)(2,1)S(1)}, bf16[48,512]{1,0:T(8,128)(2,1)S(1)}, u32[]{:S(2)}, u32[]{:S(2)}) collective-permute-start(bf16[48,512]{1,0:T(8,128)(2,1)S(1)} %get-tuple-element.35), channel_id=1, source_target_pairs={{0,32},{32,0},{64,96},{96,64},{1,33},{33,1},{65,97},{97,65},{2,34}... | collective-permute-start | bytes 147464 | tf_op jit(solution)/shard_map/ppermute | solution.py:365
  27.6 3.4 %collective-permute-start.3 = (bf16[48,512]{1,0:T(8,128)(2,1)S(1)}, bf16[48,512]{1,0:T(8,128)(2,1)S(1)}, u32[]{:S(2)}, u32[]{:S(2)}) collective-permute-start(bf16[48,512]{1,0:T(8,128)(2,1)S(1)} %get-tuple-element.36), channel_id=1, source_target_pairs={{0,1},{1,0},{2,3},{3,2},{4,5},{5,4},{6,7},{7,6},{8,9},{9,8},{10,11... | collective-permute-start | bytes 147464 | tf_op jit(solution)/shard_map/ppermute | solution.py:365
  31.0 11.0 %collective-permute-start.4 = (bf16[48,512]{1,0:T(8,128)(2,1)S(1)}, bf16[48,512]{1,0:T(8,128)(2,1)S(1)}, u32[]{:S(2)}, u32[]{:S(2)}) collective-permute-start(bf16[48,512]{1,0:T(8,128)(2,1)S(1)} %get-tuple-element.37), channel_id=1, source_target_pairs={{0,31},{1,2},{2,1},{3,4},{4,3},{5,6},{6,5},{7,8},{8,7},{9,10},{10,... | collective-permute-start | bytes 147464 | tf_op jit(solution)/shard_map/ppermute | solution.py:365
  42.0 0.0 all-to-all-done.column_ref
  42.0 0.1 coarse.1
  42.2 8.7 %collective-permute-start = (bf16[40,512]{1,0:T(8,128)(2,1)S(1)}, bf16[40,512]{1,0:T(8,128)(2,1)S(1)}, u32[]{:S(2)}, u32[]{:S(2)}) collective-permute-start(bf16[40,512]{1,0:T(8,128)(2,1)S(1)} %get-tuple-element.32), channel_id=1, source_target_pairs={{0,384},{128,256},{256,128},{384,0},{1,385},{129,257},{257,129},{3... | collective-permute-start | bytes 122888 | tf_op jit(solution)/shard_map/ppermute | solution.py:365
  50.9 0.0 collective-permute-done.1.near_x_ref
  50.9 3.7 %collective-permute-start.5 = (bf16[36,512]{1,0:T(8,128)(2,1)S(1)}, bf16[36,512]{1,0:T(8,128)(2,1)S(1)}, u32[]{:S(2)}, u32[]{:S(2)}) collective-permute-start(bf16[36,512]{1,0:T(8,128)(2,1)S(1)} %get-tuple-element.45), channel_id=1, source_target_pairs={{0,96},{32,64},{64,32},{96,0},{1,97},{33,65},{65,33},{97,1},{2,98}... | collective-permute-start | bytes 110600 | tf_op jit(solution)/shard_map/ppermute | solution.py:365
  54.6 0.0 collective-permute-done.2.near_y_ref
  54.6 0.0 collective-permute-done.3.near_z_ref
  54.6 0.0 collective-permute-done.4.far_z_ref
  54.6 5.4 %near.1 = (f32[128,512]{1,0:T(8,128)S(1)}, f32[3,64,128]{2,1,0:T(8,128)S(1)}) custom-call(f32[8,128]{1,0:T(8,128)S(1)} %get-tuple-element.33.tiles_ref, bf16[256,512]{1,0:T(8,128)(2,1)S(1)} %get-tuple-element.28.grid_ref, bf16[48,512]{1,0:T(8,128)(2,1)S(1)} %collective-permute-done.1.near_x_ref, bf16[48,512]{1,0:T(8,128)(2,1)S(1)} %collective-permute-done.2.near_y_ref, ...), custom_call_target="tpu_custom_call" | custom-call | flops 1000 | bytes 1000 | tf_op jit(solution)/shard_map/near/pallas_call | solution.py:425
  60.1 0.0 collective-permute-done.far_ref.far_x_ref
  60.1 0.7 merge.1
  60.8 3.3 %all-to-all-start.1 = ((f32[8,1,128]{2,1,0:T(1,128)}), f32[8,1,128]{2,1,0:T(1,128)S(1)}, u32[]{:S(2)}, u32[]{:S(2)}) async-start(f32[8,1,128]{2,1,0:T(1,128)} %merge.1), calls=%async_computation.1 | async-start | bytes 8192 | tf_op jit(solution)/shard_map/all_to_all | solution.py:448
  64.0 0.0 collective-permute-done.5.far_y_ref
  64.1 3.6 %far.1.near_ref = f32[3,64,128]{2,1,0:T(8,128)S(1)} custom-call(f32[8,128]{1,0:T(8,128)S(1)} %get-tuple-element.33.tiles_ref, f32[128,512]{1,0:T(8,128)S(1)} %get-tuple-element.43.field_any.part_ref, bf16[40,512]{1,0:T(8,128)(2,1)S(1)} %collective-permute-done.far_ref.far_x_ref, bf16[36,512]{1,0:T(8,128)(2,1)S(1)} %collective-permute-done.5.far_y_ref, ...), custom_call_target="tpu_custom_call" | custom-call | flops 1000000000 | bytes 4000000 | tf_op jit(solution)/shard_map/far/pallas_call | solution.py:450
  67.7 0.7 %all-to-all-done.1.parts_ref = f32[8,1,128]{2,1,0:T(1,128)S(1)} async-done(((f32[8,1,128]{2,1,0:T(1,128)}), f32[8,1,128]{2,1,0:T(1,128)S(1)}, u32[]{:S(2)}, u32[]{:S(2)}) %all-to-all-start.1) | async-done | bytes 4128 | tf_op jit(solution)/shard_map/all_to_all | solution.py:448
  68.4 0.8 %final.1 = (f32[3,64,128]{2,1,0:T(8,128)}, f32[6,64,128]{2,1,0:T(8,128)}) custom-call(f32[8,1,128]{2,1,0:T(1,128)S(1)} %all-to-all-done.1.parts_ref, s32[64,128]{1,0:T(8,128)S(1)} %get-tuple-element.44.corner_ref, f32[3,64,128]{2,1,0:T(8,128)S(1)} %far.1.near_ref, f32[3,64,128]{2,1,0:T(8,128)S(1)} %get-tuple-element.46.unit_ref, ...), custom_call_target="tpu_custom_call" | custom-call | flops 500000 | bytes 600000 | tf_op jit(solution)/shard_map/final/pallas_call | solution.py:465
Async XLA Ops:
  5.2 36.8 %all-to-all-start = ((f32[32,1,128]{2,1,0:T(1,128)}), f32[32,1,128]{2,1,0:T(1,128)S(1)}, u32[]{:S(2)}, u32[]{:S(2)}) async-start(f32[32,1,128]{2,1,0:T(1,128)} %get-tuple-element.26), calls=%async_computation | async-start | bytes 32768 | tf_op jit(solution)/shard_map/all_to_all | solution.py:397
  21.6 29.3 %collective-permute-start.1 = (bf16[48,512]{1,0:T(8,128)(2,1)S(1)}, bf16[48,512]{1,0:T(8,128)(2,1)S(1)}, u32[]{:S(2)}, u32[]{:S(2)}) collective-permute-start(bf16[48,512]{1,0:T(8,128)(2,1)S(1)} %get-tuple-element.34), channel_id=1, source_target_pairs={{0,128},{128,0},{256,384},{384,256},{1,129},{129,1},{257,385},{385... | collective-permute-start | bytes 147464 | tf_op jit(solution)/shard_map/ppermute | solution.py:365
  24.5 30.1 %collective-permute-start.2 = (bf16[48,512]{1,0:T(8,128)(2,1)S(1)}, bf16[48,512]{1,0:T(8,128)(2,1)S(1)}, u32[]{:S(2)}, u32[]{:S(2)}) collective-permute-start(bf16[48,512]{1,0:T(8,128)(2,1)S(1)} %get-tuple-element.35), channel_id=1, source_target_pairs={{0,32},{32,0},{64,96},{96,64},{1,33},{33,1},{65,97},{97,65},{2,34}... | collective-permute-start | bytes 147464 | tf_op jit(solution)/shard_map/ppermute | solution.py:365
  27.6 27.0 %collective-permute-start.3 = (bf16[48,512]{1,0:T(8,128)(2,1)S(1)}, bf16[48,512]{1,0:T(8,128)(2,1)S(1)}, u32[]{:S(2)}, u32[]{:S(2)}) collective-permute-start(bf16[48,512]{1,0:T(8,128)(2,1)S(1)} %get-tuple-element.36), channel_id=1, source_target_pairs={{0,1},{1,0},{2,3},{3,2},{4,5},{5,4},{6,7},{7,6},{8,9},{9,8},{10,11... | collective-permute-start | bytes 147464 | tf_op jit(solution)/shard_map/ppermute | solution.py:365
  31.0 23.6 %collective-permute-start.4 = (bf16[48,512]{1,0:T(8,128)(2,1)S(1)}, bf16[48,512]{1,0:T(8,128)(2,1)S(1)}, u32[]{:S(2)}, u32[]{:S(2)}) collective-permute-start(bf16[48,512]{1,0:T(8,128)(2,1)S(1)} %get-tuple-element.37), channel_id=1, source_target_pairs={{0,31},{1,2},{2,1},{3,4},{4,3},{5,6},{6,5},{7,8},{8,7},{9,10},{10,... | collective-permute-start | bytes 147464 | tf_op jit(solution)/shard_map/ppermute | solution.py:365
  42.2 17.9 %collective-permute-start = (bf16[40,512]{1,0:T(8,128)(2,1)S(1)}, bf16[40,512]{1,0:T(8,128)(2,1)S(1)}, u32[]{:S(2)}, u32[]{:S(2)}) collective-permute-start(bf16[40,512]{1,0:T(8,128)(2,1)S(1)} %get-tuple-element.32), channel_id=1, source_target_pairs={{0,384},{128,256},{256,128},{384,0},{1,385},{129,257},{257,129},{3... | collective-permute-start | bytes 122888 | tf_op jit(solution)/shard_map/ppermute | solution.py:365
  50.9 13.2 %collective-permute-start.5 = (bf16[36,512]{1,0:T(8,128)(2,1)S(1)}, bf16[36,512]{1,0:T(8,128)(2,1)S(1)}, u32[]{:S(2)}, u32[]{:S(2)}) collective-permute-start(bf16[36,512]{1,0:T(8,128)(2,1)S(1)} %get-tuple-element.45), channel_id=1, source_target_pairs={{0,96},{32,64},{64,32},{96,0},{1,97},{33,65},{65,33},{97,1},{2,98}... | collective-permute-start | bytes 110600 | tf_op jit(solution)/shard_map/ppermute | solution.py:365
  60.8 7.6 %all-to-all-start.1 = ((f32[8,1,128]{2,1,0:T(1,128)}), f32[8,1,128]{2,1,0:T(1,128)S(1)}, u32[]{:S(2)}, u32[]{:S(2)}) async-start(f32[8,1,128]{2,1,0:T(1,128)} %merge.1), calls=%async_computation.1 | async-start | bytes 8192 | tf_op jit(solution)/shard_map/all_to_all | solution.py:448

commit v9 on v7

--- a/solution.py
+++ b/solution.py
@@ -148,23 +148,24 @@
     return lax.axis_index("cx" if axis == "gx" else axis) & 1
 
 
-def face_kernel(grid_ref, near_x_ref, far_x_ref, near_y_ref, far_y_ref, near_z_ref, far_z_ref):
+def face_kernel(grid_ref, near_x_ref, far_x_ref, near_z_ref, far_z_ref, y_ref):
     row = iota((FACE, GRID_ROWS), 0)
     line = (row * 10923) >> 16
-    ids = []
-    for axis, (first, step) in zip(
-        ("gx", "gy", "gz"), ((row, 180), (line * 36 + (row - line * TD), 30), (row * TD, 5)), strict=True
-    ):
-        side = odd(axis)
-        ids += [first + step * (1 - side), first + step * side]
+    side_x, side_z = odd("gx"), odd("gz")
+    low_y = line * 36 + (row - line * TD)
+    ids = [row + 180 * (1 - side_x), row + 180 * side_x, row * TD + 5 * (1 - side_z), row * TD + 5 * side_z, low_y, low_y + 30]
     tile = jnp.where(jnp.concatenate([row] * 6, axis=0) < TD * TD, jnp.concatenate(ids, axis=0), -1)
     hot = (iota((6 * FACE, GRID_ROWS), 1) == tile).astype(jnp.bfloat16)
     faces = jnp.dot(hot, grid_ref[...], preferred_element_type=jnp.float32).astype(jnp.bfloat16)
-    for at, ref in enumerate((near_x_ref, far_x_ref, near_y_ref, far_y_ref, near_z_ref, far_z_ref)):
+    for at, ref in enumerate((near_x_ref, far_x_ref, near_z_ref, far_z_ref)):
         ref[...] = faces[at * FACE : (at + 1) * FACE]
-
-
-def coarse_kernel(column_ref, top_ref, face_ref, face_y_ref, own_ref, send_ref, pass_ref):
+    me, count = lax.axis_index("gy"), lax.axis_size("gy")
+    for step in range(count):
+        high = step == 1
+        y_ref[lax.rem(me + step, count)] = faces[(5 if high else 4) * FACE : (6 if high else 5) * FACE]
+
+
+def coarse_kernel(column_ref, top_ref, face_ref, own_ref, send_ref):
     lines = column_ref.shape[0]
     column = column_ref[...].reshape(lines, LANES)
     column = jnp.concatenate([column] * (lines * 8 // LANES), axis=1)
@@ -186,7 +187,10 @@
     sums = jnp.concatenate(parts + [jnp.zeros((1, LANES), jnp.float32)], axis=1)
     rows = face_ref[...].astype(jnp.float32)[:FAR_ROWS]
     send_ref[...] = jnp.where(iota((FAR_ROWS, TP), 0) == TD * TD, sums, rows).astype(jnp.bfloat16)
-    pass_ref[...] = face_y_ref[...].astype(jnp.float32)[: pass_ref.shape[0]].astype(jnp.bfloat16)
+
+
+def gate_kernel(face_ref, *rest):
+    rest[-1][...] = face_ref[...]
 
 
 def merge_kernel(own_ref, far_ref, field_any, out_ref):
@@ -230,24 +234,24 @@
 
 
 def near_kernel(
-    tiles_ref, grid_ref, near_x_ref, near_y_ref, near_z_ref, far_z_ref, blocks_ref, coord_ref, weights_ref,
+    tiles_ref, grid_ref, near_x_ref, near_z_ref, far_z_ref, blocks_ref, coord_ref, weights_ref,
     field_ref, unit_ref,
     ext_ref, flat_ref, grad_ref,
 ):
     ext_ref[0:GRID_ROWS] = grid_ref[...]
-    for at, ref in enumerate((near_x_ref, near_y_ref, near_z_ref, far_z_ref)):
+    for at, ref in enumerate((near_x_ref, near_z_ref, far_z_ref)):
         ext_ref[GRID_ROWS + at * FACE : GRID_ROWS + (at + 1) * FACE] = ref[...]
-    nothing = GRID_ROWS + 4 * FACE
+    nothing = GRID_ROWS + 3 * FACE
     ext_ref[nothing:] = jnp.zeros((EXT_ROWS - nothing, TP), jnp.bfloat16)
 
     tile = tile_column(tiles_ref)
     tx, ty, tz = tile_coords(tile)
-    row_x, row_y, row_z = ty * TD + tz, tx * TD + tz, tx * TD + ty
+    row_x, row_z = ty * TD + tz, tx * TD + ty
     base = GRID_ROWS
     edges = (
         ("gx", tx, 36, base + row_x, nothing + 0 * row_x),
-        ("gy", ty, TD, base + FACE + row_y, nothing + 0 * row_y),
-        ("gz", tz, 1, base + 2 * FACE + row_z, base + 3 * FACE + row_z),
+        ("gy", ty, TD, nothing + 0 * row_x, nothing + 0 * row_x),
+        ("gz", tz, 1, base + FACE + row_z, base + 2 * FACE + row_z),
     )
     targets = [tile]
     for axis, place, stride, near, far in edges:
@@ -285,26 +289,33 @@
 
 
 def far_kernel(
-    tiles_ref, part_ref, far_x_ref, far_y_ref, block_ref, coord_ref,
+    tiles_ref, part_ref, far_x_ref, y_ref, block_ref, coord_ref,
     near_ref,
     sum_ref, field_ref, grad_ref,
 ):
     tx, ty, tz = tile_coords(tile_column(tiles_ref))
-    sum_ref[...] = part_ref[...]
-    for axis, ref, place, row, block in (("gx", far_x_ref, tx, ty * TD + tz, 1), ("gy", far_y_ref, ty, tx * TD + tz, 2)):
-        own_side = odd(axis)
-        target = jnp.where(place == (TD - 1) * own_side, row, -1)
+
+    def picked(face, target):
         hot = (iota((LANES, FACE), 1) == target).astype(jnp.bfloat16)
-        rest = jnp.zeros((FACE - ref.shape[0], TP), jnp.float32)
-        face = jnp.concatenate([ref[...].astype(jnp.float32), rest], axis=0).astype(jnp.bfloat16)
-        rows = jnp.dot(hot, face, preferred_element_type=jnp.float32).astype(jnp.bfloat16)
-        for side in range(2):
-
-            @pl.when(own_side == side)
-            def _(side=side, rows=rows, block=block):
-                sum_ref[...] += lax.dot_general(
-                    rows, block_ref[block], (((1,), (side,)), ((), ())), preferred_element_type=jnp.float32
-                )
+        return jnp.dot(hot, face, preferred_element_type=jnp.float32).astype(jnp.bfloat16)
+
+    def term(rows, block, up):
+        return lax.dot_general(rows, block_ref[block], (((1,), (up,)), ((), ())), preferred_element_type=jnp.float32)
+
+    me, count = lax.axis_index("gy"), lax.axis_size("gy")
+    row = tx * TD + tz
+    above = picked(y_ref[lax.rem(me + 1, count)], jnp.where(ty == TD - 1, row, -1))
+    below = picked(y_ref[lax.rem(me + count - 1, count)], jnp.where(ty == 0, row, -1))
+    field = part_ref[...] + term(above, 2, 1) + term(below, 2, 0)
+    core = odd("gx")
+    rest = jnp.zeros((FACE - FAR_ROWS, TP), jnp.float32)
+    face = jnp.concatenate([far_x_ref[...].astype(jnp.float32), rest], axis=0).astype(jnp.bfloat16)
+    rows = picked(face, jnp.where(tx == (TD - 1) * core, ty * TD + tz, -1))
+    for side in range(2):
+
+        @pl.when(core == side)
+        def _(side=side):
+            sum_ref[...] = field + term(rows, 1, side)
 
     for part in range(TP // LANES):
         field_ref[part * LANES : (part + 1) * LANES, :] = sum_ref[:, part * LANES : (part + 1) * LANES].T
@@ -379,43 +390,51 @@
 
     faces = pl.pallas_call(
         face_kernel,
-        out_shape=(bf16(FACE, TP),) * 6,
+        out_shape=(bf16(FACE, TP),) * 4 + (bf16(lax.axis_size("gy"), FACE, TP),),
         in_specs=[VMEM],
-        out_specs=[VMEM] * 6,
+        out_specs=[VMEM] * 5,
         compiler_params=pltpu.CompilerParams(vmem_limit_bytes=8 << 20),
         cost_estimate=pl.CostEstimate(flops=80_000_000, bytes_accessed=600_000, transcendentals=0),
         name="faces",
     )(grid)
-    near_x, far_x, near_y, far_y, near_z, far_z = faces
+    near_x, far_x, near_z, far_z, face_y = faces
     far_z, near_z = exchanged(far_z, "gz", 1), exchanged(near_z, "gz", 0)
     near_x = exchanged(near_x, ("hx", "cx"), 0)
-    near_y = exchanged(near_y, "gy", 0)
-
-    own, far_x, far_y = pl.pallas_call(
+
+    own, far_x = pl.pallas_call(
         coarse_kernel,
-        out_shape=(f32(1, LANES), bf16(FAR_ROWS, TP), bf16(36, TP)),
-        in_specs=[VMEM] * 4,
-        out_specs=[VMEM] * 3,
+        out_shape=(f32(1, LANES), bf16(FAR_ROWS, TP)),
+        in_specs=[VMEM] * 3,
+        out_specs=[VMEM] * 2,
         compiler_params=pltpu.CompilerParams(vmem_limit_bytes=8 << 20),
         cost_estimate=pl.CostEstimate(flops=70_000, bytes_accessed=200_000, transcendentals=0),
         name="coarse",
-    )(column, top, far_x, far_y)
+    )(column, top, far_x)
     far_x = exchanged(far_x, ("hx", "cx"), 1)
-    far_y = exchanged(far_y, "gy", 1)
+    face_y = pl.pallas_call(
+        gate_kernel,
+        out_shape=bf16(*face_y.shape),
+        in_specs=[VMEM] + [ANY] * 3,
+        out_specs=VMEM,
+        compiler_params=pltpu.CompilerParams(vmem_limit_bytes=4 << 20),
+        cost_estimate=pl.CostEstimate(flops=1000, bytes_accessed=1000, transcendentals=0),
+        name="gate",
+    )(face_y, own, near_x, near_z)
+    face_y = lax.all_to_all(face_y, "gy", 0, 0, tiled=True)
 
     field, unit = pl.pallas_call(
         near_kernel,
         out_shape=(f32(LANES, TP), f32(3, HALF, LANES)),
-        in_specs=[VMEM] * 9,
+        in_specs=[VMEM] * 8,
         out_specs=[VMEM] * 2,
         scratch_shapes=[
             pltpu.VMEM((EXT_ROWS, TP), jnp.bfloat16), pltpu.VMEM((TP, LANES), jnp.float32),
             pltpu.VMEM((3, CS, LANES), jnp.float32),
         ],
         compiler_params=pltpu.CompilerParams(vmem_limit_bytes=16 << 20),
-        cost_estimate=pl.CostEstimate(flops=1000, bytes_accessed=1000, transcendentals=0),
+        cost_estimate=pl.CostEstimate(flops=20_000_000_000, bytes_accessed=1000, transcendentals=0),
         name="near",
-    )(tiles, grid, near_x, near_y, near_z, far_z, blocks, coords, weights)
+    )(tiles, grid, near_x, near_z, far_z, blocks, coords, weights)
 
     parts = pl.pallas_call(
         merge_kernel,
@@ -440,7 +459,7 @@
         compiler_params=pltpu.CompilerParams(vmem_limit_bytes=16 << 20),
         cost_estimate=pl.CostEstimate(flops=1_000_000_000, bytes_accessed=4_000_000, transcendentals=200_000),
         name="far",
-    )(tiles, field, far_x, far_y, blocks, coords)
+    )(tiles, field, far_x, face_y, blocks, coords)
 
     forces, virial = pl.pallas_call(
         final_kernel,

time: 68.7 us -> 68.2 us (level)
  starting transfers between devices: 52.2 us -> 50.5 us
    ppermute x6 -> x4, starting transfers between devices: 32.8 us -> 25.7 us  [exchanged(): lax.ppermute(value, axis, [(i, (i + (1 if (i + far) % 2 == 0 else -1)) %...]
    all_to_all x0 -> x1, starting transfers between devices: none -> 4.01 us  [shards(): face_y = lax.all_to_all(face_y, 'gy', 0, 0, tiled=True)]
    all_to_all x1, starting transfers between devices: 3.26 us -> 4.68 us  [shards(): parts = lax.all_to_all(parts, ('cx', 'gy'), 0, 0, tiled=True)]
    pallas_call x1 -> x2, Pallas kernels: 0.24 us -> 0.93 us  [the longest x1 0.69 us: shards(): pl.pallas_call(gate_kernel, out_shape=bf16(*face_y.shape), in_specs=[VMEM...]
  transfers between devices with their start and end apart: 8 -> 7, of which waited for: 1 -> 2; matrix products, arithmetic and copies ran while one was open for 0% -> 0% of each run, Pallas kernels for 14% -> 14%
where the time goes in v9:
time: 68.2 us; the launch traced here: 67.8 us
  starting transfers between devices  50.5 us (74%)
  Pallas kernels  14.6 us (21%)
  between operations  1.38 us (2%)
  waiting for transfers between devices  1.35 us (2%)
    ppermute x4, starting transfers between devices, exchanged(): lax.ppermute(value, axis, [(i, (i + (1 if (i + far) % 2 == 0 else -1)) %...  25.7 us
    all_to_all x1, starting transfers between devices, shards(): column = lax.all_to_all(coarse, 'gz', 0, 0, tiled=True)  16.1 us
    all_to_all x1, starting transfers between devices, shards(): parts = lax.all_to_all(parts, ('cx', 'gy'), 0, 0, tiled=True)  4.68 us
    pallas_call x1, Pallas kernels, shards(): pl.pallas_call(near_kernel, out_shape=(f32(LANES, TP), f32(3, HALF, LANES...  4.57 us
    all_to_all x1, starting transfers between devices, shards(): face_y = lax.all_to_all(face_y, 'gy', 0, 0, tiled=True)  4.01 us
    pallas_call x1, Pallas kernels, shards(): pl.pallas_call(spread_kernel, out_shape=(bf16(GRID_ROWS, TP), f32(lines,...  3.94 us
    pallas_call x1, Pallas kernels, shards(): pl.pallas_call(far_kernel, out_shape=f32(3, HALF, LANES), in_specs=[VMEM]...  3.48 us
  transfers between devices with their start and end apart: 7, of which 2 were waited for; matrix products, arithmetic and copies ran while one was open for 0% of the time, Pallas kernels for 14%

profile of v9, /device:TPU:1, one launch (start us, length us, event | category | flops | bytes accessed | tf_op | source)
XLA Modules:
  0.0 67.8 jit_solution(5970925714366450587)
XLA Ops:
  1.3 3.9 %spread.1 = (bf16[256,512]{1,0:T(8,128)(2,1)S(1)}, f32[32,1,128]{2,1,0:T(1,128)}, f32[3,64,128]{2,1,0:T(8,128)S(1)}, f32[8,128]{1,0:T(8,128)S(1)}, f32[64,128]{1...) custom-call(s32[1,1]{1,0:T(1,128)} %bitcast.7.live_ref, ...), custom_call_target="tpu_custom_call" | custom-call | flops 10000000 | bytes 1000000 | tf_op jit(solution)/shard_map/spread/pallas_call | solution.py:369
  5.2 16.1 %all-to-all-start = ((f32[32,1,128]{2,1,0:T(1,128)}), f32[32,1,128]{2,1,0:T(1,128)S(1)}, u32[]{:S(2)}, u32[]{:S(2)}) async-start(f32[32,1,128]{2,1,0:T(1,128)} %get-tuple-element.23), calls=%async_computation | async-start | bytes 32768 | tf_op jit(solution)/shard_map/all_to_all | solution.py:389
  21.3 0.2 faces.1
  21.6 2.9 %collective-permute-start.1 = (bf16[48,512]{1,0:T(8,128)(2,1)S(1)}, bf16[48,512]{1,0:T(8,128)(2,1)S(1)}, u32[]{:S(2)}, u32[]{:S(2)}) collective-permute-start(bf16[48,512]{1,0:T(8,128)(2,1)S(1)} %get-tuple-element.30), channel_id=1, source_target_pairs={{0,128},{128,0},{256,384},{384,256},{1,129},{129,1},{257,385},{385... | collective-permute-start | bytes 147464 | tf_op jit(solution)/shard_map/ppermute | solution.py:358
  24.5 3.4 %collective-permute-start.2 = (bf16[48,512]{1,0:T(8,128)(2,1)S(1)}, bf16[48,512]{1,0:T(8,128)(2,1)S(1)}, u32[]{:S(2)}, u32[]{:S(2)}) collective-permute-start(bf16[48,512]{1,0:T(8,128)(2,1)S(1)} %get-tuple-element.31), channel_id=1, source_target_pairs={{0,1},{1,0},{2,3},{3,2},{4,5},{5,4},{6,7},{7,6},{8,9},{9,8},{10,11... | collective-permute-start | bytes 147464 | tf_op jit(solution)/shard_map/ppermute | solution.py:358
  27.9 11.0 %collective-permute-start.3 = (bf16[48,512]{1,0:T(8,128)(2,1)S(1)}, bf16[48,512]{1,0:T(8,128)(2,1)S(1)}, u32[]{:S(2)}, u32[]{:S(2)}) collective-permute-start(bf16[48,512]{1,0:T(8,128)(2,1)S(1)} %get-tuple-element.32), channel_id=1, source_target_pairs={{0,31},{1,2},{2,1},{3,4},{4,3},{5,6},{6,5},{7,8},{8,7},{9,10},{10,... | collective-permute-start | bytes 147464 | tf_op jit(solution)/shard_map/ppermute | solution.py:358
  38.9 0.0 all-to-all-done.column_ref
  38.9 0.1 coarse.1
  39.0 8.4 %collective-permute-start = (bf16[40,512]{1,0:T(8,128)(2,1)S(1)}, bf16[40,512]{1,0:T(8,128)(2,1)S(1)}, u32[]{:S(2)}, u32[]{:S(2)}) collective-permute-start(bf16[40,512]{1,0:T(8,128)(2,1)S(1)} %get-tuple-element.28), channel_id=1, source_target_pairs={{0,384},{128,256},{256,128},{384,0},{1,385},{129,257},{257,129},{3... | collective-permute-start | bytes 122888 | tf_op jit(solution)/shard_map/ppermute | solution.py:358
  47.4 0.0 collective-permute-done.1.near_x_ref.rest_1_
  47.5 0.0 collective-permute-done.2.near_z_ref.rest_2_
  47.5 0.7 %gate.1 = bf16[4,48,512]{2,1,0:T(8,128)(2,1)} custom-call(bf16[4,48,512]{2,1,0:T(8,128)(2,1)S(1)} %get-tuple-element.38.face_ref, f32[1,128]{1,0:T(1,128)S(1)} %get-tuple-element.27.own_ref.rest_0_, bf16[48,512]{1,0:T(8,128)(2,1)S(1)} %collective-permute-done.1.near_x_ref.rest_1_, bf16[48,512]{1,0:T(8,128)(2,1)S(1)} %collective-permute-done.2.near_z_ref.rest_2_), custom_call_target="tpu_custom_call" | custom-call | flops 1000 | bytes 1000 | tf_op jit(solution)/shard_map/gate/pallas_call | solution.py:414
  48.2 4.0 %all-to-all-start.2 = ((bf16[4,48,512]{2,1,0:T(8,128)(2,1)}), bf16[4,48,512]{2,1,0:T(8,128)(2,1)S(1)}, u32[]{:S(2)}, u32[]{:S(2)}) async-start(bf16[4,48,512]{2,1,0:T(8,128)(2,1)} %gate.1), calls=%async_computation.2 | async-start | bytes 393216 | tf_op jit(solution)/shard_map/all_to_all | solution.py:423
  52.2 0.0 collective-permute-done.3.far_z_ref
  52.2 4.6 %near.1 = (f32[128,512]{1,0:T(8,128)S(1)}, f32[3,64,128]{2,1,0:T(8,128)S(1)}) custom-call(f32[8,128]{1,0:T(8,128)S(1)} %get-tuple-element.29.tiles_ref, bf16[256,512]{1,0:T(8,128)(2,1)S(1)} %get-tuple-element.25.grid_ref, bf16[48,512]{1,0:T(8,128)(2,1)S(1)} %collective-permute-done.1.near_x_ref.rest_1_, ...), custom_call_target="tpu_custom_call" | custom-call | flops 20000000000 | bytes 1000 | tf_op jit(solution)/shard_map/near/pallas_call | solution.py:425
  56.7 0.0 collective-permute-done.far_ref.far_x_ref
  56.8 0.7 merge.1
  57.4 0.3 all-to-all-done.2.y_ref
  57.8 4.7 %all-to-all-start.1 = ((f32[8,1,128]{2,1,0:T(1,128)}), f32[8,1,128]{2,1,0:T(1,128)S(1)}, u32[]{:S(2)}, u32[]{:S(2)}) async-start(f32[8,1,128]{2,1,0:T(1,128)} %merge.1), calls=%async_computation.1 | async-start | bytes 8192 | tf_op jit(solution)/shard_map/all_to_all | solution.py:448
  62.5 3.5 %far.1.near_ref = f32[3,64,128]{2,1,0:T(8,128)S(1)} custom-call(f32[8,128]{1,0:T(8,128)S(1)} %get-tuple-element.29.tiles_ref, f32[128,512]{1,0:T(8,128)S(1)} %get-tuple-element.36.field_any.part_ref, bf16[40,512]{1,0:T(8,128)(2,1)S(1)} %collective-permute-done.far_ref.far_x_ref, bf16[4,48,512]{2,1,0:T(8,128)(2,1)S(1)} %all-to-all-done.2.y_ref, ...), custom_call_target="tpu_custom_call" | custom-call | flops 1000000000 | bytes 4000000 | tf_op jit(solution)/shard_map/far/pallas_call | solution.py:450
  65.9 1.0 %all-to-all-done.1.parts_ref = f32[8,1,128]{2,1,0:T(1,128)S(1)} async-done(((f32[8,1,128]{2,1,0:T(1,128)}), f32[8,1,128]{2,1,0:T(1,128)S(1)}, u32[]{:S(2)}, u32[]{:S(2)}) %all-to-all-start.1) | async-done | bytes 4128 | tf_op jit(solution)/shard_map/all_to_all | solution.py:448
  66.9 0.8 %final.1 = (f32[3,64,128]{2,1,0:T(8,128)}, f32[6,64,128]{2,1,0:T(8,128)}) custom-call(f32[8,1,128]{2,1,0:T(1,128)S(1)} %all-to-all-done.1.parts_ref, s32[64,128]{1,0:T(8,128)S(1)} %get-tuple-element.37.corner_ref, f32[3,64,128]{2,1,0:T(8,128)S(1)} %far.1.near_ref, f32[3,64,128]{2,1,0:T(8,128)S(1)} %get-tuple-element.39.unit_ref, ...), custom_call_target="tpu_custom_call" | custom-call | flops 500000 | bytes 600000 | tf_op jit(solution)/shard_map/final/pallas_call | solution.py:464
Async XLA Ops:
  5.2 33.7 %all-to-all-start = ((f32[32,1,128]{2,1,0:T(1,128)}), f32[32,1,128]{2,1,0:T(1,128)S(1)}, u32[]{:S(2)}, u32[]{:S(2)}) async-start(f32[32,1,128]{2,1,0:T(1,128)} %get-tuple-element.23), calls=%async_computation | async-start | bytes 32768 | tf_op jit(solution)/shard_map/all_to_all | solution.py:389
  21.6 25.9 %collective-permute-start.1 = (bf16[48,512]{1,0:T(8,128)(2,1)S(1)}, bf16[48,512]{1,0:T(8,128)(2,1)S(1)}, u32[]{:S(2)}, u32[]{:S(2)}) collective-permute-start(bf16[48,512]{1,0:T(8,128)(2,1)S(1)} %get-tuple-element.30), channel_id=1, source_target_pairs={{0,128},{128,0},{256,384},{384,256},{1,129},{129,1},{257,385},{385... | collective-permute-start | bytes 147464 | tf_op jit(solution)/shard_map/ppermute | solution.py:358
  24.5 23.0 %collective-permute-start.2 = (bf16[48,512]{1,0:T(8,128)(2,1)S(1)}, bf16[48,512]{1,0:T(8,128)(2,1)S(1)}, u32[]{:S(2)}, u32[]{:S(2)}) collective-permute-start(bf16[48,512]{1,0:T(8,128)(2,1)S(1)} %get-tuple-element.31), channel_id=1, source_target_pairs={{0,1},{1,0},{2,3},{3,2},{4,5},{5,4},{6,7},{7,6},{8,9},{9,8},{10,11... | collective-permute-start | bytes 147464 | tf_op jit(solution)/shard_map/ppermute | solution.py:358
  27.9 24.3 %collective-permute-start.3 = (bf16[48,512]{1,0:T(8,128)(2,1)S(1)}, bf16[48,512]{1,0:T(8,128)(2,1)S(1)}, u32[]{:S(2)}, u32[]{:S(2)}) collective-permute-start(bf16[48,512]{1,0:T(8,128)(2,1)S(1)} %get-tuple-element.32), channel_id=1, source_target_pairs={{0,31},{1,2},{2,1},{3,4},{4,3},{5,6},{6,5},{7,8},{8,7},{9,10},{10,... | collective-permute-start | bytes 147464 | tf_op jit(solution)/shard_map/ppermute | solution.py:358
  39.0 17.7 %collective-permute-start = (bf16[40,512]{1,0:T(8,128)(2,1)S(1)}, bf16[40,512]{1,0:T(8,128)(2,1)S(1)}, u32[]{:S(2)}, u32[]{:S(2)}) collective-permute-start(bf16[40,512]{1,0:T(8,128)(2,1)S(1)} %get-tuple-element.28), channel_id=1, source_target_pairs={{0,384},{128,256},{256,128},{384,0},{1,385},{129,257},{257,129},{3... | collective-permute-start | bytes 122888 | tf_op jit(solution)/shard_map/ppermute | solution.py:358
  48.2 9.6 %all-to-all-start.2 = ((bf16[4,48,512]{2,1,0:T(8,128)(2,1)}), bf16[4,48,512]{2,1,0:T(8,128)(2,1)S(1)}, u32[]{:S(2)}, u32[]{:S(2)}) async-start(bf16[4,48,512]{2,1,0:T(8,128)(2,1)} %gate.1), calls=%async_computation.2 | async-start | bytes 393216 | tf_op jit(solution)/shard_map/all_to_all | solution.py:423
  57.8 9.2 %all-to-all-start.1 = ((f32[8,1,128]{2,1,0:T(1,128)}), f32[8,1,128]{2,1,0:T(1,128)S(1)}, u32[]{:S(2)}, u32[]{:S(2)}) async-start(f32[8,1,128]{2,1,0:T(1,128)} %merge.1), calls=%async_computation.1 | async-start | bytes 8192 | tf_op jit(solution)/shard_map/all_to_all | solution.py:448

commit v10 on v9

--- a/solution.py
+++ b/solution.py
@@ -148,7 +148,7 @@
     return lax.axis_index("cx" if axis == "gx" else axis) & 1
 
 
-def face_kernel(grid_ref, near_x_ref, far_x_ref, near_z_ref, far_z_ref, y_ref):
+def face_kernel(grid_ref, near_x_ref, far_x_ref, near_z_ref, far_z_ref, y_any, y_ref, sem):
     row = iota((FACE, GRID_ROWS), 0)
     line = (row * 10923) >> 16
     side_x, side_z = odd("gx"), odd("gz")
@@ -157,12 +157,15 @@
     tile = jnp.where(jnp.concatenate([row] * 6, axis=0) < TD * TD, jnp.concatenate(ids, axis=0), -1)
     hot = (iota((6 * FACE, GRID_ROWS), 1) == tile).astype(jnp.bfloat16)
     faces = jnp.dot(hot, grid_ref[...], preferred_element_type=jnp.float32).astype(jnp.bfloat16)
-    for at, ref in enumerate((near_x_ref, far_x_ref, near_z_ref, far_z_ref)):
-        ref[...] = faces[at * FACE : (at + 1) * FACE]
     me, count = lax.axis_index("gy"), lax.axis_size("gy")
     for step in range(count):
         high = step == 1
         y_ref[lax.rem(me + step, count)] = faces[(5 if high else 4) * FACE : (6 if high else 5) * FACE]
+    move = pltpu.make_async_copy(y_ref, y_any, sem)
+    move.start()
+    for at, ref in enumerate((near_x_ref, far_x_ref, near_z_ref, far_z_ref)):
+        ref[...] = faces[at * FACE : (at + 1) * FACE]
+    move.wait()
 
 
 def coarse_kernel(column_ref, top_ref, face_ref, own_ref, send_ref):
@@ -189,8 +192,8 @@
     send_ref[...] = jnp.where(iota((FAR_ROWS, TP), 0) == TD * TD, sums, rows).astype(jnp.bfloat16)
 
 
-def gate_kernel(face_ref, *rest):
-    rest[-1][...] = face_ref[...]
+def gate_kernel(*refs):
+    pass
 
 
 def merge_kernel(own_ref, far_ref, field_any, out_ref):
@@ -343,6 +346,7 @@
 VMEM = pl.BlockSpec(memory_space=pltpu.VMEM)
 SMEM = pl.BlockSpec(memory_space=pltpu.SMEM)
 ANY = pl.BlockSpec(memory_space=pl.ANY)
+HBM = pl.BlockSpec(memory_space=pltpu.HBM)
 
 
 def f32(*shape):
@@ -390,9 +394,10 @@
 
     faces = pl.pallas_call(
         face_kernel,
-        out_shape=(bf16(FACE, TP),) * 4 + (bf16(lax.axis_size("gy"), FACE, TP),),
+        out_shape=(bf16(FACE, TP),) * 4 + (pltpu.HBM((lax.axis_size("gy"), FACE, TP), jnp.bfloat16),),
         in_specs=[VMEM],
-        out_specs=[VMEM] * 5,
+        out_specs=[VMEM] * 4 + [HBM],
+        scratch_shapes=[pltpu.VMEM((lax.axis_size("gy"), FACE, TP), jnp.bfloat16), pltpu.SemaphoreType.DMA],
         compiler_params=pltpu.CompilerParams(vmem_limit_bytes=8 << 20),
         cost_estimate=pl.CostEstimate(flops=80_000_000, bytes_accessed=600_000, transcendentals=0),
         name="faces",
@@ -413,9 +418,10 @@
     far_x = exchanged(far_x, ("hx", "cx"), 1)
     face_y = pl.pallas_call(
         gate_kernel,
-        out_shape=bf16(*face_y.shape),
-        in_specs=[VMEM] + [ANY] * 3,
-        out_specs=VMEM,
+        out_shape=pltpu.HBM(face_y.shape, jnp.bfloat16),
+        in_specs=[HBM] + [ANY] * 3,
+        out_specs=HBM,
+        input_output_aliases={0: 0},
         compiler_params=pltpu.CompilerParams(vmem_limit_bytes=4 << 20),
         cost_estimate=pl.CostEstimate(flops=1000, bytes_accessed=1000, transcendentals=0),
         name="gate",

time: 68.2 us -> 68.2 us (level)
  no operation moved by 1% of the time
where the time goes in v10:
time: 68.2 us; the launch traced here: 67.8 us
  starting transfers between devices  50.5 us (74%)
  Pallas kernels  14.6 us (21%)
  between operations  1.39 us (2%)
  waiting for transfers between devices  1.35 us (2%)
    ppermute x4, starting transfers between devices, exchanged(): lax.ppermute(value, axis, [(i, (i + (1 if (i + far) % 2 == 0 else -1)) %...  25.7 us
    all_to_all x1, starting transfers between devices, shards(): column = lax.all_to_all(coarse, 'gz', 0, 0, tiled=True)  16.1 us
    all_to_all x1, starting transfers between devices, shards(): parts = lax.all_to_all(parts, ('cx', 'gy'), 0, 0, tiled=True)  4.68 us
    pallas_call x1, Pallas kernels, shards(): pl.pallas_call(near_kernel, out_shape=(f32(LANES, TP), f32(3, HALF, LANES...  4.56 us
    all_to_all x1, starting transfers between devices, shards(): face_y = lax.all_to_all(face_y, 'gy', 0, 0, tiled=True)  4.02 us
    pallas_call x1, Pallas kernels, shards(): pl.pallas_call(spread_kernel, out_shape=(bf16(GRID_ROWS, TP), f32(lines,...  3.94 us
    pallas_call x1, Pallas kernels, shards(): pl.pallas_call(far_kernel, out_shape=f32(3, HALF, LANES), in_specs=[VMEM]...  3.48 us
  transfers between devices with their start and end apart: 7, of which 2 were waited for; matrix products, arithmetic and copies ran while one was open for 0% of the time, Pallas kernels for 14%

profile of v10, /device:TPU:1, one launch (start us, length us, event | category | flops | bytes accessed | tf_op | source)
XLA Modules:
  0.0 67.8 jit_solution(324727725289460344)
XLA Ops:
  1.3 3.9 %spread.1 = (bf16[256,512]{1,0:T(8,128)(2,1)S(1)}, f32[32,1,128]{2,1,0:T(1,128)}, f32[3,64,128]{2,1,0:T(8,128)S(1)}, f32[8,128]{1,0:T(8,128)S(1)}, f32[64,128]{1...) custom-call(s32[1,1]{1,0:T(1,128)} %bitcast.7.live_ref, ...), custom_call_target="tpu_custom_call" | custom-call | flops 10000000 | bytes 1000000 | tf_op jit(solution)/shard_map/spread/pallas_call | solution.py:373
  5.2 16.1 %all-to-all-start = ((f32[32,1,128]{2,1,0:T(1,128)}), f32[32,1,128]{2,1,0:T(1,128)S(1)}, u32[]{:S(2)}, u32[]{:S(2)}) async-start(f32[32,1,128]{2,1,0:T(1,128)} %get-tuple-element.23), calls=%async_computation | async-start | bytes 32768 | tf_op jit(solution)/shard_map/all_to_all | solution.py:393
  21.3 0.9 %faces.1 = (bf16[48,512]{1,0:T(8,128)(2,1)S(1)}, bf16[48,512]{1,0:T(8,128)(2,1)S(1)}, bf16[48,512]{1,0:T(8,128)(2,1)S(1)}, bf16[48,512]{1,0:T(8,128)(2,1)S(1)}, bf16[4,48,512]{2,1,0:T(8,128)(2,1)}) custom-call(bf16[256,512]{1,0:T(8,128)(2,1)S(1)} %get-tuple-element.25.grid_ref), custom_call_target="tpu_custom_call" | custom-call | flops 80000000 | bytes 600000 | tf_op jit(solution)/shard_map/faces/pallas_call | solution.py:395
  22.3 2.9 %collective-permute-start.1 = (bf16[48,512]{1,0:T(8,128)(2,1)S(1)}, bf16[48,512]{1,0:T(8,128)(2,1)S(1)}, u32[]{:S(2)}, u32[]{:S(2)}) collective-permute-start(bf16[48,512]{1,0:T(8,128)(2,1)S(1)} %get-tuple-element.30), channel_id=1, source_target_pairs={{0,128},{128,0},{256,384},{384,256},{1,129},{129,1},{257,385},{385... | collective-permute-start | bytes 147464 | tf_op jit(solution)/shard_map/ppermute | solution.py:362
  25.1 3.4 %collective-permute-start.2 = (bf16[48,512]{1,0:T(8,128)(2,1)S(1)}, bf16[48,512]{1,0:T(8,128)(2,1)S(1)}, u32[]{:S(2)}, u32[]{:S(2)}) collective-permute-start(bf16[48,512]{1,0:T(8,128)(2,1)S(1)} %get-tuple-element.31), channel_id=1, source_target_pairs={{0,1},{1,0},{2,3},{3,2},{4,5},{5,4},{6,7},{7,6},{8,9},{9,8},{10,11... | collective-permute-start | bytes 147464 | tf_op jit(solution)/shard_map/ppermute | solution.py:362
  28.6 11.0 %collective-permute-start.3 = (bf16[48,512]{1,0:T(8,128)(2,1)S(1)}, bf16[48,512]{1,0:T(8,128)(2,1)S(1)}, u32[]{:S(2)}, u32[]{:S(2)}) collective-permute-start(bf16[48,512]{1,0:T(8,128)(2,1)S(1)} %get-tuple-element.32), channel_id=1, source_target_pairs={{0,31},{1,2},{2,1},{3,4},{4,3},{5,6},{6,5},{7,8},{8,7},{9,10},{10,... | collective-permute-start | bytes 147464 | tf_op jit(solution)/shard_map/ppermute | solution.py:362
  39.6 0.0 all-to-all-done.column_ref
  39.6 0.1 coarse.1
  39.7 8.4 %collective-permute-start = (bf16[40,512]{1,0:T(8,128)(2,1)S(1)}, bf16[40,512]{1,0:T(8,128)(2,1)S(1)}, u32[]{:S(2)}, u32[]{:S(2)}) collective-permute-start(bf16[40,512]{1,0:T(8,128)(2,1)S(1)} %get-tuple-element.28), channel_id=1, source_target_pairs={{0,384},{128,256},{256,128},{384,0},{1,385},{129,257},{257,129},{3... | collective-permute-start | bytes 122888 | tf_op jit(solution)/shard_map/ppermute | solution.py:362
  48.1 0.0 collective-permute-done.1.near_x_ref.refs_2_
  48.1 0.0 collective-permute-done.2.near_z_ref.refs_3_
  48.2 4.0 %all-to-all-start.2 = ((bf16[4,48,512]{2,1,0:T(8,128)(2,1)}), bf16[4,48,512]{2,1,0:T(8,128)(2,1)S(1)}, u32[]{:S(2)}, u32[]{:S(2)}) async-start(bf16[4,48,512]{2,1,0:T(8,128)(2,1)} %gate.1), calls=%async_computation.2 | async-start | bytes 393216 | tf_op jit(solution)/shard_map/all_to_all | solution.py:429
  52.2 0.0 collective-permute-done.3.far_z_ref
  52.2 4.6 %near.1 = (f32[128,512]{1,0:T(8,128)S(1)}, f32[3,64,128]{2,1,0:T(8,128)S(1)}) custom-call(f32[8,128]{1,0:T(8,128)S(1)} %get-tuple-element.29.tiles_ref, bf16[256,512]{1,0:T(8,128)(2,1)S(1)} %get-tuple-element.25.grid_ref, bf16[48,512]{1,0:T(8,128)(2,1)S(1)} %collective-permute-done.1.near_x_ref.refs_2_, ...), custom_call_target="tpu_custom_call" | custom-call | flops 20000000000 | bytes 1000 | tf_op jit(solution)/shard_map/near/pallas_call | solution.py:431
  56.8 0.0 collective-permute-done.far_ref.far_x_ref
  56.8 0.7 merge.1
  57.4 0.3 all-to-all-done.2.y_ref
  57.8 4.7 %all-to-all-start.1 = ((f32[8,1,128]{2,1,0:T(1,128)}), f32[8,1,128]{2,1,0:T(1,128)S(1)}, u32[]{:S(2)}, u32[]{:S(2)}) async-start(f32[8,1,128]{2,1,0:T(1,128)} %merge.1), calls=%async_computation.1 | async-start | bytes 8192 | tf_op jit(solution)/shard_map/all_to_all | solution.py:454
  62.5 3.5 %far.1.near_ref = f32[3,64,128]{2,1,0:T(8,128)S(1)} custom-call(f32[8,128]{1,0:T(8,128)S(1)} %get-tuple-element.29.tiles_ref, f32[128,512]{1,0:T(8,128)S(1)} %get-tuple-element.36.field_any.part_ref, bf16[40,512]{1,0:T(8,128)(2,1)S(1)} %collective-permute-done.far_ref.far_x_ref, bf16[4,48,512]{2,1,0:T(8,128)(2,1)S(1)} %all-to-all-done.2.y_ref, ...), custom_call_target="tpu_custom_call" | custom-call | flops 1000000000 | bytes 4000000 | tf_op jit(solution)/shard_map/far/pallas_call | solution.py:456
  66.0 1.0 %all-to-all-done.1.parts_ref = f32[8,1,128]{2,1,0:T(1,128)S(1)} async-done(((f32[8,1,128]{2,1,0:T(1,128)}), f32[8,1,128]{2,1,0:T(1,128)S(1)}, u32[]{:S(2)}, u32[]{:S(2)}) %all-to-all-start.1) | async-done | bytes 4128 | tf_op jit(solution)/shard_map/all_to_all | solution.py:454
  67.0 0.8 %final.1 = (f32[3,64,128]{2,1,0:T(8,128)}, f32[6,64,128]{2,1,0:T(8,128)}) custom-call(f32[8,1,128]{2,1,0:T(1,128)S(1)} %all-to-all-done.1.parts_ref, s32[64,128]{1,0:T(8,128)S(1)} %get-tuple-element.37.corner_ref, f32[3,64,128]{2,1,0:T(8,128)S(1)} %far.1.near_ref, f32[3,64,128]{2,1,0:T(8,128)S(1)} %get-tuple-element.39.unit_ref, ...), custom_call_target="tpu_custom_call" | custom-call | flops 500000 | bytes 600000 | tf_op jit(solution)/shard_map/final/pallas_call | solution.py:470
  (1 shorter events, 0.0 us)
Async XLA Ops:
  5.2 34.4 %all-to-all-start = ((f32[32,1,128]{2,1,0:T(1,128)}), f32[32,1,128]{2,1,0:T(1,128)S(1)}, u32[]{:S(2)}, u32[]{:S(2)}) async-start(f32[32,1,128]{2,1,0:T(1,128)} %get-tuple-element.23), calls=%async_computation | async-start | bytes 32768 | tf_op jit(solution)/shard_map/all_to_all | solution.py:393
  22.3 25.9 %collective-permute-start.1 = (bf16[48,512]{1,0:T(8,128)(2,1)S(1)}, bf16[48,512]{1,0:T(8,128)(2,1)S(1)}, u32[]{:S(2)}, u32[]{:S(2)}) collective-permute-start(bf16[48,512]{1,0:T(8,128)(2,1)S(1)} %get-tuple-element.30), channel_id=1, source_target_pairs={{0,128},{128,0},{256,384},{384,256},{1,129},{129,1},{257,385},{385... | collective-permute-start | bytes 147464 | tf_op jit(solution)/shard_map/ppermute | solution.py:362
  25.1 23.0 %collective-permute-start.2 = (bf16[48,512]{1,0:T(8,128)(2,1)S(1)}, bf16[48,512]{1,0:T(8,128)(2,1)S(1)}, u32[]{:S(2)}, u32[]{:S(2)}) collective-permute-start(bf16[48,512]{1,0:T(8,128)(2,1)S(1)} %get-tuple-element.31), channel_id=1, source_target_pairs={{0,1},{1,0},{2,3},{3,2},{4,5},{5,4},{6,7},{7,6},{8,9},{9,8},{10,11... | collective-permute-start | bytes 147464 | tf_op jit(solution)/shard_map/ppermute | solution.py:362
  28.6 23.6 %collective-permute-start.3 = (bf16[48,512]{1,0:T(8,128)(2,1)S(1)}, bf16[48,512]{1,0:T(8,128)(2,1)S(1)}, u32[]{:S(2)}, u32[]{:S(2)}) collective-permute-start(bf16[48,512]{1,0:T(8,128)(2,1)S(1)} %get-tuple-element.32), channel_id=1, source_target_pairs={{0,31},{1,2},{2,1},{3,4},{4,3},{5,6},{6,5},{7,8},{8,7},{9,10},{10,... | collective-permute-start | bytes 147464 | tf_op jit(solution)/shard_map/ppermute | solution.py:362
  39.7 17.0 %collective-permute-start = (bf16[40,512]{1,0:T(8,128)(2,1)S(1)}, bf16[40,512]{1,0:T(8,128)(2,1)S(1)}, u32[]{:S(2)}, u32[]{:S(2)}) collective-permute-start(bf16[40,512]{1,0:T(8,128)(2,1)S(1)} %get-tuple-element.28), channel_id=1, source_target_pairs={{0,384},{128,256},{256,128},{384,0},{1,385},{129,257},{257,129},{3... | collective-permute-start | bytes 122888 | tf_op jit(solution)/shard_map/ppermute | solution.py:362
  48.2 9.6 %all-to-all-start.2 = ((bf16[4,48,512]{2,1,0:T(8,128)(2,1)}), bf16[4,48,512]{2,1,0:T(8,128)(2,1)S(1)}, u32[]{:S(2)}, u32[]{:S(2)}) async-start(bf16[4,48,512]{2,1,0:T(8,128)(2,1)} %gate.1), calls=%async_computation.2 | async-start | bytes 393216 | tf_op jit(solution)/shard_map/all_to_all | solution.py:429
  57.8 9.2 %all-to-all-start.1 = ((f32[8,1,128]{2,1,0:T(1,128)}), f32[8,1,128]{2,1,0:T(1,128)S(1)}, u32[]{:S(2)}, u32[]{:S(2)}) async-start(f32[8,1,128]{2,1,0:T(1,128)} %merge.1), calls=%async_computation.1 | async-start | bytes 8192 | tf_op jit(solution)/shard_map/all_to_all | solution.py:454

commit v11 on v10

--- a/solution.py
+++ b/solution.py
@@ -153,18 +153,22 @@
     line = (row * 10923) >> 16
     side_x, side_z = odd("gx"), odd("gz")
     low_y = line * 36 + (row - line * TD)
-    ids = [row + 180 * (1 - side_x), row + 180 * side_x, row * TD + 5 * (1 - side_z), row * TD + 5 * side_z, low_y, low_y + 30]
-    tile = jnp.where(jnp.concatenate([row] * 6, axis=0) < TD * TD, jnp.concatenate(ids, axis=0), -1)
-    hot = (iota((6 * FACE, GRID_ROWS), 1) == tile).astype(jnp.bfloat16)
-    faces = jnp.dot(hot, grid_ref[...], preferred_element_type=jnp.float32).astype(jnp.bfloat16)
+    def made(ids):
+        count = len(ids)
+        tile = jnp.where(jnp.concatenate([row] * count, axis=0) < TD * TD, jnp.concatenate(ids, axis=0), -1)
+        hot = (iota((count * FACE, GRID_ROWS), 1) == tile).astype(jnp.bfloat16)
+        faces = jnp.dot(hot, grid_ref[...], preferred_element_type=jnp.float32).astype(jnp.bfloat16)
+        return [faces[at * FACE : (at + 1) * FACE] for at in range(count)]
+
+    low, high = made([low_y, low_y + 30])
     me, count = lax.axis_index("gy"), lax.axis_size("gy")
     for step in range(count):
-        high = step == 1
-        y_ref[lax.rem(me + step, count)] = faces[(5 if high else 4) * FACE : (6 if high else 5) * FACE]
+        y_ref[lax.rem(me + step, count)] = high if step == 1 else low
     move = pltpu.make_async_copy(y_ref, y_any, sem)
     move.start()
-    for at, ref in enumerate((near_x_ref, far_x_ref, near_z_ref, far_z_ref)):
-        ref[...] = faces[at * FACE : (at + 1) * FACE]
+    ids = [row + 180 * (1 - side_x), row + 180 * side_x, row * TD + 5 * (1 - side_z), row * TD + 5 * side_z]
+    for ref, face in zip((near_x_ref, far_x_ref, near_z_ref, far_z_ref), made(ids), strict=True):
+        ref[...] = face
     move.wait()
 
 
@@ -253,7 +257,7 @@
     base = GRID_ROWS
     edges = (
         ("gx", tx, 36, base + row_x, nothing + 0 * row_x),
-        ("gy", ty, TD, nothing + 0 * row_x, nothing + 0 * row_x),
+        ("gy", ty, TD, CUBES + 0 * row_x, CUBES + 0 * row_x),
         ("gz", tz, 1, base + FACE + row_z, base + 2 * FACE + row_z),
     )
     targets = [tile]
@@ -261,11 +265,11 @@
         side = jnp.broadcast_to(odd(axis), near.shape) == 1
         targets.append(jnp.where(place < TD - 1, tile + stride, jnp.where(side, far, near)))
         targets.append(jnp.where(place > 0, tile - stride, jnp.where(side, near, far)))
-    at_row = iota((LANES, EXT_ROWS), 1)
     field = None
     for at, target in enumerate(targets):
-        hot = (at_row == target).astype(jnp.bfloat16)
-        rows = jnp.dot(hot, ext_ref[...], preferred_element_type=jnp.float32).astype(jnp.bfloat16)
+        reach = GRID_ROWS if at in (0, 3, 4) else EXT_ROWS
+        hot = (iota((LANES, reach), 1) == target).astype(jnp.bfloat16)
+        rows = jnp.dot(hot, ext_ref[:reach], preferred_element_type=jnp.float32).astype(jnp.bfloat16)
         flipped = at > 0 and at % 2 == 0
         term = lax.dot_general(
             rows, blocks_ref[(at + 1) // 2], (((1,), (0 if flipped else 1,)), ((), ())), preferred_element_type=jnp.float32

time: 68.2 us -> 68 us (level)
  no operation moved by 1% of the time
where the time goes in v11:
time: 68 us; the launch traced here: 67.6 us
  starting transfers between devices  50.4 us (74%)
  Pallas kernels  14.4 us (21%)
  waiting for transfers between devices  1.47 us (2%)
  between operations  1.39 us (2%)
    ppermute x4, starting transfers between devices, exchanged(): lax.ppermute(value, axis, [(i, (i + (1 if (i + far) % 2 == 0 else -1)) %...  25.7 us
    all_to_all x1, starting transfers between devices, shards(): column = lax.all_to_all(coarse, 'gz', 0, 0, tiled=True)  16.1 us
    all_to_all x1, starting transfers between devices, shards(): parts = lax.all_to_all(parts, ('cx', 'gy'), 0, 0, tiled=True)  4.57 us
    pallas_call x1, Pallas kernels, shards(): pl.pallas_call(near_kernel, out_shape=(f32(LANES, TP), f32(3, HALF, LANES...  4.45 us
    all_to_all x1, starting transfers between devices, shards(): face_y = lax.all_to_all(face_y, 'gy', 0, 0, tiled=True)  4.03 us
    pallas_call x1, Pallas kernels, shards(): pl.pallas_call(spread_kernel, out_shape=(bf16(GRID_ROWS, TP), f32(lines,...  3.94 us
    pallas_call x1, Pallas kernels, shards(): pl.pallas_call(far_kernel, out_shape=f32(3, HALF, LANES), in_specs=[VMEM]...  3.48 us
  transfers between devices with their start and end apart: 7, of which 2 were waited for; matrix products, arithmetic and copies ran while one was open for 0% of the time, Pallas kernels for 14%

profile of v11, /device:TPU:1, one launch (start us, length us, event | category | flops | bytes accessed | tf_op | source)
XLA Modules:
  0.0 67.6 jit_solution(16617353679448506951)
XLA Ops:
  1.3 3.9 %spread.1 = (bf16[256,512]{1,0:T(8,128)(2,1)S(1)}, f32[32,1,128]{2,1,0:T(1,128)}, f32[3,64,128]{2,1,0:T(8,128)S(1)}, f32[8,128]{1,0:T(8,128)S(1)}, f32[64,128]{1...) custom-call(s32[1,1]{1,0:T(1,128)} %bitcast.7.live_ref, ...), custom_call_target="tpu_custom_call" | custom-call | flops 10000000 | bytes 1000000 | tf_op jit(solution)/shard_map/spread/pallas_call | solution.py:377
  5.2 16.1 %all-to-all-start = ((f32[32,1,128]{2,1,0:T(1,128)}), f32[32,1,128]{2,1,0:T(1,128)S(1)}, u32[]{:S(2)}, u32[]{:S(2)}) async-start(f32[32,1,128]{2,1,0:T(1,128)} %get-tuple-element.23), calls=%async_computation | async-start | bytes 32768 | tf_op jit(solution)/shard_map/all_to_all | solution.py:397
  21.3 0.9 %faces.1 = (bf16[48,512]{1,0:T(8,128)(2,1)S(1)}, bf16[48,512]{1,0:T(8,128)(2,1)S(1)}, bf16[48,512]{1,0:T(8,128)(2,1)S(1)}, bf16[48,512]{1,0:T(8,128)(2,1)S(1)}, bf16[4,48,512]{2,1,0:T(8,128)(2,1)}) custom-call(bf16[256,512]{1,0:T(8,128)(2,1)S(1)} %get-tuple-element.25.grid_ref), custom_call_target="tpu_custom_call" | custom-call | flops 80000000 | bytes 600000 | tf_op jit(solution)/shard_map/faces/pallas_call | solution.py:399
  22.2 2.9 %collective-permute-start.1 = (bf16[48,512]{1,0:T(8,128)(2,1)S(1)}, bf16[48,512]{1,0:T(8,128)(2,1)S(1)}, u32[]{:S(2)}, u32[]{:S(2)}) collective-permute-start(bf16[48,512]{1,0:T(8,128)(2,1)S(1)} %get-tuple-element.30), channel_id=1, source_target_pairs={{0,128},{128,0},{256,384},{384,256},{1,129},{129,1},{257,385},{385... | collective-permute-start | bytes 147464 | tf_op jit(solution)/shard_map/ppermute | solution.py:366
  25.1 3.4 %collective-permute-start.2 = (bf16[48,512]{1,0:T(8,128)(2,1)S(1)}, bf16[48,512]{1,0:T(8,128)(2,1)S(1)}, u32[]{:S(2)}, u32[]{:S(2)}) collective-permute-start(bf16[48,512]{1,0:T(8,128)(2,1)S(1)} %get-tuple-element.31), channel_id=1, source_target_pairs={{0,1},{1,0},{2,3},{3,2},{4,5},{5,4},{6,7},{7,6},{8,9},{9,8},{10,11... | collective-permute-start | bytes 147464 | tf_op jit(solution)/shard_map/ppermute | solution.py:366
  28.5 11.0 %collective-permute-start.3 = (bf16[48,512]{1,0:T(8,128)(2,1)S(1)}, bf16[48,512]{1,0:T(8,128)(2,1)S(1)}, u32[]{:S(2)}, u32[]{:S(2)}) collective-permute-start(bf16[48,512]{1,0:T(8,128)(2,1)S(1)} %get-tuple-element.32), channel_id=1, source_target_pairs={{0,31},{1,2},{2,1},{3,4},{4,3},{5,6},{6,5},{7,8},{8,7},{9,10},{10,... | collective-permute-start | bytes 147464 | tf_op jit(solution)/shard_map/ppermute | solution.py:366
  39.5 0.0 all-to-all-done.column_ref
  39.5 0.1 coarse.1
  39.7 8.4 %collective-permute-start = (bf16[40,512]{1,0:T(8,128)(2,1)S(1)}, bf16[40,512]{1,0:T(8,128)(2,1)S(1)}, u32[]{:S(2)}, u32[]{:S(2)}) collective-permute-start(bf16[40,512]{1,0:T(8,128)(2,1)S(1)} %get-tuple-element.28), channel_id=1, source_target_pairs={{0,384},{128,256},{256,128},{384,0},{1,385},{129,257},{257,129},{3... | collective-permute-start | bytes 122888 | tf_op jit(solution)/shard_map/ppermute | solution.py:366
  48.1 0.0 collective-permute-done.1.near_x_ref.refs_2_
  48.1 0.0 collective-permute-done.2.near_z_ref.refs_3_
  48.1 4.0 %all-to-all-start.2 = ((bf16[4,48,512]{2,1,0:T(8,128)(2,1)}), bf16[4,48,512]{2,1,0:T(8,128)(2,1)S(1)}, u32[]{:S(2)}, u32[]{:S(2)}) async-start(bf16[4,48,512]{2,1,0:T(8,128)(2,1)} %gate.1), calls=%async_computation.2 | async-start | bytes 393216 | tf_op jit(solution)/shard_map/all_to_all | solution.py:433
  52.1 0.0 collective-permute-done.3.far_z_ref
  52.1 4.4 %near.1 = (f32[128,512]{1,0:T(8,128)S(1)}, f32[3,64,128]{2,1,0:T(8,128)S(1)}) custom-call(f32[8,128]{1,0:T(8,128)S(1)} %get-tuple-element.29.tiles_ref, bf16[256,512]{1,0:T(8,128)(2,1)S(1)} %get-tuple-element.25.grid_ref, bf16[48,512]{1,0:T(8,128)(2,1)S(1)} %collective-permute-done.1.near_x_ref.refs_2_, ...), custom_call_target="tpu_custom_call" | custom-call | flops 20000000000 | bytes 1000 | tf_op jit(solution)/shard_map/near/pallas_call | solution.py:435
  56.6 0.0 collective-permute-done.far_ref.far_x_ref
  56.6 0.7 merge.1
  57.3 0.5 all-to-all-done.2.y_ref
  57.7 4.6 %all-to-all-start.1 = ((f32[8,1,128]{2,1,0:T(1,128)}), f32[8,1,128]{2,1,0:T(1,128)S(1)}, u32[]{:S(2)}, u32[]{:S(2)}) async-start(f32[8,1,128]{2,1,0:T(1,128)} %merge.1), calls=%async_computation.1 | async-start | bytes 8192 | tf_op jit(solution)/shard_map/all_to_all | solution.py:458
  62.3 3.5 %far.1.near_ref = f32[3,64,128]{2,1,0:T(8,128)S(1)} custom-call(f32[8,128]{1,0:T(8,128)S(1)} %get-tuple-element.29.tiles_ref, f32[128,512]{1,0:T(8,128)S(1)} %get-tuple-element.36.field_any.part_ref, bf16[40,512]{1,0:T(8,128)(2,1)S(1)} %collective-permute-done.far_ref.far_x_ref, bf16[4,48,512]{2,1,0:T(8,128)(2,1)S(1)} %all-to-all-done.2.y_ref, ...), custom_call_target="tpu_custom_call" | custom-call | flops 1000000000 | bytes 4000000 | tf_op jit(solution)/shard_map/far/pallas_call | solution.py:460
  65.8 1.0 %all-to-all-done.1.parts_ref = f32[8,1,128]{2,1,0:T(1,128)S(1)} async-done(((f32[8,1,128]{2,1,0:T(1,128)}), f32[8,1,128]{2,1,0:T(1,128)S(1)}, u32[]{:S(2)}, u32[]{:S(2)}) %all-to-all-start.1) | async-done | bytes 4128 | tf_op jit(solution)/shard_map/all_to_all | solution.py:458
  66.8 0.8 %final.1 = (f32[3,64,128]{2,1,0:T(8,128)}, f32[6,64,128]{2,1,0:T(8,128)}) custom-call(f32[8,1,128]{2,1,0:T(1,128)S(1)} %all-to-all-done.1.parts_ref, s32[64,128]{1,0:T(8,128)S(1)} %get-tuple-element.37.corner_ref, f32[3,64,128]{2,1,0:T(8,128)S(1)} %far.1.near_ref, f32[3,64,128]{2,1,0:T(8,128)S(1)} %get-tuple-element.39.unit_ref, ...), custom_call_target="tpu_custom_call" | custom-call | flops 500000 | bytes 600000 | tf_op jit(solution)/shard_map/final/pallas_call | solution.py:474
  (1 shorter events, 0.0 us)
Async XLA Ops:
  5.2 34.3 %all-to-all-start = ((f32[32,1,128]{2,1,0:T(1,128)}), f32[32,1,128]{2,1,0:T(1,128)S(1)}, u32[]{:S(2)}, u32[]{:S(2)}) async-start(f32[32,1,128]{2,1,0:T(1,128)} %get-tuple-element.23), calls=%async_computation | async-start | bytes 32768 | tf_op jit(solution)/shard_map/all_to_all | solution.py:397
  22.2 25.9 %collective-permute-start.1 = (bf16[48,512]{1,0:T(8,128)(2,1)S(1)}, bf16[48,512]{1,0:T(8,128)(2,1)S(1)}, u32[]{:S(2)}, u32[]{:S(2)}) collective-permute-start(bf16[48,512]{1,0:T(8,128)(2,1)S(1)} %get-tuple-element.30), channel_id=1, source_target_pairs={{0,128},{128,0},{256,384},{384,256},{1,129},{129,1},{257,385},{385... | collective-permute-start | bytes 147464 | tf_op jit(solution)/shard_map/ppermute | solution.py:366
  25.1 23.0 %collective-permute-start.2 = (bf16[48,512]{1,0:T(8,128)(2,1)S(1)}, bf16[48,512]{1,0:T(8,128)(2,1)S(1)}, u32[]{:S(2)}, u32[]{:S(2)}) collective-permute-start(bf16[48,512]{1,0:T(8,128)(2,1)S(1)} %get-tuple-element.31), channel_id=1, source_target_pairs={{0,1},{1,0},{2,3},{3,2},{4,5},{5,4},{6,7},{7,6},{8,9},{9,8},{10,11... | collective-permute-start | bytes 147464 | tf_op jit(solution)/shard_map/ppermute | solution.py:366
  28.5 23.6 %collective-permute-start.3 = (bf16[48,512]{1,0:T(8,128)(2,1)S(1)}, bf16[48,512]{1,0:T(8,128)(2,1)S(1)}, u32[]{:S(2)}, u32[]{:S(2)}) collective-permute-start(bf16[48,512]{1,0:T(8,128)(2,1)S(1)} %get-tuple-element.32), channel_id=1, source_target_pairs={{0,31},{1,2},{2,1},{3,4},{4,3},{5,6},{6,5},{7,8},{8,7},{9,10},{10,... | collective-permute-start | bytes 147464 | tf_op jit(solution)/shard_map/ppermute | solution.py:366
  39.7 16.9 %collective-permute-start = (bf16[40,512]{1,0:T(8,128)(2,1)S(1)}, bf16[40,512]{1,0:T(8,128)(2,1)S(1)}, u32[]{:S(2)}, u32[]{:S(2)}) collective-permute-start(bf16[40,512]{1,0:T(8,128)(2,1)S(1)} %get-tuple-element.28), channel_id=1, source_target_pairs={{0,384},{128,256},{256,128},{384,0},{1,385},{129,257},{257,129},{3... | collective-permute-start | bytes 122888 | tf_op jit(solution)/shard_map/ppermute | solution.py:366
  48.1 9.6 %all-to-all-start.2 = ((bf16[4,48,512]{2,1,0:T(8,128)(2,1)}), bf16[4,48,512]{2,1,0:T(8,128)(2,1)S(1)}, u32[]{:S(2)}, u32[]{:S(2)}) async-start(bf16[4,48,512]{2,1,0:T(8,128)(2,1)} %gate.1), calls=%async_computation.2 | async-start | bytes 393216 | tf_op jit(solution)/shard_map/all_to_all | solution.py:433
  57.7 9.1 %all-to-all-start.1 = ((f32[8,1,128]{2,1,0:T(1,128)}), f32[8,1,128]{2,1,0:T(1,128)S(1)}, u32[]{:S(2)}, u32[]{:S(2)}) async-start(f32[8,1,128]{2,1,0:T(1,128)} %merge.1), calls=%async_computation.1 | async-start | bytes 8192 | tf_op jit(solution)/shard_map/all_to_all | solution.py:458

commit v12 on v11

--- a/solution.py
+++ b/solution.py
@@ -108,7 +108,7 @@
             return tuple(new)
 
         start = tuple(jnp.zeros((TL, LANES), jnp.float32) for _ in range(32))
-        total = lax.fori_loop(0, CS, step, start, unroll=4)
+        total = lax.fori_loop(0, CS, step, start, unroll=8)
         for slot in range(32):
             cell_ref[pl.ds((32 * half + slot) * TL, TL), :] = total[slot]
 

time: 68 us -> 67.8 us (level)
  no operation moved by 1% of the time
where the time goes in v12:
time: 67.8 us; the launch traced here: 67.4 us
  starting transfers between devices  50.4 us (74%)
  Pallas kernels  14.2 us (21%)
  waiting for transfers between devices  1.47 us (2%)
  between operations  1.39 us (2%)
    ppermute x4, starting transfers between devices, exchanged(): lax.ppermute(value, axis, [(i, (i + (1 if (i + far) % 2 == 0 else -1)) %...  25.7 us
    all_to_all x1, starting transfers between devices, shards(): column = lax.all_to_all(coarse, 'gz', 0, 0, tiled=True)  16.1 us
    all_to_all x1, starting transfers between devices, shards(): parts = lax.all_to_all(parts, ('cx', 'gy'), 0, 0, tiled=True)  4.56 us
    pallas_call x1, Pallas kernels, shards(): pl.pallas_call(near_kernel, out_shape=(f32(LANES, TP), f32(3, HALF, LANES...  4.44 us
    all_to_all x1, starting transfers between devices, shards(): face_y = lax.all_to_all(face_y, 'gy', 0, 0, tiled=True)  4.02 us
    pallas_call x1, Pallas kernels, shards(): pl.pallas_call(spread_kernel, out_shape=(bf16(GRID_ROWS, TP), f32(lines,...  3.73 us
    pallas_call x1, Pallas kernels, shards(): pl.pallas_call(far_kernel, out_shape=f32(3, HALF, LANES), in_specs=[VMEM]...  3.48 us
  transfers between devices with their start and end apart: 7, of which 2 were waited for; matrix products, arithmetic and copies ran while one was open for 0% of the time, Pallas kernels for 14%

profile of v12, /device:TPU:1, one launch (start us, length us, event | category | flops | bytes accessed | tf_op | source)
XLA Modules:
  0.0 67.4 jit_solution(12437182360519975825)
XLA Ops:
  1.3 3.7 %spread.1 = (bf16[256,512]{1,0:T(8,128)(2,1)S(1)}, f32[32,1,128]{2,1,0:T(1,128)}, f32[3,64,128]{2,1,0:T(8,128)S(1)}, f32[8,128]{1,0:T(8,128)S(1)}, f32[64,128]{1...) custom-call(s32[1,1]{1,0:T(1,128)} %bitcast.7.live_ref, ...), custom_call_target="tpu_custom_call" | custom-call | flops 10000000 | bytes 1000000 | tf_op jit(solution)/shard_map/spread/pallas_call | solution.py:377
  5.0 16.1 %all-to-all-start = ((f32[32,1,128]{2,1,0:T(1,128)}), f32[32,1,128]{2,1,0:T(1,128)S(1)}, u32[]{:S(2)}, u32[]{:S(2)}) async-start(f32[32,1,128]{2,1,0:T(1,128)} %get-tuple-element.23), calls=%async_computation | async-start | bytes 32768 | tf_op jit(solution)/shard_map/all_to_all | solution.py:397
  21.1 0.9 %faces.1 = (bf16[48,512]{1,0:T(8,128)(2,1)S(1)}, bf16[48,512]{1,0:T(8,128)(2,1)S(1)}, bf16[48,512]{1,0:T(8,128)(2,1)S(1)}, bf16[48,512]{1,0:T(8,128)(2,1)S(1)}, bf16[4,48,512]{2,1,0:T(8,128)(2,1)}) custom-call(bf16[256,512]{1,0:T(8,128)(2,1)S(1)} %get-tuple-element.25.grid_ref), custom_call_target="tpu_custom_call" | custom-call | flops 80000000 | bytes 600000 | tf_op jit(solution)/shard_map/faces/pallas_call | solution.py:399
  22.0 2.9 %collective-permute-start.1 = (bf16[48,512]{1,0:T(8,128)(2,1)S(1)}, bf16[48,512]{1,0:T(8,128)(2,1)S(1)}, u32[]{:S(2)}, u32[]{:S(2)}) collective-permute-start(bf16[48,512]{1,0:T(8,128)(2,1)S(1)} %get-tuple-element.30), channel_id=1, source_target_pairs={{0,128},{128,0},{256,384},{384,256},{1,129},{129,1},{257,385},{385... | collective-permute-start | bytes 147464 | tf_op jit(solution)/shard_map/ppermute | solution.py:366
  24.9 3.4 %collective-permute-start.2 = (bf16[48,512]{1,0:T(8,128)(2,1)S(1)}, bf16[48,512]{1,0:T(8,128)(2,1)S(1)}, u32[]{:S(2)}, u32[]{:S(2)}) collective-permute-start(bf16[48,512]{1,0:T(8,128)(2,1)S(1)} %get-tuple-element.31), channel_id=1, source_target_pairs={{0,1},{1,0},{2,3},{3,2},{4,5},{5,4},{6,7},{7,6},{8,9},{9,8},{10,11... | collective-permute-start | bytes 147464 | tf_op jit(solution)/shard_map/ppermute | solution.py:366
  28.3 11.0 %collective-permute-start.3 = (bf16[48,512]{1,0:T(8,128)(2,1)S(1)}, bf16[48,512]{1,0:T(8,128)(2,1)S(1)}, u32[]{:S(2)}, u32[]{:S(2)}) collective-permute-start(bf16[48,512]{1,0:T(8,128)(2,1)S(1)} %get-tuple-element.32), channel_id=1, source_target_pairs={{0,31},{1,2},{2,1},{3,4},{4,3},{5,6},{6,5},{7,8},{8,7},{9,10},{10,... | collective-permute-start | bytes 147464 | tf_op jit(solution)/shard_map/ppermute | solution.py:366
  39.3 0.0 all-to-all-done.column_ref
  39.3 0.1 coarse.1
  39.5 8.4 %collective-permute-start = (bf16[40,512]{1,0:T(8,128)(2,1)S(1)}, bf16[40,512]{1,0:T(8,128)(2,1)S(1)}, u32[]{:S(2)}, u32[]{:S(2)}) collective-permute-start(bf16[40,512]{1,0:T(8,128)(2,1)S(1)} %get-tuple-element.28), channel_id=1, source_target_pairs={{0,384},{128,256},{256,128},{384,0},{1,385},{129,257},{257,129},{3... | collective-permute-start | bytes 122888 | tf_op jit(solution)/shard_map/ppermute | solution.py:366
  47.9 0.0 collective-permute-done.1.near_x_ref.refs_2_
  47.9 0.0 collective-permute-done.2.near_z_ref.refs_3_
  47.9 4.0 %all-to-all-start.2 = ((bf16[4,48,512]{2,1,0:T(8,128)(2,1)}), bf16[4,48,512]{2,1,0:T(8,128)(2,1)S(1)}, u32[]{:S(2)}, u32[]{:S(2)}) async-start(bf16[4,48,512]{2,1,0:T(8,128)(2,1)} %gate.1), calls=%async_computation.2 | async-start | bytes 393216 | tf_op jit(solution)/shard_map/all_to_all | solution.py:433
  51.9 0.0 collective-permute-done.3.far_z_ref
  51.9 4.4 %near.1 = (f32[128,512]{1,0:T(8,128)S(1)}, f32[3,64,128]{2,1,0:T(8,128)S(1)}) custom-call(f32[8,128]{1,0:T(8,128)S(1)} %get-tuple-element.29.tiles_ref, bf16[256,512]{1,0:T(8,128)(2,1)S(1)} %get-tuple-element.25.grid_ref, bf16[48,512]{1,0:T(8,128)(2,1)S(1)} %collective-permute-done.1.near_x_ref.refs_2_, ...), custom_call_target="tpu_custom_call" | custom-call | flops 20000000000 | bytes 1000 | tf_op jit(solution)/shard_map/near/pallas_call | solution.py:435
  56.4 0.0 collective-permute-done.far_ref.far_x_ref
  56.4 0.7 %merge.1 = f32[8,1,128]{2,1,0:T(1,128)} custom-call(f32[1,128]{1,0:T(1,128)S(1)} %get-tuple-element.27.own_ref.refs_1_, bf16[40,512]{1,0:T(8,128)(2,1)S(1)} %collective-permute-done.far_ref.far_x_ref, f32[128,512]{1,0:T(8,128)S(1)} %get-tuple-element.36.field_any.part_ref), custom_call_target="tpu_custom_call" | custom-call | flops 10000 | bytes 60000 | tf_op jit(solution)/shard_map/merge/pallas_call | solution.py:449
  57.1 0.5 all-to-all-done.2.y_ref
  57.5 4.6 %all-to-all-start.1 = ((f32[8,1,128]{2,1,0:T(1,128)}), f32[8,1,128]{2,1,0:T(1,128)S(1)}, u32[]{:S(2)}, u32[]{:S(2)}) async-start(f32[8,1,128]{2,1,0:T(1,128)} %merge.1), calls=%async_computation.1 | async-start | bytes 8192 | tf_op jit(solution)/shard_map/all_to_all | solution.py:458
  62.1 3.5 %far.1.near_ref = f32[3,64,128]{2,1,0:T(8,128)S(1)} custom-call(f32[8,128]{1,0:T(8,128)S(1)} %get-tuple-element.29.tiles_ref, f32[128,512]{1,0:T(8,128)S(1)} %get-tuple-element.36.field_any.part_ref, bf16[40,512]{1,0:T(8,128)(2,1)S(1)} %collective-permute-done.far_ref.far_x_ref, bf16[4,48,512]{2,1,0:T(8,128)(2,1)S(1)} %all-to-all-done.2.y_ref, ...), custom_call_target="tpu_custom_call" | custom-call | flops 1000000000 | bytes 4000000 | tf_op jit(solution)/shard_map/far/pallas_call | solution.py:460
  65.6 1.0 %all-to-all-done.1.parts_ref = f32[8,1,128]{2,1,0:T(1,128)S(1)} async-done(((f32[8,1,128]{2,1,0:T(1,128)}), f32[8,1,128]{2,1,0:T(1,128)S(1)}, u32[]{:S(2)}, u32[]{:S(2)}) %all-to-all-start.1) | async-done | bytes 4128 | tf_op jit(solution)/shard_map/all_to_all | solution.py:458
  66.6 0.8 %final.1 = (f32[3,64,128]{2,1,0:T(8,128)}, f32[6,64,128]{2,1,0:T(8,128)}) custom-call(f32[8,1,128]{2,1,0:T(1,128)S(1)} %all-to-all-done.1.parts_ref, s32[64,128]{1,0:T(8,128)S(1)} %get-tuple-element.37.corner_ref, f32[3,64,128]{2,1,0:T(8,128)S(1)} %far.1.near_ref, f32[3,64,128]{2,1,0:T(8,128)S(1)} %get-tuple-element.39.unit_ref, ...), custom_call_target="tpu_custom_call" | custom-call | flops 500000 | bytes 600000 | tf_op jit(solution)/shard_map/final/pallas_call | solution.py:474
  (1 shorter events, 0.0 us)
Async XLA Ops:
  5.0 34.3 %all-to-all-start = ((f32[32,1,128]{2,1,0:T(1,128)}), f32[32,1,128]{2,1,0:T(1,128)S(1)}, u32[]{:S(2)}, u32[]{:S(2)}) async-start(f32[32,1,128]{2,1,0:T(1,128)} %get-tuple-element.23), calls=%async_computation | async-start | bytes 32768 | tf_op jit(solution)/shard_map/all_to_all | solution.py:397
  22.0 25.9 %collective-permute-start.1 = (bf16[48,512]{1,0:T(8,128)(2,1)S(1)}, bf16[48,512]{1,0:T(8,128)(2,1)S(1)}, u32[]{:S(2)}, u32[]{:S(2)}) collective-permute-start(bf16[48,512]{1,0:T(8,128)(2,1)S(1)} %get-tuple-element.30), channel_id=1, source_target_pairs={{0,128},{128,0},{256,384},{384,256},{1,129},{129,1},{257,385},{385... | collective-permute-start | bytes 147464 | tf_op jit(solution)/shard_map/ppermute | solution.py:366
  24.9 23.0 %collective-permute-start.2 = (bf16[48,512]{1,0:T(8,128)(2,1)S(1)}, bf16[48,512]{1,0:T(8,128)(2,1)S(1)}, u32[]{:S(2)}, u32[]{:S(2)}) collective-permute-start(bf16[48,512]{1,0:T(8,128)(2,1)S(1)} %get-tuple-element.31), channel_id=1, source_target_pairs={{0,1},{1,0},{2,3},{3,2},{4,5},{5,4},{6,7},{7,6},{8,9},{9,8},{10,11... | collective-permute-start | bytes 147464 | tf_op jit(solution)/shard_map/ppermute | solution.py:366
  28.3 23.6 %collective-permute-start.3 = (bf16[48,512]{1,0:T(8,128)(2,1)S(1)}, bf16[48,512]{1,0:T(8,128)(2,1)S(1)}, u32[]{:S(2)}, u32[]{:S(2)}) collective-permute-start(bf16[48,512]{1,0:T(8,128)(2,1)S(1)} %get-tuple-element.32), channel_id=1, source_target_pairs={{0,31},{1,2},{2,1},{3,4},{4,3},{5,6},{6,5},{7,8},{8,7},{9,10},{10,... | collective-permute-start | bytes 147464 | tf_op jit(solution)/shard_map/ppermute | solution.py:366
  39.5 16.9 %collective-permute-start = (bf16[40,512]{1,0:T(8,128)(2,1)S(1)}, bf16[40,512]{1,0:T(8,128)(2,1)S(1)}, u32[]{:S(2)}, u32[]{:S(2)}) collective-permute-start(bf16[40,512]{1,0:T(8,128)(2,1)S(1)} %get-tuple-element.28), channel_id=1, source_target_pairs={{0,384},{128,256},{256,128},{384,0},{1,385},{129,257},{257,129},{3... | collective-permute-start | bytes 122888 | tf_op jit(solution)/shard_map/ppermute | solution.py:366
  47.9 9.6 %all-to-all-start.2 = ((bf16[4,48,512]{2,1,0:T(8,128)(2,1)}), bf16[4,48,512]{2,1,0:T(8,128)(2,1)S(1)}, u32[]{:S(2)}, u32[]{:S(2)}) async-start(bf16[4,48,512]{2,1,0:T(8,128)(2,1)} %gate.1), calls=%async_computation.2 | async-start | bytes 393216 | tf_op jit(solution)/shard_map/all_to_all | solution.py:433
  57.5 9.1 %all-to-all-start.1 = ((f32[8,1,128]{2,1,0:T(1,128)}), f32[8,1,128]{2,1,0:T(1,128)S(1)}, u32[]{:S(2)}, u32[]{:S(2)}) async-start(f32[8,1,128]{2,1,0:T(1,128)} %merge.1), calls=%async_computation.1 | async-start | bytes 8192 | tf_op jit(solution)/shard_map/all_to_all | solution.py:458
